TPU v7x, 256 devices: a whole 4x4x8 slice. The times are simulated.
256 devices in a mesh: role: 2 (over core), gx: 16 (over y_hi, z), gy: 8 (over x, y_lo).
Axes of the slice: x: 4, y: 4 (y_hi: 2, y_lo: 2; y = y_hi * 2 + y_lo), z: 8, core: 2. Of those that a mesh axis runs over, the one named last changes fastest.
Arguments:
- state: float32 [2, 4, 16, 128, 1024], P('role', None, None, 'gx', 'gy'), may hold values from -4 to 4
- turbine_mask: int32 [16, 128, 1024], P(None, 'gx', 'gy'), may hold values 0 or 1
- sample_x: int32 [1024], P('gy'), may hold values from 0 to 127, as said below
- gust_start: int32 [1], replicated, may hold values from -40 to 0
- gust_level: int32 [1024], P('gy'), may hold values from 0 to 3
Outputs:
- new_state: float32 [2, 4, 16, 128, 1024], P('role', None, None, 'gx', 'gy')
Inputs may be any that keep to these rules, and one draw needn't show every extreme that they name: `sample_x`: row y's sampling column lies among columns 8 * (y mod (16)) to 8 * (y mod (16)) + 7.
All inputs are finite; a program needn't handle non-finite values. No bound on the sum of `turbine_mask` on one device may be relied on, other than what follows from the above.
Results may differ from a plain program's by a relative error of at most 0.0001.
Values sent between devices are 32-bit elements; how exact they have to be, the bound alone decides.
No kernel may reach another device: no remote copies, remote signals or barrier semaphores. Data moves between devices by JAX's collectives and lax.ppermute only.
A program may use at most 64 MiB of HBM per device.

v0:
```python
import math

import jax
import jax.numpy as jnp
from jax import lax
from jax.sharding import PartitionSpec as P

SWEEPS = 6


DT = 0.25
SMAG = 0.1
BETA = 0.5
PRINV = 3.0
CDRAG = 1.0
RISE = 40.0
EPS = 1e-06
SECTION_C = (1.0 / 3.0, 0.5, 1.0)
SECTION_T = (0.0, 1.0 / 3.0, 0.5)


def shifted(block, axis, distance):
    devices = range(lax.axis_size(axis))
    route = [(i - distance, i) for i in devices if i - distance in devices]
    return lax.ppermute(block, axis, route)


def extended(cells, sides, width):
    for axis, dim in sides:
        count = lax.axis_size(axis)
        head = lax.slice_in_dim(cells, 0, width, axis=dim)
        tail = lax.slice_in_dim(cells, cells.shape[dim] - width, cells.shape[dim], axis=dim)
        cells = jnp.concatenate(
            [
                lax.ppermute(tail, axis, [(i, (i + 1) % count) for i in range(count)]),
                cells,
                lax.ppermute(head, axis, [((i + 1) % count, i) for i in range(count)]),
            ],
            axis=dim,
        )
    return cells


def set_x_ends(padded, left_face, first_tile, last_tile):
    left_col = jnp.where(first_tile, left_face, padded[..., 0, :])
    right_fill = padded[..., -2, :]
    right_col = jnp.where(last_tile, right_fill, padded[..., -1, :])
    return jnp.concatenate(
        [left_col[..., None, :], padded[..., 1:-1, :], right_col[..., None, :]], axis=-2
    )


def zero_ends(padded, width, first_tile, last_tile):
    column_pos = jnp.arange(padded.shape[1])[None, :, None]
    outside = first_tile & (column_pos < width) | last_tile & (
        column_pos >= padded.shape[1] - width
    )
    return jnp.where(outside, 0.0, padded)


def tendencies(state_q, x_padded, y_padded, mean_theta, drag_field):
    wall = (jnp.arange(4) != 2).astype(state_q.dtype)[:, None, None, None]
    z_padded = jnp.concatenate([state_q[:, :1] * wall, state_q, state_q[:, -1:] * wall], axis=1)
    grad_x = (x_padded[:, :, 2:, :] - x_padded[:, :, :-2, :]) * 0.5
    grad_y = (y_padded[..., 2:] - y_padded[..., :-2]) * 0.5
    grad_z = (z_padded[:, 2:] - z_padded[:, :-2]) * 0.5
    laplace = (
        x_padded[:, :, 2:, :]
        + x_padded[:, :, :-2, :]
        + y_padded[..., 2:]
        + y_padded[..., :-2]
        + z_padded[:, 2:]
        + z_padded[:, :-2]
        - 6.0 * state_q
    )
    u_vel, v_vel, w_vel, theta = (state_q[0], state_q[1], state_q[2], state_q[3])
    carried = u_vel * grad_x + v_vel * grad_y + w_vel * grad_z
    shear_xy = 0.5 * (grad_y[0] + grad_x[1])
    shear_xz = 0.5 * (grad_z[0] + grad_x[2])
    shear_yz = 0.5 * (grad_z[1] + grad_y[2])
    strain = (
        grad_x[0] * grad_x[0]
        + grad_y[1] * grad_y[1]
        + grad_z[2] * grad_z[2]
        + 2.0 * (shear_xy * shear_xy + shear_xz * shear_xz + shear_yz * shear_yz)
    )
    eddy_visc = SMAG * jnp.sqrt(2.0 * strain + EPS)
    wind_speed = jnp.sqrt(u_vel * u_vel + v_vel * v_vel + EPS)
    resist = drag_field * wind_speed
    rate_u = eddy_visc * laplace[0] - carried[0] - resist * u_vel
    rate_v = eddy_visc * laplace[1] - carried[1] - resist * v_vel
    rate_w = eddy_visc * laplace[2] - carried[2] + BETA * (theta - mean_theta)
    rate_t = PRINV * eddy_visc * laplace[3] - carried[3]
    return jnp.stack([rate_u, rate_v, rate_w, rate_t])


def divergence(tentative, u_x, v_y):
    w_vel = tentative[2]
    w_pad = jnp.concatenate([jnp.zeros_like(w_vel[:1]), w_vel, jnp.zeros_like(w_vel[:1])], axis=0)
    return (
        (u_x[:, 2:, :] - u_x[:, :-2, :]) * 0.5
        + (v_y[..., 2:] - v_y[..., :-2]) * 0.5
        + (w_pad[2:] - w_pad[:-2]) * 0.5
    )


def jacobi_sweep(padded, source):
    centre = padded[:, 1:-1, 1:-1]
    z_pad = jnp.concatenate([centre[:1], centre, centre[-1:]], axis=0)
    neighbours = (
        padded[:, 2:, 1:-1]
        + padded[:, :-2, 1:-1]
        + padded[:, 1:-1, 2:]
        + padded[:, 1:-1, :-2]
        + z_pad[2:]
        + z_pad[:-2]
    )
    return (neighbours - source) / 6.0


def per_device(state, turbine_mask, sample_x, gust_start, gust_level):
    start_q = state[0]
    tile_x = start_q.shape[2]
    tile_y = start_q.shape[3]
    role_index = lax.axis_index("role")
    column = lax.axis_index("gx")
    count_x = lax.axis_size("gx")
    total_cells = float(tile_x * count_x * tile_y * lax.axis_size("gy"))
    successor = role_index == 1
    first_tile = successor & (column == 0)
    last_tile = successor & (column == count_x - 1)
    drag_field = jnp.where(successor, CDRAG * turbine_mask.astype(jnp.float32), 0.0)
    owner_tile = sample_x // tile_x
    offset = sample_x - owner_tile * tile_x
    holder = ((role_index == 0) & (owner_tile == column))[None, None, :]
    sample_index = jnp.broadcast_to(offset[None, None, None, :], (4, start_q.shape[1], 1, tile_y))
    gust_amp = 1.5 + gust_level.astype(jnp.float32)
    start_step = gust_start[0].astype(jnp.float32)
    current = start_q
    for section in range(3):
        section_step = SECTION_C[section] * DT
        rise_frac = jnp.clip((SECTION_T[section] - start_step) / RISE, 0.0, 1.0)
        gust_speed = gust_amp * 0.5 * (1.0 - jnp.cos(math.pi * rise_frac))
        local_plane = jnp.take_along_axis(current, sample_index, axis=2)[:, :, 0, :]
        held_plane = jnp.where(holder, local_plane, 0.0)
        inflow = lax.psum(held_plane, "gx")
        inflow = shifted(inflow, "role", 1)
        inflow = inflow.at[0].add(gust_speed[None, :])
        level_sums = lax.psum(jnp.sum(current[3], axis=(1, 2)), ("gx", "gy"))
        mean_theta = (level_sums / total_cells)[:, None, None]
        bordered = extended(current, (("gx", 2), ("gy", 3)), 1)
        x_padded = set_x_ends(bordered[:, :, :, 1:-1], inflow, first_tile, last_tile)
        y_padded = bordered[:, :, 1:-1, :]
        tendency_now = tendencies(current, x_padded, y_padded, mean_theta, drag_field)
        tentative = start_q + section_step * tendency_now
        velocity_pair = extended(tentative[:2], (("gx", 2), ("gy", 3)), 1)
        u_x = set_x_ends(velocity_pair[0, :, :, 1:-1], inflow[0], first_tile, last_tile)
        v_y = velocity_pair[1, :, 1:-1, :]
        source = divergence(tentative, u_x, v_y) / section_step
        pressure = jnp.zeros_like(source)
        for sweep_index in range(SWEEPS):
            pressure_edge = extended(pressure, (("gx", 1), ("gy", 2)), 1)
            pressure = jacobi_sweep(zero_ends(pressure_edge, 1, first_tile, last_tile), source)
        final_edge = extended(pressure, (("gx", 1), ("gy", 2)), 1)
        final_edge = zero_ends(final_edge, 1, first_tile, last_tile)
        grad_x = (final_edge[:, 2:, 1:-1] - final_edge[:, :-2, 1:-1]) * 0.5
        grad_y = (final_edge[:, 1:-1, 2:] - final_edge[:, 1:-1, :-2]) * 0.5
        z_pad = jnp.concatenate([pressure[:1], pressure, pressure[-1:]], axis=0)
        grad_z = (z_pad[2:] - z_pad[:-2]) * 0.5
        current = jnp.stack(
            [
                tentative[0] - section_step * grad_x,
                tentative[1] - section_step * grad_y,
                tentative[2] - section_step * grad_z,
                tentative[3],
            ]
        )
    return current[None]


def solution(mesh):
    placed = (P("role", None, None, "gx", "gy"), P(None, "gx", "gy"), P("gy"), P(), P("gy"))
    return jax.shard_map(
        per_device,
        mesh=mesh,
        in_specs=placed,
        out_specs=P("role", None, None, "gx", "gy"),
        check_vma=False,
    )
```

profile of v0, /device:TPU:32, one launch (start us, length us, event | category | flops | bytes accessed | tf_op | source)
XLA Modules:
  0.0 1897.7 jit_solution(10196993398744177811)
XLA Ops:
  3.2 78.6 %gather_fusion = f32[8192]{0:T(1024)S(1)} fusion(f32[4,16,8,128]{3,1,0,2:T(8,128)S(1)} %bitcast.244, s32[8192]{0:T(1024)S(1)} %bitcast.241), kind=kCustom, calls=%fused_computation.clone | custom fusion | bytes 196608 | tf_op jit(solution)/shard_map/jit(take_along_axis)/gather | solution.py:144
  81.9 78.1 %psum.42 = f32[4,16,128]{2,1,0:T(8,128)S(1)} all-reduce(f32[4,16,128]{2,1,0:T(8,128)S(1)} %bitcast_select_fusion.5), channel_id=1, replica_groups=mesh['role'=2,'gx'=16,'gy'=8] {'gx'}, use_global_device_ids=true, to_apply=%region_0.2 | all-reduce | flops 8192 | bytes 65536 | tf_op jit(solution)/shard_map/psum | solution.py:146
  161.3 6.0 collective-permute-start
  168.4 324.1 %psum.43 = f32[16]{0:T(128)S(1)} all-reduce(f32[16]{0:T(128)S(1)} %get-tuple-element.128), channel_id=1, replica_groups=mesh['role'=2,'gx'=16,'gy'=8] {'gx','gy'}, use_global_device_ids=true, to_apply=%region_2.4 | all-reduce | flops 16 | bytes 128 | tf_op jit(solution)/shard_map/psum | solution.py:149
  500.1 21.6 %collective-permute-done.2 = f32[4,16,1,128]{3,1,0,2:T(8,128)S(1)} collective-permute-done((f32[4,16,1,128]{3,1,0,2:T(8,128)S(1)}, f32[4,16,1,128]{3,1,0,2:T(8,128)S(1)}, u32[]{:S(2)}, u32[]{:S(2)}) %collective-permute-start.2) | collective-permute-done | bytes 32800 | tf_op jit(solution)/shard_map/ppermute | solution.py:35
  523.9 8.6 collective-permute-done.3
  534.3 7.6 collective-permute-start.10
  568.8 4.2 collective-permute-start.18
  598.6 4.1 collective-permute-start.26
  606.4 8.9 collective-permute-start.28
  632.1 327.3 %psum.45 = f32[16]{0:T(128)S(1)} all-reduce(f32[16]{0:T(128)S(1)} %get-tuple-element.117), channel_id=1, replica_groups=mesh['role'=2,'gx'=16,'gy'=8] {'gx','gy'}, use_global_device_ids=true, to_apply=%region_5.7 | all-reduce | flops 16 | bytes 128 | tf_op jit(solution)/shard_map/psum | solution.py:149
  959.9 20.0 %collective-permute-start.34 = (f32[16,1,128]{2,0,1:T(8,128)S(1)}, f32[16,1,128]{2,0,1:T(8,128)S(1)}, u32[]{:S(2)}, u32[]{:S(2)}) collective-permute-start(f32[16,1,128]{2,0,1:T(8,128)S(1)} %get-tuple-element.249), channel_id=1, source_target_pairs={{8,0},{16,8},{24,16},{32,24},{40,32},{48,40},{56,48},{64,56},{72,6... | collective-permute-start | bytes 24584 | tf_op jit(solution)/shard_map/ppermute | solution.py:37
  990.7 78.6 %gather_fusion.1 = f32[8192]{0:T(1024)S(1)} fusion(f32[4,16,8,128]{3,1,2,0:T(8,128)S(1)} %pad_maximum_fusion.69, s32[8192]{0:T(1024)S(1)} %bitcast.242), kind=kCustom, calls=%fused_computation.1.clone | custom fusion | bytes 196608 | tf_op jit(solution)/shard_map/jit(take_along_axis)/gather | solution.py:144
  1069.4 5.5 collective-permute-start.37
  1074.9 72.1 %psum.44 = f32[4,16,128]{2,1,0:T(8,128)S(1)} all-reduce(f32[4,16,128]{2,1,0:T(8,128)S(1)} %bitcast_select_fusion.3), channel_id=1, replica_groups=mesh['role'=2,'gx'=16,'gy'=8] {'gx'}, use_global_device_ids=true, to_apply=%region_3.5 | all-reduce | flops 8192 | bytes 65536 | tf_op jit(solution)/shard_map/psum | solution.py:146
  1148.6 4.3 collective-permute-start.40
  1153.0 4.9 collective-permute-done.41
  1160.4 6.4 collective-permute-start.43
  1177.0 4.2 collective-permute-done.44
  1181.4 4.1 collective-permute-start.47
  1212.0 4.2 collective-permute-start.55
  1252.1 327.0 %psum.47 = f32[16]{0:T(128)S(1)} all-reduce(f32[16]{0:T(128)S(1)} %get-tuple-element.106), channel_id=1, replica_groups=mesh['role'=2,'gx'=16,'gy'=8] {'gx','gy'}, use_global_device_ids=true, to_apply=%region_8.10 | all-reduce | flops 16 | bytes 128 | tf_op jit(solution)/shard_map/psum | solution.py:149
  1579.6 20.0 %collective-permute-start.67 = (f32[16,1,128]{2,0,1:T(8,128)S(1)}, f32[16,1,128]{2,0,1:T(8,128)S(1)}, u32[]{:S(2)}, u32[]{:S(2)}) collective-permute-start(f32[16,1,128]{2,0,1:T(8,128)S(1)} %get-tuple-element.235), channel_id=1, source_target_pairs={{8,0},{16,8},{24,16},{32,24},{40,32},{48,40},{56,48},{64,56},{72,6... | collective-permute-start | bytes 24584 | tf_op jit(solution)/shard_map/ppermute | solution.py:37
  1610.6 78.6 %gather_fusion.2 = f32[8192]{0:T(1024)S(1)} fusion(f32[4,16,8,128]{3,1,2,0:T(8,128)S(1)} %pad_maximum_fusion.70, s32[8192]{0:T(1024)S(1)} %bitcast.243), kind=kCustom, calls=%fused_computation.2.clone | custom fusion | bytes 196608 | tf_op jit(solution)/shard_map/jit(take_along_axis)/gather | solution.py:144
  1689.3 5.6 collective-permute-start.70
  1694.9 72.1 %psum.46 = f32[4,16,128]{2,1,0:T(8,128)S(1)} all-reduce(f32[4,16,128]{2,1,0:T(8,128)S(1)} %bitcast_select_fusion.1), channel_id=1, replica_groups=mesh['role'=2,'gx'=16,'gy'=8] {'gx'}, use_global_device_ids=true, to_apply=%region_6.8 | all-reduce | flops 8192 | bytes 65536 | tf_op jit(solution)/shard_map/psum | solution.py:146
  1768.7 4.1 collective-permute-start.73
  1772.9 5.1 collective-permute-done.74
  1780.2 5.4 collective-permute-start.75
  1798.7 5.8 collective-permute-start.80
  1805.9 6.5 collective-permute-done.79
  1819.6 5.9 collective-permute-start.84
  (428 shorter events, 285.4 us)
Async XLA Ops:
  0.0 492.6 %collective-permute-start.6 = (f32[16,1,128]{2,0,1:T(8,128)S(1)}, f32[16,1,128]{2,0,1:T(8,128)S(1)}, u32[]{:S(2)}, u32[]{:S(2)}) collective-permute-start(f32[16,1,128]{2,0,1:T(8,128)S(1)} %broadcast.339), channel_id=1, source_target_pairs={{8,0},{16,8},{24,16},{32,24},{40,32},{48,40},{56,48},{64,56},{72,6... | collective-permute-start | bytes 24584 | tf_op jit(solution)/shard_map/ppermute | solution.py:37
  1.8 490.8 %collective-permute-start.5 = (f32[16,1,128]{2,0,1:T(8,128)S(1)}, f32[16,1,128]{2,0,1:T(8,128)S(1)}, u32[]{:S(2)}, u32[]{:S(2)}) collective-permute-start(f32[16,1,128]{2,0,1:T(8,128)S(1)} %broadcast.339), channel_id=1, source_target_pairs={{0,8},{8,16},{16,24},{24,32},{32,40},{40,48},{48,56},{56,64},{64,7... | collective-permute-start | bytes 24584 | tf_op jit(solution)/shard_map/ppermute | solution.py:35
  160.0 340.0 %collective-permute-start.1 = (f32[4,16,128]{2,1,0:T(8,128)S(1)}, f32[4,16,128]{2,1,0:T(8,128)S(1)}, u32[]{:S(2)}, u32[]{:S(2)}) collective-permute-start(f32[4,16,128]{2,1,0:T(8,128)S(1)} %psum.42), channel_id=1, source_target_pairs={{0,128},{1,129},{2,130},{3,131},{4,132},{5,133},{6,134},{7,135},{8... | collective-permute-start | bytes 98312 | tf_op jit(solution)/shard_map/ppermute | solution.py:25
  161.3 338.6 %collective-permute-start = (f32[4,16,1,128]{3,1,0,2:T(8,128)S(1)}, f32[4,16,1,128]{3,1,0,2:T(8,128)S(1)}, u32[]{:S(2)}, u32[]{:S(2)}) collective-permute-start(f32[4,16,1,128]{3,1,0,2:T(8,128)S(1)} %slice.1856), channel_id=1, source_target_pairs={{8,0},{16,8},{24,16},{32,24},{40,32},{48,40},{56,48},{64,56},{72,6... | collective-permute-start | bytes 98312 | tf_op jit(solution)/shard_map/ppermute | solution.py:37
  499.9 21.7 %collective-permute-start.2 = (f32[4,16,1,128]{3,1,0,2:T(8,128)S(1)}, f32[4,16,1,128]{3,1,0,2:T(8,128)S(1)}, u32[]{:S(2)}, u32[]{:S(2)}) collective-permute-start(f32[4,16,1,128]{3,1,0,2:T(8,128)S(1)} %get-tuple-element.137), channel_id=1, source_target_pairs={{0,8},{8,16},{16,24},{24,32},{32,40},{40,48},{48,56},{56,64},{64,7... | collective-permute-start | bytes 98312 | tf_op jit(solution)/shard_map/ppermute | solution.py:35
  521.8 10.7 collective-permute-start.3
  522.0 10.5 collective-permute-start.4
  534.3 9.0 collective-permute-start.10
  546.0 7.7 collective-permute-start.11
  606.4 13.4 collective-permute-start.28
  630.0 329.4 %collective-permute-start.32 = (f32[16,10,1]{2,0,1:T(8,128)S(1)}, f32[16,10,1]{2,0,1:T(8,128)S(1)}, u32[]{:S(2)}, u32[]{:S(2)}) collective-permute-start(f32[16,10,1]{2,0,1:T(8,128)S(1)} %get-tuple-element.207), channel_id=1, source_target_pairs={{1,0},{2,1},{3,2},{4,3},{5,4},{6,5},{7,6},{0,7},{9,8},{10,9},{11,1... | collective-permute-start | bytes 1928 | tf_op jit(solution)/shard_map/ppermute | solution.py:37
  630.2 329.2 %collective-permute-start.31 = (f32[16,10,1]{2,0,1:T(8,128)S(1)}, f32[16,10,1]{2,0,1:T(8,128)S(1)}, u32[]{:S(2)}, u32[]{:S(2)}) collective-permute-start(f32[16,10,1]{2,0,1:T(8,128)S(1)} %get-tuple-element.206), channel_id=1, source_target_pairs={{0,1},{1,2},{2,3},{3,4},{4,5},{5,6},{6,7},{7,0},{8,9},{9,10},{10,1... | collective-permute-start | bytes 1928 | tf_op jit(solution)/shard_map/ppermute | solution.py:35
  959.9 21.3 %collective-permute-start.34 = (f32[16,1,128]{2,0,1:T(8,128)S(1)}, f32[16,1,128]{2,0,1:T(8,128)S(1)}, u32[]{:S(2)}, u32[]{:S(2)}) collective-permute-start(f32[16,1,128]{2,0,1:T(8,128)S(1)} %get-tuple-element.249), channel_id=1, source_target_pairs={{8,0},{16,8},{24,16},{32,24},{40,32},{48,40},{56,48},{64,56},{72,6... | collective-permute-start | bytes 24584 | tf_op jit(solution)/shard_map/ppermute | solution.py:37
  1069.4 79.0 %collective-permute-start.37 = (f32[4,16,1,128]{3,1,0,2:T(8,128)S(1)}, f32[4,16,1,128]{3,1,0,2:T(8,128)S(1)}, u32[]{:S(2)}, u32[]{:S(2)}) collective-permute-start(f32[4,16,1,128]{3,1,0,2:T(8,128)S(1)} %get-tuple-element.121), channel_id=1, source_target_pairs={{8,0},{16,8},{24,16},{32,24},{40,32},{48,40},{56,48},{64,56},{72,6... | collective-permute-start | bytes 98312 | tf_op jit(solution)/shard_map/ppermute | solution.py:37
  1074.8 73.5 %collective-permute-start.39 = (f32[4,16,1,128]{3,1,0,2:T(8,128)S(1)}, f32[4,16,1,128]{3,1,0,2:T(8,128)S(1)}, u32[]{:S(2)}, u32[]{:S(2)}) collective-permute-start(f32[4,16,1,128]{3,1,0,2:T(8,128)S(1)} %get-tuple-element.120), channel_id=1, source_target_pairs={{0,8},{8,16},{16,24},{24,32},{32,40},{40,48},{48,56},{56,64},{64,7... | collective-permute-start | bytes 98312 | tf_op jit(solution)/shard_map/ppermute | solution.py:35
  1148.5 9.4 collective-permute-start.41
  1148.6 10.9 collective-permute-start.40
  1160.4 7.8 collective-permute-start.43
  1173.2 8.0 collective-permute-start.44
  1250.0 329.1 %collective-permute-start.65 = (f32[16,10,1]{2,0,1:T(8,128)S(1)}, f32[16,10,1]{2,0,1:T(8,128)S(1)}, u32[]{:S(2)}, u32[]{:S(2)}) collective-permute-start(f32[16,10,1]{2,0,1:T(8,128)S(1)} %get-tuple-element.193), channel_id=1, source_target_pairs={{1,0},{2,1},{3,2},{4,3},{5,4},{6,5},{7,6},{0,7},{9,8},{10,9},{11,1... | collective-permute-start | bytes 1928 | tf_op jit(solution)/shard_map/ppermute | solution.py:37
  1250.1 329.1 %collective-permute-start.64 = (f32[16,10,1]{2,0,1:T(8,128)S(1)}, f32[16,10,1]{2,0,1:T(8,128)S(1)}, u32[]{:S(2)}, u32[]{:S(2)}) collective-permute-start(f32[16,10,1]{2,0,1:T(8,128)S(1)} %get-tuple-element.192), channel_id=1, source_target_pairs={{0,1},{1,2},{2,3},{3,4},{4,5},{5,6},{6,7},{7,0},{8,9},{9,10},{10,1... | collective-permute-start | bytes 1928 | tf_op jit(solution)/shard_map/ppermute | solution.py:35
  1579.6 21.3 %collective-permute-start.67 = (f32[16,1,128]{2,0,1:T(8,128)S(1)}, f32[16,1,128]{2,0,1:T(8,128)S(1)}, u32[]{:S(2)}, u32[]{:S(2)}) collective-permute-start(f32[16,1,128]{2,0,1:T(8,128)S(1)} %get-tuple-element.235), channel_id=1, source_target_pairs={{8,0},{16,8},{24,16},{32,24},{40,32},{48,40},{56,48},{64,56},{72,6... | collective-permute-start | bytes 24584 | tf_op jit(solution)/shard_map/ppermute | solution.py:37
  1689.3 79.1 %collective-permute-start.70 = (f32[4,16,1,128]{3,1,0,2:T(8,128)S(1)}, f32[4,16,1,128]{3,1,0,2:T(8,128)S(1)}, u32[]{:S(2)}, u32[]{:S(2)}) collective-permute-start(f32[4,16,1,128]{3,1,0,2:T(8,128)S(1)} %get-tuple-element.110), channel_id=1, source_target_pairs={{8,0},{16,8},{24,16},{32,24},{40,32},{48,40},{56,48},{64,56},{72,6... | collective-permute-start | bytes 98312 | tf_op jit(solution)/shard_map/ppermute | solution.py:37
  1694.9 73.5 %collective-permute-start.72 = (f32[4,16,1,128]{3,1,0,2:T(8,128)S(1)}, f32[4,16,1,128]{3,1,0,2:T(8,128)S(1)}, u32[]{:S(2)}, u32[]{:S(2)}) collective-permute-start(f32[4,16,1,128]{3,1,0,2:T(8,128)S(1)} %get-tuple-element.109), channel_id=1, source_target_pairs={{0,8},{8,16},{16,24},{24,32},{32,40},{40,48},{48,56},{56,64},{64,7... | collective-permute-start | bytes 98312 | tf_op jit(solution)/shard_map/ppermute | solution.py:35
  1768.6 9.4 collective-permute-start.74
  1768.7 10.7 collective-permute-start.73
  1780.2 7.9 collective-permute-start.75
  1791.1 7.5 collective-permute-start.77
  1798.7 7.1 collective-permute-start.80
  1804.5 7.9 collective-permute-start.79
  1819.6 7.3 collective-permute-start.84
  1859.1 7.5 collective-permute-start.93
  (75 other events, 849.5 us)
where the time goes:
time: 1910 us; the launch traced here: 1900 us
  blocking collectives  1200 us (63%)
  local copies, waits for them, and re-layouts  244 us (13%)
  waiting for transfers between devices  224 us (12%)
  starting transfers between devices  216 us (11%)
    psum x3, blocking collectives, per_device(): level_sums = lax.psum(jnp.sum(current[3], axis=(1, 2)), ('gx', 'gy'))  978 us
    gather x3, local copies, waits for them, and re-layouts, per_device(): local_plane = jnp.take_along_axis(current, sample_index, axis=2)[:, :, 0, :]  236 us
    psum x3, blocking collectives, per_device(): inflow = lax.psum(held_plane, 'gx')  222 us
    ppermute x50, starting transfers between devices, extended(): lax.ppermute(head, axis, [((i + 1) % count, i) for i in range(count)])  164 us
    ppermute x50, waiting for transfers between devices, extended(): lax.ppermute(tail, axis, [(i, (i + 1) % count) for i in range(count)])  132 us
    ppermute x50, waiting for transfers between devices, extended(): lax.ppermute(head, axis, [((i + 1) % count, i) for i in range(count)])  91.5 us
    ppermute x50, starting transfers between devices, extended(): lax.ppermute(tail, axis, [(i, (i + 1) % count) for i in range(count)])  48.5 us
  transfers between devices with their start and end apart: 103, of which 88 were waited for; matrix products, arithmetic and copies ran while one was open for 4% of the time, Pallas kernels for 0%

commit v1 on v0

v1 whole, which is shorter than its diff:
```python
import functools
import math

import jax
import jax.numpy as jnp
from jax import lax
from jax.experimental import pallas as pl
from jax.experimental.pallas import tpu as pltpu
from jax.sharding import PartitionSpec as P

SWEEPS = 6
DT = 0.25
SMAG = 0.1
BETA = 0.5
PRINV = 3.0
CDRAG = 1.0
RISE = 40.0
EPS = 1e-06
SECTION_C = (1.0 / 3.0, 0.5, 1.0)
SECTION_T = (0.0, 1.0 / 3.0, 0.5)

NZ = 16
NX = 128
ROWS = 8
EXT = 3 * ROWS
BLOCKS = 16
CELLS = 131072.0
SIXTH = 1.0 / 6.0
FIELD = ROWS * NZ
DRAG_AT = 4 * FIELD


def lanes(rows=NZ):
    return lax.broadcasted_iota(jnp.int32, (rows, NX), 1)


def levels():
    return lax.broadcasted_iota(jnp.int32, (NZ, NX), 0)


def turn(v, shift, axis):
    return pltpu.roll(v, shift, axis=axis)


def up(v, ghost=None):
    return jnp.where(levels() == NZ - 1, v if ghost is None else ghost, turn(v, NZ - 1, 0))


def down(v, ghost=None):
    return jnp.where(levels() == 0, v if ghost is None else ghost, turn(v, 1, 0))


class Walls:
    def __init__(self, walled):
        lane = lanes()
        limit = jnp.where(walled, NX, -NX)
        self.first = lane == limit - NX
        self.last = lane == limit - 1

    def after(self, v):
        return jnp.where(self.last, v, turn(v, NX - 1, 1))

    def before(self, v, ghost):
        return jnp.where(self.first, ghost, turn(v, 1, 1))

    def p_after(self, v):
        return jnp.where(self.last, 0.0, turn(v, NX - 1, 1))

    def p_before(self, v):
        return jnp.where(self.first, 0.0, turn(v, 1, 1))


def mean_change(walls, mean, step):
    source = -0.5 * BETA * (up(mean, 0.0) - down(mean, 0.0))
    press = -SIXTH * source
    for _ in range(SWEEPS - 1):
        around = walls.p_after(press) + walls.p_before(press) + 2.0 * press
        press = (around + up(press) + down(press) - source) * SIXTH
    d_u = (-0.5 * step) * (walls.p_after(press) - walls.p_before(press))
    d_w = -step * (BETA * mean + 0.5 * (up(press) - down(press)))
    return d_u, d_w


def level_lanes(sums):
    spread = jnp.where(lanes() == levels(), jnp.broadcast_to(sums, (NZ, NX)), 0.0)
    return jnp.sum(spread, axis=0, keepdims=True)


def lane_means(row, start):
    spread = jnp.where(lanes() == levels() + start, jnp.broadcast_to(row, (NZ, NX)), 0.0)
    mean = jnp.sum(spread, axis=1, keepdims=True) * (1.0 / CELLS)
    return jnp.broadcast_to(mean, (NZ, NX))


def swap_blocks(v):
    row = levels()
    group = lanes() // 8
    for bit in (8, 4, 2, 1):
        row_set = (row & bit) != 0
        group_set = (group & bit) != 0
        from_low = turn(turn(v, NZ - bit, 0), 8 * bit, 1)
        from_high = turn(turn(v, bit, 0), NX - 8 * bit, 1)
        v = jnp.where(row_set == group_set, v, jnp.where(row_set, from_high, from_low))
    return v


def owner_of(block, flip):
    straight = block if block < 8 else 23 - block
    other = 15 - block if block < 8 else block - 8
    return jnp.where(flip == 0, straight, other)


def sampled(picked, f, r, cells, sample):
    shift = lax.rem(f * ROWS + r - sample[r] + 2 * NX, NX)
    return jnp.where(lanes() == f * ROWS + r, turn(cells, shift, 1), picked)


def with_gust(picked, gust):
    lane = lanes()
    for r in range(ROWS):
        picked = picked + jnp.where(lane == r, gust[r], 0.0)
    return picked


def pack_kernel(info, state, drag, out):
    flip = info[1]
    for f in range(5):
        flat = (state[f] if f < 4 else drag[...]).T
        for block in range(BLOCKS):
            out[owner_of(block, flip), f] = flat[ROWS * block : ROWS * (block + 1)]


def first_kernel(info, sample, gust, chunks, buf, plane, sums_out):
    del info
    picked = jnp.zeros((NZ, NX), jnp.float32)
    sums = jnp.zeros((NZ, NX), jnp.float32)
    for f in range(5):
        for r in range(ROWS):
            spot = f * ROWS + r
            cells = swap_blocks(chunks[pl.ds(spot, BLOCKS, stride=5 * ROWS), :])
            buf[spot * NZ : (spot + 1) * NZ, :] = cells
            if f < 4:
                picked = sampled(picked, f, r, cells, sample)
            if f == 3:
                sums = sums + cells
    picked = with_gust(picked, gust)
    plane[...] = picked
    buf[5 * FIELD :, :] = picked
    sums_out[...] = level_lanes(jnp.sum(sums, axis=1, keepdims=True))


def section_kernel(section, info, *refs):
    refs = list(refs)

    def take(n):
        out = refs[:n]
        del refs[:n]
        return out

    if section < 2:
        sample, gust = take(2)
    starts = take(3)
    bufs = take(3) if section else starts
    if section < 2 or section == 2:
        (sums_in,) = take(1)
    if section < 2:
        new_out, plane_out, sums_out = take(3)
    else:
        (chunks_out,) = take(1)
    ext, tent, press, src, face = refs

    role = info[0]
    step = SECTION_C[section] * DT
    walls = Walls(role == 1)
    plane_at = (4 if section else 5) * FIELD

    if section == 1:
        totals = jnp.concatenate(
            [
                jnp.sum(sums_in[: sums_in.shape[0] // 2], axis=0, keepdims=True),
                jnp.sum(sums_in[sums_in.shape[0] // 2 :], axis=0, keepdims=True),
            ]
        )
        own = jnp.where(role == 0, totals[:1], totals[1:])
        prev_step = SECTION_C[0] * DT
        d_u, d_w = mean_change(walls, lane_means(own, 0), prev_step)
        _, pre_w = mean_change(Walls(role < 0), lane_means(totals[:1], 0), prev_step)
        mean = lane_means(own, NZ)

    for side in range(3):
        plane = bufs[side][plane_at : plane_at + NZ, :]
        for r in range(ROWS):
            j = side * ROWS + r
            for f in range(4):
                at = (f * ROWS + r) * NZ
                cells = bufs[side][at : at + NZ, :]
                shift = (NX - (f * ROWS + r)) % NX
                ghost = turn(plane, shift, 1) if shift else plane
                if section == 1 and f == 0:
                    cells = cells + d_u
                if section == 1 and f == 2:
                    cells = cells + d_w
                    ghost = ghost + pre_w
                ext[f, j] = cells
                face[f, j] = ghost

    def rate_row(side, r):
        j = side * ROWS + r
        mid = [ext[f, j] for f in range(3)]
        nxt = [ext[f, j + 1] for f in range(3)]
        prv = [ext[f, j - 1] for f in range(3)]
        after = [walls.after(m) for m in mid]
        before = [walls.before(mid[f], face[f, j]) for f in range(3)]
        hi = [up(mid[0]), up(mid[1]), up(mid[2], 0.0)]
        lo = [down(mid[0]), down(mid[1]), down(mid[2], 0.0)]
        u, v, w = mid
        g_x = [(after[f] - before[f]) * 0.5 for f in range(3)]
        g_y = [(nxt[f] - prv[f]) * 0.5 for f in range(3)]
        g_z = [(hi[f] - lo[f]) * 0.5 for f in range(3)]
        a = g_y[0] + g_x[1]
        b = g_z[0] + g_x[2]
        e = g_z[1] + g_y[2]
        strain = g_x[0] * g_x[0] + g_y[1] * g_y[1] + g_z[2] * g_z[2] + 0.5 * (a * a + b * b + e * e)
        nu = SMAG * jnp.sqrt(2.0 * strain + EPS)
        at = pl.multiple_of(DRAG_AT + r * NZ, NZ)
        resist = starts[side][pl.ds(at, NZ), :] * jnp.sqrt(u * u + v * v + EPS)
        rates = []
        for f in range(3):
            lap = after[f] + before[f] + nxt[f] + prv[f] + hi[f] + lo[f] - 6.0 * mid[f]
            rates.append(nu * lap - (u * g_x[f] + v * g_y[f] + w * g_z[f]))
        rates[0] = rates[0] - resist * u
        rates[1] = rates[1] - resist * v
        theta = ext[3, j]
        rates[2] = rates[2] + BETA * (theta - mean if section == 1 else theta)
        for f in range(3):
            at = pl.multiple_of((f * ROWS + r) * NZ, NZ)
            tent[f, j] = starts[side][pl.ds(at, NZ), :] + step * rates[f]
        return u, v, w, nu, theta

    def heat_row(r, u, v, w, nu, mid):
        j = ROWS + r
        nxt = ext[3, j + 1]
        prv = ext[3, j - 1]
        after = walls.after(mid)
        before = walls.before(mid, face[3, j])
        hi = up(mid)
        lo = down(mid)
        g_x = (after - before) * 0.5
        g_y = (nxt - prv) * 0.5
        g_z = (hi - lo) * 0.5
        lap = after + before + nxt + prv + hi + lo - 6.0 * mid
        rate = PRINV * nu * lap - (u * g_x + v * g_y + w * g_z)
        at = pl.multiple_of((3 * ROWS + r) * NZ, NZ)
        tent[3, j] = starts[1][pl.ds(at, NZ), :] + step * rate

    def outer(side, r, carry):
        rate_row(side, r)
        return carry

    def inner(r, carry):
        heat_row(r, *rate_row(1, r))
        return carry

    lax.fori_loop(1, ROWS, functools.partial(outer, 0), 0)
    lax.fori_loop(0, ROWS, inner, 0)
    lax.fori_loop(0, ROWS - 1, functools.partial(outer, 2), 0)

    for j in range(2, EXT - 2):
        u = tent[0, j]
        w = tent[2, j]
        div = walls.after(u) - walls.before(u, face[0, j])
        div = div + (tent[1, j + 1] - tent[1, j - 1]) + (up(w, 0.0) - down(w, 0.0))
        scaled = div * (0.5 * SIXTH / step)
        src[j] = scaled
        press[0, j] = -scaled
    for sweep in range(1, SWEEPS):
        old = press.at[(sweep - 1) % 2]
        new = press.at[sweep % 2]
        for j in range(2 + sweep, EXT - 2 - sweep):
            mid = old[j]
            total = walls.p_after(mid) + walls.p_before(mid) + old[j + 1] + old[j - 1]
            total = total + up(mid) + down(mid)
            new[j] = total * SIXTH - src[j]
    final = press.at[(SWEEPS - 1) % 2]

    picked = jnp.zeros((NZ, NX), jnp.float32)
    sums = jnp.zeros((NZ, NX), jnp.float32)
    half = 0.5 * step
    for r in range(ROWS):
        j = ROWS + r
        mid = final[j]
        fresh = (
            tent[0, j] - half * (walls.p_after(mid) - walls.p_before(mid)),
            tent[1, j] - half * (final[j + 1] - final[j - 1]),
            tent[2, j] - half * (up(mid) - down(mid)),
            tent[3, j],
        )
        for f in range(4):
            spot = f * ROWS + r
            if section < 2:
                new_out[spot * NZ : (spot + 1) * NZ, :] = fresh[f]
                picked = sampled(picked, f, r, fresh[f], sample)
            else:
                chunks_out[pl.ds(spot, BLOCKS, stride=5 * ROWS), :] = swap_blocks(fresh[f])
        sums = sums + fresh[3]
    if section < 2:
        picked = with_gust(picked, gust)
        new_out[plane_at if section else 4 * FIELD :, :] = picked
        plane_out[...] = picked
        row = level_lanes(jnp.sum(sums, axis=1, keepdims=True))
        sums_out[...] = turn(row, NZ, 1) + sums_in[...] if section == 0 else row
    else:
        row = jnp.sum(sums_in[...], axis=0, keepdims=True)
        for block in range(BLOCKS):
            at = (block * 5 + 4) * ROWS
            chunks_out[at : at + ROWS, :] = jnp.broadcast_to(row, (ROWS, NX))


def last_kernel(info, chunks, out):
    role = info[0]
    flip = info[1]
    gx = info[2]
    row = chunks[0, 4, :1]
    for block in range(1, BLOCKS):
        row = row + chunks[block, 4, :1]
    changes = mean_change(Walls(role == 1), lane_means(row, 0), SECTION_C[2] * DT)
    shift = lax.rem(NX - ROWS * gx, NX)
    for f in range(4):
        flat = jnp.concatenate([chunks[owner_of(block, flip), f] for block in range(BLOCKS)])
        out[f] = flat.T
        if f in (0, 2):
            change = turn(changes[f // 2], shift, 1)
            for x in range(8):
                rows = pl.ds(x, NZ, stride=8)
                out[f, rows, :] += jnp.broadcast_to(change[:, x : x + 1], (NZ, NX))


VMEM = pl.BlockSpec(memory_space=pltpu.VMEM)
SMEM = pl.BlockSpec(memory_space=pltpu.SMEM)


def shape(*dims):
    return jax.ShapeDtypeStruct(dims, jnp.float32)


def call(body, name, small, args, outs, scratch=()):
    return pl.pallas_call(
        body,
        name=name,
        out_shape=outs,
        in_specs=[SMEM] * len(small) + [VMEM] * len(args),
        out_specs=[VMEM] * len(outs),
        scratch_shapes=list(scratch),
        compiler_params=pltpu.CompilerParams(vmem_limit_bytes=48 * 1024 * 1024),
    )(*small, *args)


def section_call(section, small, args):
    if section < 2:
        outs = [shape(4 * FIELD + NZ, NX), shape(NZ, NX), shape(1, NX)]
    else:
        outs = [shape(BLOCKS * 5 * ROWS, NX)]
    row = (NZ, NX)
    scratch = [(4, EXT), (4, EXT), (2, EXT), (EXT,), (4, EXT)]
    scratch = [pltpu.VMEM((*lead, *row), jnp.float32) for lead in scratch]
    body = functools.partial(section_kernel, section)
    return call(body, f"section{section}", small, args, outs, scratch)


def ring_order():
    order = []
    for gy in range(8):
        low = list(range(8))
        high = list(range(15, 7, -1))
        order += [gx * 8 + gy for gx in (low + high if gy % 2 == 0 else high + low)]
    return order


def around(cells, distance):
    order = ring_order()
    route = [(d, order[(i + distance) % len(order)]) for i, d in enumerate(order)]
    return lax.ppermute(cells, ("gx", "gy"), route)


def inflow_to(buf, plane):
    plane = lax.ppermute(plane, "role", [(0, 1)])
    return lax.dynamic_update_slice(buf, plane, (buf.shape[0] - NZ, 0))


def halo(buf):
    return around(buf, 1), buf, around(buf, -1)


def every(row, axes, count):
    return lax.all_to_all(jnp.broadcast_to(row[None], (count, 1, NX)), axes, 0, 0)[:, 0]


def per_device(state, turbine_mask, sample_x, gust_start, gust_level):
    role = lax.axis_index("role")
    gx = lax.axis_index("gx")
    flip = lax.axis_index("gy") % 2
    info = jnp.stack([role, flip, gx]).astype(jnp.int32)
    drag = jnp.where(role == 1, CDRAG * turbine_mask.astype(jnp.float32), 0.0)
    block = jnp.where(gx < 8, jnp.where(flip == 0, gx, gx + 8), jnp.where(flip == 0, 23 - gx, 15 - gx))
    sample = lax.dynamic_slice(sample_x, (block * ROWS,), (ROWS,)).astype(jnp.int32)
    level = lax.dynamic_slice(gust_level, (block * ROWS,), (ROWS,))
    amp = 1.5 + level.astype(jnp.float32)
    began = gust_start[0].astype(jnp.float32)
    gusts = []
    for section in range(3):
        rise = jnp.clip((SECTION_T[section] - began) / RISE, 0.0, 1.0)
        gusts.append(amp * 0.5 * (1.0 - jnp.cos(math.pi * rise)))

    args = (state.reshape(4, 128, 128), drag.reshape(128, 128))
    (chunks,) = call(pack_kernel, "pack", (info,), args, [shape(BLOCKS, 5, ROWS, NX)])
    chunks = lax.all_to_all(chunks, "gx", 0, 0)
    outs = [shape(5 * FIELD + NZ, NX), shape(NZ, NX), shape(1, NX)]
    args = (chunks.reshape(BLOCKS * 5 * ROWS, NX),)
    buf, plane, sums0 = call(first_kernel, "first", (info, sample, gusts[0]), args, outs)
    starts = halo(inflow_to(buf, plane))
    buf, plane, sums = section_call(0, (info, sample, gusts[1]), (*starts, sums0))
    bufs = halo(inflow_to(buf, plane))
    totals = every(sums, ("role", "gx", "gy"), 256)
    buf, plane, sums = section_call(1, (info, sample, gusts[2]), (*starts, *bufs, totals))
    bufs = halo(inflow_to(buf, plane))
    totals = every(sums, "gy", 8)
    (chunks,) = section_call(2, (info,), (*starts, *bufs, totals))
    chunks = lax.all_to_all(chunks.reshape(BLOCKS, 5, ROWS, NX), "gx", 0, 0)
    (out,) = call(last_kernel, "last", (info,), (chunks,), [shape(4, 128, 128)])
    return out.reshape(1, 4, NZ, 8, 128)


def solution(mesh):
    placed = (P("role", None, None, "gx", "gy"), P(None, "gx", "gy"), P("gy"), P(), P("gy"))
    return jax.shard_map(
        per_device,
        mesh=mesh,
        in_specs=placed,
        out_specs=P("role", None, None, "gx", "gy"),
        check_vma=False,
    )
```

time: 1910 us -> 134 us (0.07)
  blocking collectives: 1200 us -> 55.9 us
  local copies, waits for them, and re-layouts: 244 us -> 2.41 us
  waiting for transfers between devices: 224 us -> 24.2 us
  starting transfers between devices: 216 us -> 25.5 us
  Pallas kernels: 0 us -> 23.4 us
    psum x6 -> x0, blocking collectives: 1200 us -> none  [the longest x3 978 us: per_device(): level_sums = lax.psum(jnp.sum(current[3], axis=(1, 2)), ('gx', 'gy'))]
    gather x3 -> x0, local copies, waits for them, and re-layouts: 236 us -> none  [per_device(): local_plane = jnp.take_along_axis(current, sample_index, axis=2)[:, :, 0, :]]
    ppermute x103 -> x9, waiting for transfers between devices: 224 us -> 13.9 us  [the longest x6 11.5 us: around(): return lax.ppermute(cells, ('gx', 'gy'), route)]
    ppermute x103 -> x9, starting transfers between devices: 216 us -> 14.3 us  [the longest x6 9.86 us: around(): return lax.ppermute(cells, ('gx', 'gy'), route)]
    all_to_all x0 -> x3, blocking collectives: none -> 55.9 us  [the longest x2 33 us: every(): lax.all_to_all(jnp.broadcast_to(row[None], (count, 1, NX)), axes, 0, 0)]
    pallas_call x0 -> x6, Pallas kernels: none -> 23.4 us  [call(): pl.pallas_call(body, name=name, out_shape=outs, in_specs=[SMEM] * len(sma...]
  transfers between devices with their start and end apart: 103 -> 10, of which waited for: 88 -> 6; matrix products, arithmetic and copies ran while one was open for 4% -> 0% of each run, Pallas kernels for 0% -> 0%
where the time goes in v1:
time: 134 us; the launch traced here: 133 us
  blocking collectives  55.9 us (42%)
  starting transfers between devices  25.5 us (19%)
  waiting for transfers between devices  24.2 us (18%)
  Pallas kernels  23.4 us (17%)
  local copies, waits for them, and re-layouts  2.41 us (2%)
    all_to_all x2, blocking collectives, every(): lax.all_to_all(jnp.broadcast_to(row[None], (count, 1, NX)), axes, 0, 0)  33 us
    pallas_call x6, Pallas kernels, call(): pl.pallas_call(body, name=name, out_shape=outs, in_specs=[SMEM] * len(sma...  23.4 us
    all_to_all x1, blocking collectives, per_device(): chunks = lax.all_to_all(chunks.reshape(BLOCKS, 5, ROWS, NX), 'gx', 0, 0)  22.9 us
    ppermute x6, waiting for transfers between devices, around(): return lax.ppermute(cells, ('gx', 'gy'), route)  11.5 us
    all_to_all x1, starting transfers between devices, per_device(): chunks = lax.all_to_all(chunks, 'gx', 0, 0)  11.2 us
    all_to_all x1, waiting for transfers between devices, per_device(): chunks = lax.all_to_all(chunks, 'gx', 0, 0)  10.3 us
    ppermute x6, starting transfers between devices, around(): return lax.ppermute(cells, ('gx', 'gy'), route)  9.86 us
    ppermute x3, starting transfers between devices, inflow_to(): plane = lax.ppermute(plane, 'role', [(0, 1)])  4.46 us
  transfers between devices with their start and end apart: 10, of which 6 were waited for; matrix products, arithmetic and copies ran while one was open for 0% of the time, Pallas kernels for 0%

profile of v1, /device:TPU:32, one launch (start us, length us, event | category | flops | bytes accessed | tf_op | source)
XLA Modules:
  0.0 133.4 jit_solution(4894331366950876188)
XLA Ops:
  0.0 0.8 select_bitcast_fusion.drag
  0.8 0.1 pad_add_fusion.info
  0.9 0.9 copy-done
  1.9 1.4 %pack.1 = f32[16,5,8,128]{3,2,1,0:T(8,128)} custom-call(s32[3]{0:T(128)S(1)} %pad_add_fusion.info, f32[4,128,128]{2,1,0:T(8,128)S(1)} %bitcast.19, f32[128,128]{1,0:T(8,128)S(1)} %select_bitcast_fusion.drag), custom_call_target="tpu_custom_call" | custom-call | tf_op jit(solution)/shard_map/pack/pallas_call | solution.py:347
  3.3 11.2 %all-to-all-start = ((f32[16,5,8,128]{3,2,1,0:T(8,128)}), f32[16,5,8,128]{3,2,1,0:T(8,128)S(1)}, u32[]{:S(2)}, u32[]{:S(2)}) async-start(f32[16,5,8,128]{3,2,1,0:T(8,128)} %pack.1), calls=%async_computation | async-start | bytes 655360 | tf_op jit(solution)/shard_map/all_to_all | solution.py:416
  15.4 0.6 copy-done.2
  16.1 0.1 dynamic_slice.6.sample.refs_0_
  16.1 0.7 copy-done.1
  16.8 0.1 broadcast_multiply_fusion
  16.9 10.3 %all-to-all-done = f32[16,5,8,128]{3,2,1,0:T(8,128)S(1)} async-done(((f32[16,5,8,128]{3,2,1,0:T(8,128)}), f32[16,5,8,128]{3,2,1,0:T(8,128)S(1)}, u32[]{:S(2)}, u32[]{:S(2)}) %all-to-all-start) | async-done | bytes 327712 | tf_op jit(solution)/shard_map/all_to_all | solution.py:416
  27.2 6.0 %first.1 = (f32[656,128]{1,0:T(8,128)S(1)}, f32[16,128]{1,0:T(8,128)S(1)}, f32[1,128]{1,0:T(1,128)S(1)}) custom-call(s32[3]{0:T(128)S(1)} %pad_add_fusion.info, s32[8]{0:T(128)S(1)} %dynamic_slice.6.sample.refs_0_, f32[8]{0:T(128)S(1)} %get-tuple-element.25.gust, f32[640,128]{1,0:T(8,128)S(1)} %bitcast.17), custom_call_target="tpu_custom_call" | custom-call | tf_op jit(solution)/shard_map/first/pallas_call | solution.py:347
  33.2 1.3 collective-permute-start
  34.5 0.8 collective-permute-done
  35.3 0.3 collective-permute-start.2
  35.6 1.7 %collective-permute-start.1 = (f32[656,128]{1,0:T(8,128)S(1)}, f32[656,128]{1,0:T(8,128)S(1)}, u32[]{:S(2)}, u32[]{:S(2)}) collective-permute-start(f32[656,128]{1,0:T(8,128)S(1)} %constant_dynamic-update-slice_fusion.2.refs_3_.refs_1_), channel_id=1, source_target_pairs={{0,8},{8,16},{16,24},{24,32},{32,40},{40,48},{48,56},{56,120},{120... | collective-permute-start | bytes 1007624 | tf_op jit(solution)/shard_map/ppermute | solution.py:382
  37.3 8.1 %collective-permute-done.2.refs_4_.refs_2_ = f32[656,128]{1,0:T(8,128)S(1)} collective-permute-done((f32[656,128]{1,0:T(8,128)S(1)}, f32[656,128]{1,0:T(8,128)S(1)}, u32[]{:S(2)}, u32[]{:S(2)}) %collective-permute-start.2) | collective-permute-done | bytes 335904 | tf_op jit(solution)/shard_map/ppermute | solution.py:382
  45.4 3.4 %collective-permute-done.1.refs_2_.refs_0_ = f32[656,128]{1,0:T(8,128)S(1)} collective-permute-done((f32[656,128]{1,0:T(8,128)S(1)}, f32[656,128]{1,0:T(8,128)S(1)}, u32[]{:S(2)}, u32[]{:S(2)}) %collective-permute-start.1) | collective-permute-done | bytes 335904 | tf_op jit(solution)/shard_map/ppermute | solution.py:382
  48.8 3.8 %section0.1 = (f32[528,128]{1,0:T(8,128)S(1)}, f32[16,128]{1,0:T(8,128)S(1)}, f32[1,128]{1,0:T(1,128)S(1)}) custom-call(s32[3]{0:T(128)S(1)} %pad_add_fusion.info, s32[8]{0:T(128)S(1)} %dynamic_slice.6.sample.refs_0_, f32[8]{0:T(128)S(1)} %get-tuple-element.23.refs_1_, f32[656,128]{1,0:T(8,128)S(1)} %collective-permute-done.1.refs_2_.refs_0_, ...), custom_call_target="tpu_custom_call" | custom-call | tf_op jit(solution)/shard_map/section0/pallas_call | solution.py:347
  52.6 1.4 %collective-permute-start.3 = (f32[16,128]{1,0:T(8,128)S(1)}, f32[16,128]{1,0:T(8,128)S(1)}, u32[]{:S(2)}, u32[]{:S(2)}) collective-permute-start(f32[16,128]{1,0:T(8,128)S(1)} %get-tuple-element.18), channel_id=1, source_target_pairs={{0,128},{1,129},{2,130},{3,131},{4,132},{5,133},{6,134},{7,135},{8... | collective-permute-start | bytes 24584 | tf_op jit(solution)/shard_map/ppermute | solution.py:386
  54.1 0.8 collective-permute-done.3
  54.9 5.8 %collective-permute-start.5 = (f32[528,128]{1,0:T(8,128)S(1)}, f32[528,128]{1,0:T(8,128)S(1)}, u32[]{:S(2)}, u32[]{:S(2)}) collective-permute-start(f32[528,128]{1,0:T(8,128)S(1)} %constant_dynamic-update-slice_fusion.1.refs_6_), channel_id=1, source_target_pairs={{0,63},{8,0},{16,8},{24,16},{32,24},{40,32},{48,40},{56,48},{120,5... | collective-permute-start | bytes 811016 | tf_op jit(solution)/shard_map/ppermute | solution.py:382
  60.7 0.1 broadcast_in_dim.22
  60.8 23.9 %all_to_all.20 = f32[256,1,128]{2,1,0:T(1,128)S(1)} all-to-all(f32[256,1,128]{2,1,0:T(1,128)S(1)} %broadcast_in_dim.22), channel_id=1, replica_groups=mesh['role'=2,'gx'=16,'gy'=8] {'role','gx','gy'}, dimensions={0} | all-to-all | bytes 262144 | tf_op jit(solution)/shard_map/all_to_all | solution.py:395
  84.7 4.2 %section1.1 = (f32[528,128]{1,0:T(8,128)S(1)}, f32[16,128]{1,0:T(8,128)S(1)}, f32[1,128]{1,0:T(1,128)S(1)}) custom-call(s32[3]{0:T(128)S(1)} %pad_add_fusion.info, s32[8]{0:T(128)S(1)} %dynamic_slice.6.sample.refs_0_, f32[8]{0:T(128)S(1)} %get-tuple-element.24.refs_1_, f32[656,128]{1,0:T(8,128)S(1)} %collective-permute-done.1.refs_2_.refs_0_, ...), custom_call_target="tpu_custom_call" | custom-call | tf_op jit(solution)/shard_map/section1/pallas_call | solution.py:347
  88.9 1.7 %collective-permute-start.6 = (f32[16,128]{1,0:T(8,128)S(1)}, f32[16,128]{1,0:T(8,128)S(1)}, u32[]{:S(2)}, u32[]{:S(2)}) collective-permute-start(f32[16,128]{1,0:T(8,128)S(1)} %get-tuple-element.21), channel_id=1, source_target_pairs={{0,128},{1,129},{2,130},{3,131},{4,132},{5,133},{6,134},{7,135},{8... | collective-permute-start | bytes 24584 | tf_op jit(solution)/shard_map/ppermute | solution.py:386
  90.6 0.8 collective-permute-done.6
  91.4 1.0 collective-permute-start.8
  92.4 1.0 collective-permute-start.7
  93.5 9.1 %all_to_all.21 = f32[8,1,128]{2,1,0:T(1,128)S(1)} all-to-all(f32[8,1,128]{2,1,0:T(1,128)S(1)} %broadcast_in_dim.24), channel_id=1, replica_groups=mesh['role'=2,'gx'=16,'gy'=8] {'gy'}, dimensions={0} | all-to-all | bytes 8192 | tf_op jit(solution)/shard_map/all_to_all | solution.py:395
  102.5 6.0 %section2.1 = f32[640,128]{1,0:T(8,128)S(1)} custom-call(s32[3]{0:T(128)S(1)} %pad_add_fusion.info, f32[656,128]{1,0:T(8,128)S(1)} %collective-permute-done.1.refs_2_.refs_0_, f32[656,128]{1,0:T(8,128)S(1)} %constant_dynamic-update-slice_fusion.2.refs_3_.refs_1_, f32[656,128]{1,0:T(8,128)S(1)} %collective-permute-done.2.refs_4_.refs_2_, ...), custom_call_target="tpu_custom_call" | custom-call | tf_op jit(solution)/shard_map/section2/pallas_call | solution.py:347
  108.5 22.9 %all_to_all.22.chunks = f32[16,5,8,128]{3,2,1,0:T(8,128)S(1)} all-to-all(f32[16,5,8,128]{3,2,1,0:T(8,128)S(1)} %bitcast.16), channel_id=1, replica_groups=mesh['role'=2,'gx'=16,'gy'=8] {'gx'}, dimensions={0} | all-to-all | bytes 655360 | tf_op jit(solution)/shard_map/all_to_all | solution.py:428
  131.4 2.0 %last.1 = f32[4,128,128]{2,1,0:T(8,128)} custom-call(s32[3]{0:T(128)S(1)} %pad_add_fusion.info, f32[16,5,8,128]{3,2,1,0:T(8,128)S(1)} %all_to_all.22.chunks), custom_call_target="tpu_custom_call" | custom-call | tf_op jit(solution)/shard_map/last/pallas_call | solution.py:347
  (12 shorter events, 0.0 us)
Async XLA Ops:
  0.9 1.0 copy-start
  3.3 23.9 %all-to-all-start = ((f32[16,5,8,128]{3,2,1,0:T(8,128)}), f32[16,5,8,128]{3,2,1,0:T(8,128)S(1)}, u32[]{:S(2)}, u32[]{:S(2)}) async-start(f32[16,5,8,128]{3,2,1,0:T(8,128)} %pack.1), calls=%async_computation | async-start | bytes 655360 | tf_op jit(solution)/shard_map/all_to_all | solution.py:416
  15.4 0.7 copy-start.2
  16.1 0.7 copy-start.1
  33.2 2.1 %collective-permute-start = (f32[16,128]{1,0:T(8,128)S(1)}, f32[16,128]{1,0:T(8,128)S(1)}, u32[]{:S(2)}, u32[]{:S(2)}) collective-permute-start(f32[16,128]{1,0:T(8,128)S(1)} %get-tuple-element.15), channel_id=1, source_target_pairs={{0,128},{1,129},{2,130},{3,131},{4,132},{5,133},{6,134},{7,135},{8... | collective-permute-start | bytes 24584 | tf_op jit(solution)/shard_map/ppermute | solution.py:386
  35.3 10.1 %collective-permute-start.2 = (f32[656,128]{1,0:T(8,128)S(1)}, f32[656,128]{1,0:T(8,128)S(1)}, u32[]{:S(2)}, u32[]{:S(2)}) collective-permute-start(f32[656,128]{1,0:T(8,128)S(1)} %constant_dynamic-update-slice_fusion.2.refs_3_.refs_1_), channel_id=1, source_target_pairs={{0,63},{8,0},{16,8},{24,16},{32,24},{40,32},{48,40},{56,48},{120,5... | collective-permute-start | bytes 1007624 | tf_op jit(solution)/shard_map/ppermute | solution.py:382
  35.6 13.2 %collective-permute-start.1 = (f32[656,128]{1,0:T(8,128)S(1)}, f32[656,128]{1,0:T(8,128)S(1)}, u32[]{:S(2)}, u32[]{:S(2)}) collective-permute-start(f32[656,128]{1,0:T(8,128)S(1)} %constant_dynamic-update-slice_fusion.2.refs_3_.refs_1_), channel_id=1, source_target_pairs={{0,8},{8,16},{16,24},{24,32},{32,40},{40,48},{48,56},{56,120},{120... | collective-permute-start | bytes 1007624 | tf_op jit(solution)/shard_map/ppermute | solution.py:382
  52.6 2.3 %collective-permute-start.3 = (f32[16,128]{1,0:T(8,128)S(1)}, f32[16,128]{1,0:T(8,128)S(1)}, u32[]{:S(2)}, u32[]{:S(2)}) collective-permute-start(f32[16,128]{1,0:T(8,128)S(1)} %get-tuple-element.18), channel_id=1, source_target_pairs={{0,128},{1,129},{2,130},{3,131},{4,132},{5,133},{6,134},{7,135},{8... | collective-permute-start | bytes 24584 | tf_op jit(solution)/shard_map/ppermute | solution.py:386
  54.9 29.8 %collective-permute-start.5 = (f32[528,128]{1,0:T(8,128)S(1)}, f32[528,128]{1,0:T(8,128)S(1)}, u32[]{:S(2)}, u32[]{:S(2)}) collective-permute-start(f32[528,128]{1,0:T(8,128)S(1)} %constant_dynamic-update-slice_fusion.1.refs_6_), channel_id=1, source_target_pairs={{0,63},{8,0},{16,8},{24,16},{32,24},{40,32},{48,40},{56,48},{120,5... | collective-permute-start | bytes 811016 | tf_op jit(solution)/shard_map/ppermute | solution.py:382
  60.7 24.0 %collective-permute-start.4 = (f32[528,128]{1,0:T(8,128)S(1)}, f32[528,128]{1,0:T(8,128)S(1)}, u32[]{:S(2)}, u32[]{:S(2)}) collective-permute-start(f32[528,128]{1,0:T(8,128)S(1)} %constant_dynamic-update-slice_fusion.1.refs_6_), channel_id=1, source_target_pairs={{0,8},{8,16},{16,24},{24,32},{32,40},{40,48},{48,56},{56,120},{120... | collective-permute-start | bytes 811016 | tf_op jit(solution)/shard_map/ppermute | solution.py:382
  88.9 2.5 %collective-permute-start.6 = (f32[16,128]{1,0:T(8,128)S(1)}, f32[16,128]{1,0:T(8,128)S(1)}, u32[]{:S(2)}, u32[]{:S(2)}) collective-permute-start(f32[16,128]{1,0:T(8,128)S(1)} %get-tuple-element.21), channel_id=1, source_target_pairs={{0,128},{1,129},{2,130},{3,131},{4,132},{5,133},{6,134},{7,135},{8... | collective-permute-start | bytes 24584 | tf_op jit(solution)/shard_map/ppermute | solution.py:386
  91.4 11.1 %collective-permute-start.8 = (f32[528,128]{1,0:T(8,128)S(1)}, f32[528,128]{1,0:T(8,128)S(1)}, u32[]{:S(2)}, u32[]{:S(2)}) collective-permute-start(f32[528,128]{1,0:T(8,128)S(1)} %constant_dynamic-update-slice_fusion.refs_4_), channel_id=1, source_target_pairs={{0,63},{8,0},{16,8},{24,16},{32,24},{40,32},{48,40},{56,48},{120,5... | collective-permute-start | bytes 811016 | tf_op jit(solution)/shard_map/ppermute | solution.py:382
  92.4 10.1 %collective-permute-start.7 = (f32[528,128]{1,0:T(8,128)S(1)}, f32[528,128]{1,0:T(8,128)S(1)}, u32[]{:S(2)}, u32[]{:S(2)}) collective-permute-start(f32[528,128]{1,0:T(8,128)S(1)} %constant_dynamic-update-slice_fusion.refs_4_), channel_id=1, source_target_pairs={{0,8},{8,16},{16,24},{24,32},{32,40},{40,48},{48,56},{56,120},{120... | collective-permute-start | bytes 811016 | tf_op jit(solution)/shard_map/ppermute | solution.py:382

commit v2 on v1

--- a/solution.py
+++ b/solution.py
@@ -92,21 +92,29 @@
     return jnp.broadcast_to(mean, (NZ, NX))
 
 
-def swap_blocks(v):
-    row = levels()
-    group = lanes() // 8
-    for bit in (8, 4, 2, 1):
-        row_set = (row & bit) != 0
-        group_set = (group & bit) != 0
-        from_low = turn(turn(v, NZ - bit, 0), 8 * bit, 1)
-        from_high = turn(turn(v, bit, 0), NX - 8 * bit, 1)
-        v = jnp.where(row_set == group_set, v, jnp.where(row_set, from_high, from_low))
-    return v
+def role_totals(rows, role):
+    pre = jnp.sum(rows[:8], axis=0, keepdims=True)
+    suc = jnp.sum(rows[8:], axis=0, keepdims=True)
+    return pre, jnp.where(role == 0, pre, suc)
+
+
+def skewed(tiles):
+    group = lanes(ROWS) // 8
+    tiles = [tiles[-i % BLOCKS] for i in range(BLOCKS)]
+    for bit in (1, 2, 4, 8):
+        moved = (group & bit) != 0
+        tiles = [jnp.where(moved, tiles[(i - bit) % BLOCKS], tiles[i]) for i in range(BLOCKS)]
+    return tiles
+
+
+def turned(tile, groups):
+    shift = 8 * groups % NX
+    return turn(tile, shift, 1) if shift else tile
 
 
 def owner_of(block, flip):
     straight = block if block < 8 else 23 - block
-    other = 15 - block if block < 8 else block - 8
+    other = (8 if block == 0 else 16 - block) if block < 8 else (block - 7) % 8
     return jnp.where(flip == 0, straight, other)
 
 
@@ -126,6 +134,7 @@
     flip = info[1]
     for f in range(5):
         flat = (state[f] if f < 4 else drag[...]).T
+        flat = turn(flat, ROWS * info[2], 1)
         for block in range(BLOCKS):
             out[owner_of(block, flip), f] = flat[ROWS * block : ROWS * (block + 1)]
 
@@ -135,18 +144,20 @@
     picked = jnp.zeros((NZ, NX), jnp.float32)
     sums = jnp.zeros((NZ, NX), jnp.float32)
     for f in range(5):
+        tiles = skewed([chunks[s, f] for s in range(BLOCKS)])
+        for z in range(NZ):
+            buf[pl.ds(f * FIELD + z, ROWS, stride=NZ), :] = turned(tiles[z], -z)
+    for f in range(4):
         for r in range(ROWS):
             spot = f * ROWS + r
-            cells = swap_blocks(chunks[pl.ds(spot, BLOCKS, stride=5 * ROWS), :])
-            buf[spot * NZ : (spot + 1) * NZ, :] = cells
-            if f < 4:
-                picked = sampled(picked, f, r, cells, sample)
+            cells = buf[spot * NZ : (spot + 1) * NZ, :]
+            picked = sampled(picked, f, r, cells, sample)
             if f == 3:
                 sums = sums + cells
+    sums_out[...] = level_lanes(jnp.sum(sums, axis=1, keepdims=True))
     picked = with_gust(picked, gust)
     plane[...] = picked
     buf[5 * FIELD :, :] = picked
-    sums_out[...] = level_lanes(jnp.sum(sums, axis=1, keepdims=True))
 
 
 def section_kernel(section, info, *refs):
@@ -161,31 +172,30 @@
         sample, gust = take(2)
     starts = take(3)
     bufs = take(3) if section else starts
-    if section < 2 or section == 2:
-        (sums_in,) = take(1)
+    (sums_in,) = take(1)
     if section < 2:
         new_out, plane_out, sums_out = take(3)
     else:
         (chunks_out,) = take(1)
-    ext, tent, press, src, face = refs
+    ext, tent, press, src, face, natural = refs
 
     role = info[0]
     step = SECTION_C[section] * DT
     walls = Walls(role == 1)
     plane_at = (4 if section else 5) * FIELD
 
-    if section == 1:
-        totals = jnp.concatenate(
-            [
-                jnp.sum(sums_in[: sums_in.shape[0] // 2], axis=0, keepdims=True),
-                jnp.sum(sums_in[sums_in.shape[0] // 2 :], axis=0, keepdims=True),
-            ]
-        )
-        own = jnp.where(role == 0, totals[:1], totals[1:])
-        prev_step = SECTION_C[0] * DT
-        d_u, d_w = mean_change(walls, lane_means(own, 0), prev_step)
-        _, pre_w = mean_change(Walls(role < 0), lane_means(totals[:1], 0), prev_step)
-        mean = lane_means(own, NZ)
+    if section:
+        if section == 1:
+            row = jnp.sum(sums_in[...], axis=0, keepdims=True)
+            pre = turn(row, NX - NZ, 1)
+            own = jnp.where(role == 0, pre, turn(row, NX - 2 * NZ, 1))
+            spot = 0
+        else:
+            pre, own = role_totals(sums_in, role)
+            spot = NZ
+        prev_step = SECTION_C[section - 1] * DT
+        d_u, d_w = mean_change(walls, lane_means(own, spot), prev_step)
+        _, pre_w = mean_change(Walls(role < 0), lane_means(pre, spot), prev_step)
 
     for side in range(3):
         plane = bufs[side][plane_at : plane_at + NZ, :]
@@ -196,9 +206,9 @@
                 cells = bufs[side][at : at + NZ, :]
                 shift = (NX - (f * ROWS + r)) % NX
                 ghost = turn(plane, shift, 1) if shift else plane
-                if section == 1 and f == 0:
+                if section and f == 0:
                     cells = cells + d_u
-                if section == 1 and f == 2:
+                if section and f == 2:
                     cells = cells + d_w
                     ghost = ghost + pre_w
                 ext[f, j] = cells
@@ -231,7 +241,7 @@
         rates[0] = rates[0] - resist * u
         rates[1] = rates[1] - resist * v
         theta = ext[3, j]
-        rates[2] = rates[2] + BETA * (theta - mean if section == 1 else theta)
+        rates[2] = rates[2] + BETA * theta
         for f in range(3):
             at = pl.multiple_of((f * ROWS + r) * NZ, NZ)
             tent[f, j] = starts[side][pl.ds(at, NZ), :] + step * rates[f]
@@ -261,9 +271,9 @@
         heat_row(r, *rate_row(1, r))
         return carry
 
-    lax.fori_loop(1, ROWS, functools.partial(outer, 0), 0)
-    lax.fori_loop(0, ROWS, inner, 0)
-    lax.fori_loop(0, ROWS - 1, functools.partial(outer, 2), 0)
+    lax.fori_loop(1, ROWS, functools.partial(outer, 0), 0, unroll=True)
+    lax.fori_loop(0, ROWS, inner, 0, unroll=True)
+    lax.fori_loop(0, ROWS - 1, functools.partial(outer, 2), 0, unroll=True)
 
     for j in range(2, EXT - 2):
         u = tent[0, j]
@@ -301,19 +311,32 @@
                 new_out[spot * NZ : (spot + 1) * NZ, :] = fresh[f]
                 picked = sampled(picked, f, r, fresh[f], sample)
             else:
-                chunks_out[pl.ds(spot, BLOCKS, stride=5 * ROWS), :] = swap_blocks(fresh[f])
+                natural[pl.ds(f * FIELD + r, NZ, stride=ROWS), :] = fresh[f]
         sums = sums + fresh[3]
     if section < 2:
         picked = with_gust(picked, gust)
         new_out[plane_at if section else 4 * FIELD :, :] = picked
         plane_out[...] = picked
         row = level_lanes(jnp.sum(sums, axis=1, keepdims=True))
-        sums_out[...] = turn(row, NZ, 1) + sums_in[...] if section == 0 else row
+        if section == 0:
+            for part in range(2):
+                rows = sums_in[8 * part : 8 * (part + 1)]
+                row = row + turn(jnp.sum(rows, axis=0, keepdims=True), NZ * (part + 1), 1)
+        else:
+            kept = jnp.where(lanes(1) < NZ, jnp.sum(sums_in[...], axis=0, keepdims=True), 0.0)
+            row = row + turn(kept, NZ, 1)
+        sums_out[...] = row
     else:
-        row = jnp.sum(sums_in[...], axis=0, keepdims=True)
-        for block in range(BLOCKS):
-            at = (block * 5 + 4) * ROWS
-            chunks_out[at : at + ROWS, :] = jnp.broadcast_to(row, (ROWS, NX))
+        for f in range(4):
+            tiles = []
+            for z in range(NZ):
+                at = f * FIELD + z * ROWS
+                tiles.append(turned(natural[at : at + ROWS, :], z))
+            tiles = skewed(tiles)
+            for s in range(BLOCKS):
+                chunks_out[s, f] = tiles[s]
+        for s in range(BLOCKS):
+            chunks_out[s, 4] = jnp.broadcast_to(own, (ROWS, NX))
 
 
 def last_kernel(info, chunks, out):
@@ -327,7 +350,7 @@
     shift = lax.rem(NX - ROWS * gx, NX)
     for f in range(4):
         flat = jnp.concatenate([chunks[owner_of(block, flip), f] for block in range(BLOCKS)])
-        out[f] = flat.T
+        out[f] = turn(flat, shift, 1).T
         if f in (0, 2):
             change = turn(changes[f // 2], shift, 1)
             for x in range(8):
@@ -359,10 +382,11 @@
     if section < 2:
         outs = [shape(4 * FIELD + NZ, NX), shape(NZ, NX), shape(1, NX)]
     else:
-        outs = [shape(BLOCKS * 5 * ROWS, NX)]
+        outs = [shape(BLOCKS, 5, ROWS, NX)]
     row = (NZ, NX)
     scratch = [(4, EXT), (4, EXT), (2, EXT), (EXT,), (4, EXT)]
     scratch = [pltpu.VMEM((*lead, *row), jnp.float32) for lead in scratch]
+    scratch.append(pltpu.VMEM((4 * FIELD, NX), jnp.float32))
     body = functools.partial(section_kernel, section)
     return call(body, f"section{section}", small, args, outs, scratch)
 
@@ -370,9 +394,9 @@
 def ring_order():
     order = []
     for gy in range(8):
-        low = list(range(8))
-        high = list(range(15, 7, -1))
-        order += [gx * 8 + gy for gx in (low + high if gy % 2 == 0 else high + low)]
+        even = [*range(8), *range(15, 7, -1)]
+        odd = [8, *range(15, 8, -1), *range(1, 8), 0]
+        order += [gx * 8 + gy for gx in (odd if gy % 2 else even)]
     return order
 
 
@@ -401,7 +425,9 @@
     flip = lax.axis_index("gy") % 2
     info = jnp.stack([role, flip, gx]).astype(jnp.int32)
     drag = jnp.where(role == 1, CDRAG * turbine_mask.astype(jnp.float32), 0.0)
-    block = jnp.where(gx < 8, jnp.where(flip == 0, gx, gx + 8), jnp.where(flip == 0, 23 - gx, 15 - gx))
+    even = jnp.where(gx < 8, gx, 23 - gx)
+    odd = jnp.where(gx < 8, 8 + (gx + 7) % 8, jnp.where(gx == 8, 0, 16 - gx))
+    block = jnp.where(flip == 0, even, odd)
     sample = lax.dynamic_slice(sample_x, (block * ROWS,), (ROWS,)).astype(jnp.int32)
     level = lax.dynamic_slice(gust_level, (block * ROWS,), (ROWS,))
     amp = 1.5 + level.astype(jnp.float32)
@@ -415,17 +441,18 @@
     (chunks,) = call(pack_kernel, "pack", (info,), args, [shape(BLOCKS, 5, ROWS, NX)])
     chunks = lax.all_to_all(chunks, "gx", 0, 0)
     outs = [shape(5 * FIELD + NZ, NX), shape(NZ, NX), shape(1, NX)]
-    args = (chunks.reshape(BLOCKS * 5 * ROWS, NX),)
-    buf, plane, sums0 = call(first_kernel, "first", (info, sample, gusts[0]), args, outs)
+    args = (chunks,)
+    buf, plane, sums = call(first_kernel, "first", (info, sample, gusts[0]), args, outs)
     starts = halo(inflow_to(buf, plane))
-    buf, plane, sums = section_call(0, (info, sample, gusts[1]), (*starts, sums0))
+    totals = every(sums, ("role", "gy"), 16)
+    buf, plane, sums = section_call(0, (info, sample, gusts[1]), (*starts, totals))
     bufs = halo(inflow_to(buf, plane))
-    totals = every(sums, ("role", "gx", "gy"), 256)
+    totals = every(sums, "gx", 16)
     buf, plane, sums = section_call(1, (info, sample, gusts[2]), (*starts, *bufs, totals))
     bufs = halo(inflow_to(buf, plane))
-    totals = every(sums, "gy", 8)
+    totals = every(sums, ("role", "gy"), 16)
     (chunks,) = section_call(2, (info,), (*starts, *bufs, totals))
-    chunks = lax.all_to_all(chunks.reshape(BLOCKS, 5, ROWS, NX), "gx", 0, 0)
+    chunks = lax.all_to_all(chunks, "gx", 0, 0)
     (out,) = call(last_kernel, "last", (info,), (chunks,), [shape(4, 128, 128)])
     return out.reshape(1, 4, NZ, 8, 128)
 

time: 134 us -> 105 us (0.78)
  waiting for transfers between devices: 24.2 us -> 12.8 us
  Pallas kernels: 23.4 us -> 12.1 us
  blocking collectives: 55.9 us -> 53 us
  starting transfers between devices: 25.5 us -> 22.6 us
    ppermute x6, waiting for transfers between devices: 11.5 us -> 0.02 us  [around(): return lax.ppermute(cells, ('gx', 'gy'), route)]
    pallas_call x6, Pallas kernels: 23.4 us -> 12.1 us  [call(): pl.pallas_call(body, name=name, out_shape=outs, in_specs=[SMEM] * len(sma...]
    all_to_all x1, blocking collectives: 22.9 us -> 18.7 us  [per_device(): chunks = lax.all_to_all(chunks, 'gx', 0, 0)]
    ppermute x6, starting transfers between devices: 9.86 us -> 7.14 us  [around(): return lax.ppermute(cells, ('gx', 'gy'), route)]
    all_to_all x2 -> x3, blocking collectives: 33 us -> 34.3 us  [every(): lax.all_to_all(jnp.broadcast_to(row[None], (count, 1, NX)), axes, 0, 0)]
  transfers between devices with their start and end apart: 10 -> 10, of which waited for: 6 -> 4; matrix products, arithmetic and copies ran while one was open for 0% -> 0% of each run, Pallas kernels for 0% -> 0%
where the time goes in v2:
time: 105 us
  blocking collectives  53 us (50%)
  starting transfers between devices  22.6 us (22%)
  waiting for transfers between devices  12.8 us (12%)
  Pallas kernels  12.1 us (12%)
  local copies, waits for them, and re-layouts  2.35 us (2%)
    all_to_all x3, blocking collectives, every(): lax.all_to_all(jnp.broadcast_to(row[None], (count, 1, NX)), axes, 0, 0)  34.3 us
    all_to_all x1, blocking collectives, per_device(): chunks = lax.all_to_all(chunks, 'gx', 0, 0)  18.7 us
    pallas_call x6, Pallas kernels, call(): pl.pallas_call(body, name=name, out_shape=outs, in_specs=[SMEM] * len(sma...  12.1 us
    all_to_all x1, starting transfers between devices, per_device(): chunks = lax.all_to_all(chunks, 'gx', 0, 0)  11.2 us
    all_to_all x1, waiting for transfers between devices, per_device(): chunks = lax.all_to_all(chunks, 'gx', 0, 0)  10.3 us
    ppermute x6, starting transfers between devices, around(): return lax.ppermute(cells, ('gx', 'gy'), route)  7.14 us
    ppermute x3, starting transfers between devices, inflow_to(): plane = lax.ppermute(plane, 'role', [(0, 1)])  4.29 us
    ppermute x3, waiting for transfers between devices, inflow_to(): plane = lax.ppermute(plane, 'role', [(0, 1)])  2.43 us
  transfers between devices with their start and end apart: 10, of which 4 were waited for; matrix products, arithmetic and copies ran while one was open for 0% of the time, Pallas kernels for 0%

profile of v2, /device:TPU:32, one launch (start us, length us, event | category | flops | bytes accessed | tf_op | source)
XLA Modules:
  0.0 104.8 jit_solution(2732217944796359324)
XLA Ops:
  0.0 0.8 select_bitcast_fusion.drag
  0.8 0.1 pad_add_fusion.info
  0.9 0.9 copy-done
  1.9 1.6 %pack.1 = f32[16,5,8,128]{3,2,1,0:T(8,128)} custom-call(s32[3]{0:T(128)S(1)} %pad_add_fusion.info, f32[4,128,128]{2,1,0:T(8,128)S(1)} %bitcast.16, f32[128,128]{1,0:T(8,128)S(1)} %select_bitcast_fusion.drag), custom_call_target="tpu_custom_call" | custom-call | tf_op jit(solution)/shard_map/pack/pallas_call | solution.py:370
  3.4 11.2 %all-to-all-start = ((f32[16,5,8,128]{3,2,1,0:T(8,128)}), f32[16,5,8,128]{3,2,1,0:T(8,128)S(1)}, u32[]{:S(2)}, u32[]{:S(2)}) async-start(f32[16,5,8,128]{3,2,1,0:T(8,128)} %pack.1), calls=%async_computation | async-start | bytes 655360 | tf_op jit(solution)/shard_map/all_to_all | solution.py:442
  15.5 0.0 copy-start.2
  15.6 0.6 copy-done.2
  16.2 0.1 dynamic_slice.6.sample.refs_0_
  16.3 0.7 copy-done.1
  16.9 0.1 broadcast_multiply_fusion
  17.0 10.3 %all-to-all-done.chunks = f32[16,5,8,128]{3,2,1,0:T(8,128)S(1)} async-done(((f32[16,5,8,128]{3,2,1,0:T(8,128)}), f32[16,5,8,128]{3,2,1,0:T(8,128)S(1)}, u32[]{:S(2)}, u32[]{:S(2)}) %all-to-all-start) | async-done | bytes 327712 | tf_op jit(solution)/shard_map/all_to_all | solution.py:442
  27.3 0.8 first.1
  28.2 1.3 %collective-permute-start = (f32[16,128]{1,0:T(8,128)S(1)}, f32[16,128]{1,0:T(8,128)S(1)}, u32[]{:S(2)}, u32[]{:S(2)}) collective-permute-start(f32[16,128]{1,0:T(8,128)S(1)} %get-tuple-element.15), channel_id=1, source_target_pairs={{0,128},{1,129},{2,130},{3,131},{4,132},{5,133},{6,134},{7,135},{8... | collective-permute-start | bytes 24584 | tf_op jit(solution)/shard_map/ppermute | solution.py:410
  29.5 0.8 collective-permute-done
  30.3 0.3 collective-permute-start.2
  30.6 1.7 %collective-permute-start.1 = (f32[656,128]{1,0:T(8,128)S(1)}, f32[656,128]{1,0:T(8,128)S(1)}, u32[]{:S(2)}, u32[]{:S(2)}) collective-permute-start(f32[656,128]{1,0:T(8,128)S(1)} %constant_dynamic-update-slice_fusion.2.refs_3_.refs_1_), channel_id=1, source_target_pairs={{0,8},{8,16},{16,24},{24,32},{32,40},{40,48},{48,56},{56,120},{120... | collective-permute-start | bytes 1007624 | tf_op jit(solution)/shard_map/ppermute | solution.py:406
  32.3 10.4 %all_to_all.25 = f32[16,1,128]{2,1,0:T(1,128)S(1)} all-to-all(f32[16,1,128]{2,1,0:T(1,128)S(1)} %broadcast_in_dim.30), channel_id=1, replica_groups=mesh['role'=2,'gx'=16,'gy'=8] {'role','gy'}, dimensions={0} | all-to-all | bytes 16384 | tf_op jit(solution)/shard_map/all_to_all | solution.py:419
  42.7 0.0 collective-permute-done.2.refs_4_.refs_2_
  42.7 2.5 %section0.1 = (f32[528,128]{1,0:T(8,128)S(1)}, f32[16,128]{1,0:T(8,128)S(1)}, f32[1,128]{1,0:T(1,128)S(1)}) custom-call(s32[3]{0:T(128)S(1)} %pad_add_fusion.info, s32[8]{0:T(128)S(1)} %dynamic_slice.6.sample.refs_0_, f32[8]{0:T(128)S(1)} %get-tuple-element.23.refs_1_, f32[656,128]{1,0:T(8,128)S(1)} %collective-permute-done.1.refs_2_.refs_0_, ...), custom_call_target="tpu_custom_call" | custom-call | tf_op jit(solution)/shard_map/section0/pallas_call | solution.py:370
  45.2 1.7 %collective-permute-start.3 = (f32[16,128]{1,0:T(8,128)S(1)}, f32[16,128]{1,0:T(8,128)S(1)}, u32[]{:S(2)}, u32[]{:S(2)}) collective-permute-start(f32[16,128]{1,0:T(8,128)S(1)} %get-tuple-element.18), channel_id=1, source_target_pairs={{0,128},{1,129},{2,130},{3,131},{4,132},{5,133},{6,134},{7,135},{8... | collective-permute-start | bytes 24584 | tf_op jit(solution)/shard_map/ppermute | solution.py:410
  46.9 0.8 collective-permute-done.3
  47.7 3.1 %collective-permute-start.5 = (f32[528,128]{1,0:T(8,128)S(1)}, f32[528,128]{1,0:T(8,128)S(1)}, u32[]{:S(2)}, u32[]{:S(2)}) collective-permute-start(f32[528,128]{1,0:T(8,128)S(1)} %constant_dynamic-update-slice_fusion.1.refs_6_), channel_id=1, source_target_pairs={{0,7},{8,0},{16,8},{24,16},{32,24},{40,32},{48,40},{56,48},{120,56... | collective-permute-start | bytes 811016 | tf_op jit(solution)/shard_map/ppermute | solution.py:406
  50.8 15.3 %all_to_all.26 = f32[16,1,128]{2,1,0:T(1,128)S(1)} all-to-all(f32[16,1,128]{2,1,0:T(1,128)S(1)} %broadcast_in_dim.32), channel_id=1, replica_groups=mesh['role'=2,'gx'=16,'gy'=8] {'gx'}, dimensions={0} | all-to-all | bytes 16384 | tf_op jit(solution)/shard_map/all_to_all | solution.py:419
  66.1 2.6 %section1.1 = (f32[528,128]{1,0:T(8,128)S(1)}, f32[16,128]{1,0:T(8,128)S(1)}, f32[1,128]{1,0:T(1,128)S(1)}) custom-call(s32[3]{0:T(128)S(1)} %pad_add_fusion.info, s32[8]{0:T(128)S(1)} %dynamic_slice.6.sample.refs_0_, f32[8]{0:T(128)S(1)} %get-tuple-element.24.refs_1_, f32[656,128]{1,0:T(8,128)S(1)} %collective-permute-done.1.refs_2_.refs_0_, ...), custom_call_target="tpu_custom_call" | custom-call | tf_op jit(solution)/shard_map/section1/pallas_call | solution.py:370
  68.7 1.3 %collective-permute-start.6 = (f32[16,128]{1,0:T(8,128)S(1)}, f32[16,128]{1,0:T(8,128)S(1)}, u32[]{:S(2)}, u32[]{:S(2)}) collective-permute-start(f32[16,128]{1,0:T(8,128)S(1)} %get-tuple-element.21), channel_id=1, source_target_pairs={{0,128},{1,129},{2,130},{3,131},{4,132},{5,133},{6,134},{7,135},{8... | collective-permute-start | bytes 24584 | tf_op jit(solution)/shard_map/ppermute | solution.py:410
  70.0 0.8 collective-permute-done.6
  70.8 1.4 %collective-permute-start.8 = (f32[528,128]{1,0:T(8,128)S(1)}, f32[528,128]{1,0:T(8,128)S(1)}, u32[]{:S(2)}, u32[]{:S(2)}) collective-permute-start(f32[528,128]{1,0:T(8,128)S(1)} %constant_dynamic-update-slice_fusion.refs_4_), channel_id=1, source_target_pairs={{0,7},{8,0},{16,8},{24,16},{32,24},{40,32},{48,40},{56,48},{120,56... | collective-permute-start | bytes 811016 | tf_op jit(solution)/shard_map/ppermute | solution.py:406
  72.3 0.6 collective-permute-start.7
  72.9 8.6 %all_to_all.27 = f32[16,1,128]{2,1,0:T(1,128)S(1)} all-to-all(f32[16,1,128]{2,1,0:T(1,128)S(1)} %broadcast_in_dim.34), channel_id=1, replica_groups=mesh['role'=2,'gx'=16,'gy'=8] {'role','gy'}, dimensions={0} | all-to-all | bytes 16384 | tf_op jit(solution)/shard_map/all_to_all | solution.py:419
  81.4 2.5 %section2.1 = f32[16,5,8,128]{3,2,1,0:T(8,128)S(1)} custom-call(s32[3]{0:T(128)S(1)} %pad_add_fusion.info, f32[656,128]{1,0:T(8,128)S(1)} %collective-permute-done.1.refs_2_.refs_0_, f32[656,128]{1,0:T(8,128)S(1)} %constant_dynamic-update-slice_fusion.2.refs_3_.refs_1_, f32[656,128]{1,0:T(8,128)S(1)} %collective-permute-done.2.refs_4_.refs_2_, ...), custom_call_target="tpu_custom_call" | custom-call | tf_op jit(solution)/shard_map/section2/pallas_call | solution.py:370
  83.9 18.7 %all_to_all.28.chunks = f32[16,5,8,128]{3,2,1,0:T(8,128)S(1)} all-to-all(f32[16,5,8,128]{3,2,1,0:T(8,128)S(1)} %section2.1), channel_id=1, replica_groups=mesh['role'=2,'gx'=16,'gy'=8] {'gx'}, dimensions={0} | all-to-all | bytes 655360 | tf_op jit(solution)/shard_map/all_to_all | solution.py:455
  102.7 2.2 %last.1 = f32[4,128,128]{2,1,0:T(8,128)} custom-call(s32[3]{0:T(128)S(1)} %pad_add_fusion.info, f32[16,5,8,128]{3,2,1,0:T(8,128)S(1)} %all_to_all.28.chunks), custom_call_target="tpu_custom_call" | custom-call | tf_op jit(solution)/shard_map/last/pallas_call | solution.py:370
  (14 shorter events, 0.0 us)
Async XLA Ops:
  0.9 1.0 copy-start
  3.4 23.9 %all-to-all-start = ((f32[16,5,8,128]{3,2,1,0:T(8,128)}), f32[16,5,8,128]{3,2,1,0:T(8,128)S(1)}, u32[]{:S(2)}, u32[]{:S(2)}) async-start(f32[16,5,8,128]{3,2,1,0:T(8,128)} %pack.1), calls=%async_computation | async-start | bytes 655360 | tf_op jit(solution)/shard_map/all_to_all | solution.py:442
  15.5 0.7 copy-start.2
  16.3 0.7 copy-start.1
  28.2 2.1 %collective-permute-start = (f32[16,128]{1,0:T(8,128)S(1)}, f32[16,128]{1,0:T(8,128)S(1)}, u32[]{:S(2)}, u32[]{:S(2)}) collective-permute-start(f32[16,128]{1,0:T(8,128)S(1)} %get-tuple-element.15), channel_id=1, source_target_pairs={{0,128},{1,129},{2,130},{3,131},{4,132},{5,133},{6,134},{7,135},{8... | collective-permute-start | bytes 24584 | tf_op jit(solution)/shard_map/ppermute | solution.py:410
  30.3 12.4 %collective-permute-start.2 = (f32[656,128]{1,0:T(8,128)S(1)}, f32[656,128]{1,0:T(8,128)S(1)}, u32[]{:S(2)}, u32[]{:S(2)}) collective-permute-start(f32[656,128]{1,0:T(8,128)S(1)} %constant_dynamic-update-slice_fusion.2.refs_3_.refs_1_), channel_id=1, source_target_pairs={{0,7},{8,0},{16,8},{24,16},{32,24},{40,32},{48,40},{56,48},{120,56... | collective-permute-start | bytes 1007624 | tf_op jit(solution)/shard_map/ppermute | solution.py:406
  30.6 12.1 %collective-permute-start.1 = (f32[656,128]{1,0:T(8,128)S(1)}, f32[656,128]{1,0:T(8,128)S(1)}, u32[]{:S(2)}, u32[]{:S(2)}) collective-permute-start(f32[656,128]{1,0:T(8,128)S(1)} %constant_dynamic-update-slice_fusion.2.refs_3_.refs_1_), channel_id=1, source_target_pairs={{0,8},{8,16},{16,24},{24,32},{32,40},{40,48},{48,56},{56,120},{120... | collective-permute-start | bytes 1007624 | tf_op jit(solution)/shard_map/ppermute | solution.py:406
  45.2 2.5 %collective-permute-start.3 = (f32[16,128]{1,0:T(8,128)S(1)}, f32[16,128]{1,0:T(8,128)S(1)}, u32[]{:S(2)}, u32[]{:S(2)}) collective-permute-start(f32[16,128]{1,0:T(8,128)S(1)} %get-tuple-element.18), channel_id=1, source_target_pairs={{0,128},{1,129},{2,130},{3,131},{4,132},{5,133},{6,134},{7,135},{8... | collective-permute-start | bytes 24584 | tf_op jit(solution)/shard_map/ppermute | solution.py:410
  47.7 18.4 %collective-permute-start.5 = (f32[528,128]{1,0:T(8,128)S(1)}, f32[528,128]{1,0:T(8,128)S(1)}, u32[]{:S(2)}, u32[]{:S(2)}) collective-permute-start(f32[528,128]{1,0:T(8,128)S(1)} %constant_dynamic-update-slice_fusion.1.refs_6_), channel_id=1, source_target_pairs={{0,7},{8,0},{16,8},{24,16},{32,24},{40,32},{48,40},{56,48},{120,56... | collective-permute-start | bytes 811016 | tf_op jit(solution)/shard_map/ppermute | solution.py:406
  50.8 15.3 %collective-permute-start.4 = (f32[528,128]{1,0:T(8,128)S(1)}, f32[528,128]{1,0:T(8,128)S(1)}, u32[]{:S(2)}, u32[]{:S(2)}) collective-permute-start(f32[528,128]{1,0:T(8,128)S(1)} %constant_dynamic-update-slice_fusion.1.refs_6_), channel_id=1, source_target_pairs={{0,8},{8,16},{16,24},{24,32},{32,40},{40,48},{48,56},{56,120},{120... | collective-permute-start | bytes 811016 | tf_op jit(solution)/shard_map/ppermute | solution.py:406
  68.7 2.1 %collective-permute-start.6 = (f32[16,128]{1,0:T(8,128)S(1)}, f32[16,128]{1,0:T(8,128)S(1)}, u32[]{:S(2)}, u32[]{:S(2)}) collective-permute-start(f32[16,128]{1,0:T(8,128)S(1)} %get-tuple-element.21), channel_id=1, source_target_pairs={{0,128},{1,129},{2,130},{3,131},{4,132},{5,133},{6,134},{7,135},{8... | collective-permute-start | bytes 24584 | tf_op jit(solution)/shard_map/ppermute | solution.py:410
  70.8 10.6 %collective-permute-start.8 = (f32[528,128]{1,0:T(8,128)S(1)}, f32[528,128]{1,0:T(8,128)S(1)}, u32[]{:S(2)}, u32[]{:S(2)}) collective-permute-start(f32[528,128]{1,0:T(8,128)S(1)} %constant_dynamic-update-slice_fusion.refs_4_), channel_id=1, source_target_pairs={{0,7},{8,0},{16,8},{24,16},{32,24},{40,32},{48,40},{56,48},{120,56... | collective-permute-start | bytes 811016 | tf_op jit(solution)/shard_map/ppermute | solution.py:406
  72.3 9.2 %collective-permute-start.7 = (f32[528,128]{1,0:T(8,128)S(1)}, f32[528,128]{1,0:T(8,128)S(1)}, u32[]{:S(2)}, u32[]{:S(2)}) collective-permute-start(f32[528,128]{1,0:T(8,128)S(1)} %constant_dynamic-update-slice_fusion.refs_4_), channel_id=1, source_target_pairs={{0,8},{8,16},{16,24},{24,32},{32,40},{40,48},{48,56},{56,120},{120... | collective-permute-start | bytes 811016 | tf_op jit(solution)/shard_map/ppermute | solution.py:406

commit v3 on v2

--- a/solution.py
+++ b/solution.py
@@ -43,11 +43,31 @@
 
 
 def up(v, ghost=None):
-    return jnp.where(levels() == NZ - 1, v if ghost is None else ghost, turn(v, NZ - 1, 0))
+    low, high = v[:8], v[8:]
+    edge = lax.broadcasted_iota(jnp.int32, (8, NX), 0) == 7
+    low_up, high_up = turn(low, 7, 0), turn(high, 7, 0)
+    top = jnp.where(edge, high if ghost is None else ghost, high_up)
+    return jnp.concatenate([jnp.where(edge, high_up, low_up), top])
 
 
 def down(v, ghost=None):
-    return jnp.where(levels() == 0, v if ghost is None else ghost, turn(v, 1, 0))
+    low, high = v[:8], v[8:]
+    edge = lax.broadcasted_iota(jnp.int32, (8, NX), 0) == 0
+    low_down, high_down = turn(low, 1, 0), turn(high, 1, 0)
+    base = jnp.where(edge, low if ghost is None else ghost, low_down)
+    return jnp.concatenate([base, jnp.where(edge, low_down, high_down)])
+
+
+def swap_blocks(v):
+    row = levels()
+    group = lanes() // 8
+    for bit in (8, 4, 2, 1):
+        row_set = (row & bit) != 0
+        group_set = (group & bit) != 0
+        from_low = turn(turn(v, NZ - bit, 0), 8 * bit, 1)
+        from_high = turn(turn(v, bit, 0), NX - 8 * bit, 1)
+        v = jnp.where(row_set == group_set, v, jnp.where(row_set, from_high, from_low))
+    return v
 
 
 class Walls:
@@ -86,15 +106,18 @@
     return jnp.sum(spread, axis=0, keepdims=True)
 
 
-def lane_means(row, start):
-    spread = jnp.where(lanes() == levels() + start, jnp.broadcast_to(row, (NZ, NX)), 0.0)
+def lane_means(row, start, width=1):
+    low = levels() * width + start
+    lane = lanes()
+    spread = jnp.where((lane >= low) & (lane < low + width), jnp.broadcast_to(row, (NZ, NX)), 0.0)
     mean = jnp.sum(spread, axis=1, keepdims=True) * (1.0 / CELLS)
     return jnp.broadcast_to(mean, (NZ, NX))
 
 
 def role_totals(rows, role):
-    pre = jnp.sum(rows[:8], axis=0, keepdims=True)
-    suc = jnp.sum(rows[8:], axis=0, keepdims=True)
+    half = rows.shape[0] // 2
+    pre = jnp.sum(rows[:half], axis=0, keepdims=True)
+    suc = jnp.sum(rows[half:], axis=0, keepdims=True)
     return pre, jnp.where(role == 0, pre, suc)
 
 
@@ -130,10 +153,19 @@
     return picked
 
 
-def pack_kernel(info, state, drag, out):
+def pack_kernel(info, state, mask, out):
+    role = info[0]
     flip = info[1]
     for f in range(5):
-        flat = (state[f] if f < 4 else drag[...]).T
+        if f < 4:
+            cells = state[f]
+        else:
+            cells = jnp.where(role == 1, CDRAG * mask[...].astype(jnp.float32), 0.0)
+        flat = cells.T
+        if f == 3:
+            row = jnp.broadcast_to(jnp.sum(flat, axis=0, keepdims=True), (ROWS, NX))
+            for block in range(BLOCKS):
+                out[block, 5] = row
         flat = turn(flat, ROWS * info[2], 1)
         for block in range(BLOCKS):
             out[owner_of(block, flip), f] = flat[ROWS * block : ROWS * (block + 1)]
@@ -142,7 +174,10 @@
 def first_kernel(info, sample, gust, chunks, buf, plane, sums_out):
     del info
     picked = jnp.zeros((NZ, NX), jnp.float32)
-    sums = jnp.zeros((NZ, NX), jnp.float32)
+    sums = chunks[0, 5, :1]
+    for s in range(1, BLOCKS):
+        sums = sums + chunks[s, 5, :1]
+    sums_out[...] = sums
     for f in range(5):
         tiles = skewed([chunks[s, f] for s in range(BLOCKS)])
         for z in range(NZ):
@@ -152,9 +187,6 @@
             spot = f * ROWS + r
             cells = buf[spot * NZ : (spot + 1) * NZ, :]
             picked = sampled(picked, f, r, cells, sample)
-            if f == 3:
-                sums = sums + cells
-    sums_out[...] = level_lanes(jnp.sum(sums, axis=1, keepdims=True))
     picked = with_gust(picked, gust)
     plane[...] = picked
     buf[5 * FIELD :, :] = picked
@@ -172,7 +204,8 @@
         sample, gust = take(2)
     starts = take(3)
     bufs = take(3) if section else starts
-    (sums_in,) = take(1)
+    if section:
+        (sums_in,) = take(1)
     if section < 2:
         new_out, plane_out, sums_out = take(3)
     else:
@@ -185,17 +218,19 @@
     plane_at = (4 if section else 5) * FIELD
 
     if section:
-        if section == 1:
-            row = jnp.sum(sums_in[...], axis=0, keepdims=True)
-            pre = turn(row, NX - NZ, 1)
-            own = jnp.where(role == 0, pre, turn(row, NX - 2 * NZ, 1))
-            spot = 0
-        else:
-            pre, own = role_totals(sums_in, role)
-            spot = NZ
+        pre, own = role_totals(sums_in, role)
+        spot = (0, 8) if section == 1 else (NZ, 1)
         prev_step = SECTION_C[section - 1] * DT
-        d_u, d_w = mean_change(walls, lane_means(own, spot), prev_step)
-        _, pre_w = mean_change(Walls(role < 0), lane_means(pre, spot), prev_step)
+        d_u, d_w = mean_change(walls, lane_means(own, *spot), prev_step)
+        _, pre_w = mean_change(Walls(role < 0), lane_means(pre, *spot), prev_step)
+
+    if section == 2:
+        changes = mean_change(walls, lane_means(own * 0.5, 0), step)
+        now_u, now_w = (swap_blocks(change) for change in changes)
+        row = lax.broadcasted_iota(jnp.int32, (ROWS, NX), 0)
+        for s in range(BLOCKS):
+            share = jnp.where(row == 0, now_u[s : s + 1], now_w[s : s + 1])
+            chunks_out[s, 4] = share
 
     for side in range(3):
         plane = bufs[side][plane_at : plane_at + NZ, :]
@@ -317,15 +352,7 @@
         picked = with_gust(picked, gust)
         new_out[plane_at if section else 4 * FIELD :, :] = picked
         plane_out[...] = picked
-        row = level_lanes(jnp.sum(sums, axis=1, keepdims=True))
-        if section == 0:
-            for part in range(2):
-                rows = sums_in[8 * part : 8 * (part + 1)]
-                row = row + turn(jnp.sum(rows, axis=0, keepdims=True), NZ * (part + 1), 1)
-        else:
-            kept = jnp.where(lanes(1) < NZ, jnp.sum(sums_in[...], axis=0, keepdims=True), 0.0)
-            row = row + turn(kept, NZ, 1)
-        sums_out[...] = row
+        sums_out[...] = level_lanes(jnp.sum(sums, axis=1, keepdims=True))
     else:
         for f in range(4):
             tiles = []
@@ -335,44 +362,43 @@
             tiles = skewed(tiles)
             for s in range(BLOCKS):
                 chunks_out[s, f] = tiles[s]
-        for s in range(BLOCKS):
-            chunks_out[s, 4] = jnp.broadcast_to(own, (ROWS, NX))
-
-
-def last_kernel(info, chunks, out):
-    role = info[0]
+
+
+def last_kernel(info, chunks, out, held, left):
     flip = info[1]
     gx = info[2]
-    row = chunks[0, 4, :1]
+    share = chunks[0, 4]
     for block in range(1, BLOCKS):
-        row = row + chunks[block, 4, :1]
-    changes = mean_change(Walls(role == 1), lane_means(row, 0), SECTION_C[2] * DT)
+        share = share + chunks[block, 4]
     shift = lax.rem(NX - ROWS * gx, NX)
+    copies = [pltpu.make_async_copy(held.at[f], out.at[f], left.at[f]) for f in range(4)]
     for f in range(4):
         flat = jnp.concatenate([chunks[owner_of(block, flip), f] for block in range(BLOCKS)])
-        out[f] = turn(flat, shift, 1).T
+        flat = turn(flat, shift, 1)
         if f in (0, 2):
-            change = turn(changes[f // 2], shift, 1)
-            for x in range(8):
-                rows = pl.ds(x, NZ, stride=8)
-                out[f, rows, :] += jnp.broadcast_to(change[:, x : x + 1], (NZ, NX))
+            flat = flat + share[f // 2 : f // 2 + 1]
+        held[f] = flat.T
+        copies[f].start()
+    for copy in copies:
+        copy.wait()
 
 
 VMEM = pl.BlockSpec(memory_space=pltpu.VMEM)
 SMEM = pl.BlockSpec(memory_space=pltpu.SMEM)
+HBM = pl.BlockSpec(memory_space=pltpu.HBM)
 
 
 def shape(*dims):
     return jax.ShapeDtypeStruct(dims, jnp.float32)
 
 
-def call(body, name, small, args, outs, scratch=()):
+def call(body, name, small, args, outs, scratch=(), in_place=(VMEM, VMEM)):
     return pl.pallas_call(
         body,
         name=name,
         out_shape=outs,
-        in_specs=[SMEM] * len(small) + [VMEM] * len(args),
-        out_specs=[VMEM] * len(outs),
+        in_specs=[SMEM] * len(small) + [in_place[0]] * len(args),
+        out_specs=[in_place[1]] * len(outs),
         scratch_shapes=list(scratch),
         compiler_params=pltpu.CompilerParams(vmem_limit_bytes=48 * 1024 * 1024),
     )(*small, *args)
@@ -419,12 +445,24 @@
     return lax.all_to_all(jnp.broadcast_to(row[None], (count, 1, NX)), axes, 0, 0)[:, 0]
 
 
+def along_z(row):
+    groups = [list(range(8)), list(range(8, 16))]
+    rows = jnp.broadcast_to(row[None], (8, 1, NX))
+    return lax.all_to_all(rows, "gx", 0, 0, axis_index_groups=groups)[:, 0]
+
+
+def across_z(row):
+    high = [(role * 16 + half * 8) * 8 for role in range(2) for half in range(2)]
+    groups = [[h + z * 8 + gy for h in high for gy in range(8)] for z in range(8)]
+    rows = jnp.broadcast_to(row[None], (32, 1, NX))
+    return lax.all_to_all(rows, ("role", "gx", "gy"), 0, 0, axis_index_groups=groups)[:, 0]
+
+
 def per_device(state, turbine_mask, sample_x, gust_start, gust_level):
     role = lax.axis_index("role")
     gx = lax.axis_index("gx")
     flip = lax.axis_index("gy") % 2
     info = jnp.stack([role, flip, gx]).astype(jnp.int32)
-    drag = jnp.where(role == 1, CDRAG * turbine_mask.astype(jnp.float32), 0.0)
     even = jnp.where(gx < 8, gx, 23 - gx)
     odd = jnp.where(gx < 8, 8 + (gx + 7) % 8, jnp.where(gx == 8, 0, 16 - gx))
     block = jnp.where(flip == 0, even, odd)
@@ -437,23 +475,29 @@
         rise = jnp.clip((SECTION_T[section] - began) / RISE, 0.0, 1.0)
         gusts.append(amp * 0.5 * (1.0 - jnp.cos(math.pi * rise)))
 
-    args = (state.reshape(4, 128, 128), drag.reshape(128, 128))
-    (chunks,) = call(pack_kernel, "pack", (info,), args, [shape(BLOCKS, 5, ROWS, NX)])
+    args = (state.reshape(4, 128, 128), turbine_mask.reshape(128, 128))
+    (chunks,) = call(pack_kernel, "pack", (info,), args, [shape(BLOCKS, 6, ROWS, NX)])
     chunks = lax.all_to_all(chunks, "gx", 0, 0)
     outs = [shape(5 * FIELD + NZ, NX), shape(NZ, NX), shape(1, NX)]
     args = (chunks,)
     buf, plane, sums = call(first_kernel, "first", (info, sample, gusts[0]), args, outs)
     starts = halo(inflow_to(buf, plane))
     totals = every(sums, ("role", "gy"), 16)
-    buf, plane, sums = section_call(0, (info, sample, gusts[1]), (*starts, totals))
+    buf, plane, sums = section_call(0, (info, sample, gusts[1]), starts)
+    plane, totals = lax.optimization_barrier((plane, totals))
     bufs = halo(inflow_to(buf, plane))
-    totals = every(sums, "gx", 16)
+    rows = along_z(sums)
     buf, plane, sums = section_call(1, (info, sample, gusts[2]), (*starts, *bufs, totals))
+    plane, rows = lax.optimization_barrier((plane, rows))
     bufs = halo(inflow_to(buf, plane))
-    totals = every(sums, ("role", "gy"), 16)
+    row = jnp.sum(rows, axis=0, keepdims=True)
+    row = jnp.concatenate([sums[:, :NZ], row[:, : NX - NZ]], axis=1)
+    totals = across_z(row)
     (chunks,) = section_call(2, (info,), (*starts, *bufs, totals))
     chunks = lax.all_to_all(chunks, "gx", 0, 0)
-    (out,) = call(last_kernel, "last", (info,), (chunks,), [shape(4, 128, 128)])
+    scratch = [pltpu.VMEM((4, 128, 128), jnp.float32), pltpu.SemaphoreType.DMA((4,))]
+    outs = [shape(4, 128, 128)]
+    (out,) = call(last_kernel, "last", (info,), (chunks,), outs, scratch, (VMEM, HBM))
     return out.reshape(1, 4, NZ, 8, 128)
 
 

time: 105 us -> 104 us (level)
  blocking collectives: 53 us -> 31.1 us
  starting transfers between devices: 22.6 us -> 33.8 us
  waiting for transfers between devices: 12.8 us -> 21.9 us
  local copies, waits for them, and re-layouts: 2.35 us -> 4.38 us
    all_to_all x3 -> x1, blocking collectives: 34.3 us -> 12.6 us  [across_z(): lax.all_to_all(rows, ('role', 'gx', 'gy'), 0, 0, axis_index_groups=groups)]
    all_to_all x0 -> x2, starting transfers between devices: none -> 9.96 us  [the longest x1 5.44 us: along_z(): return lax.all_to_all(rows, 'gx', 0, 0, axis_index_groups=groups)[:, 0]]
    ppermute x6, waiting for transfers between devices: 0.02 us -> 6.83 us  [around(): return lax.ppermute(cells, ('gx', 'gy'), route)]
    ppermute x6, starting transfers between devices: 7.14 us -> 8.58 us  [around(): return lax.ppermute(cells, ('gx', 'gy'), route)]
    all_to_all x1, waiting for transfers between devices: 10.3 us -> 11.5 us  [per_device(): chunks = lax.all_to_all(chunks, 'gx', 0, 0)]
    all_to_all x0 -> x2, waiting for transfers between devices: none -> 1.07 us  [the longest x1 1.07 us: along_z(): return lax.all_to_all(rows, 'gx', 0, 0, axis_index_groups=groups)[:, 0]]
    unnamed x6 -> x8, local copies, waits for them, and re-layouts: 2.26 us -> 3.1 us
  transfers between devices with their start and end apart: 10 -> 12, of which waited for: 4 -> 9; matrix products, arithmetic and copies ran while one was open for 0% -> 1% of each run, Pallas kernels for 0% -> 5%
where the time goes in v3:
time: 104 us; the launch traced here: 103 us
  starting transfers between devices  33.8 us (32%)
  blocking collectives  31.1 us (30%)
  waiting for transfers between devices  21.9 us (21%)
  Pallas kernels  11.1 us (11%)
  local copies, waits for them, and re-layouts  4.38 us (4%)
    all_to_all x1, blocking collectives, per_device(): chunks = lax.all_to_all(chunks, 'gx', 0, 0)  18.5 us
    all_to_all x1, blocking collectives, across_z(): lax.all_to_all(rows, ('role', 'gx', 'gy'), 0, 0, axis_index_groups=groups)  12.6 us
    all_to_all x1, waiting for transfers between devices, per_device(): chunks = lax.all_to_all(chunks, 'gx', 0, 0)  11.5 us
    all_to_all x1, starting transfers between devices, per_device(): chunks = lax.all_to_all(chunks, 'gx', 0, 0)  11.2 us
    pallas_call x6, Pallas kernels, call(): pl.pallas_call(body, name=name, out_shape=outs, in_specs=[SMEM] * len(sma...  11.1 us
    ppermute x6, starting transfers between devices, around(): return lax.ppermute(cells, ('gx', 'gy'), route)  8.58 us
    ppermute x6, waiting for transfers between devices, around(): return lax.ppermute(cells, ('gx', 'gy'), route)  6.83 us
    all_to_all x1, starting transfers between devices, along_z(): return lax.all_to_all(rows, 'gx', 0, 0, axis_index_groups=groups)[:, 0]  5.44 us
  transfers between devices with their start and end apart: 12, of which 9 were waited for; matrix products, arithmetic and copies ran while one was open for 1% of the time, Pallas kernels for 5%

profile of v3, /device:TPU:32, one launch (start us, length us, event | category | flops | bytes accessed | tf_op | source)
XLA Modules:
  0.0 103.4 jit_solution(14882657629613666391)
XLA Ops:
  0.1 0.9 copy-done
  1.0 0.8 copy-done.1
  1.9 1.6 %pack.1 = f32[16,6,8,128]{3,2,1,0:T(8,128)} custom-call(s32[3]{0:T(128)S(1)} %pad_add_fusion.info, f32[4,128,128]{2,1,0:T(8,128)S(1)} %bitcast.19, s32[128,128]{1,0:T(8,128)S(1)} %bitcast.21), custom_call_target="tpu_custom_call" | custom-call | tf_op jit(solution)/shard_map/pack/pallas_call | solution.py:396
  3.5 11.2 %all-to-all-start = ((f32[16,6,8,128]{3,2,1,0:T(8,128)}), f32[16,6,8,128]{3,2,1,0:T(8,128)S(1)}, u32[]{:S(2)}, u32[]{:S(2)}) async-start(f32[16,6,8,128]{3,2,1,0:T(8,128)} %pack.1), calls=%async_computation | async-start | bytes 786432 | tf_op jit(solution)/shard_map/all_to_all | solution.py:480
  15.6 0.6 copy-done.3
  16.3 0.7 copy-done.2
  17.0 11.5 %all-to-all-done.chunks = f32[16,6,8,128]{3,2,1,0:T(8,128)S(1)} async-done(((f32[16,6,8,128]{3,2,1,0:T(8,128)}), f32[16,6,8,128]{3,2,1,0:T(8,128)S(1)}, u32[]{:S(2)}, u32[]{:S(2)}) %all-to-all-start) | async-done | bytes 393248 | tf_op jit(solution)/shard_map/all_to_all | solution.py:480
  28.6 0.8 first.1
  29.4 1.3 %collective-permute-start = (f32[16,128]{1,0:T(8,128)S(1)}, f32[16,128]{1,0:T(8,128)S(1)}, u32[]{:S(2)}, u32[]{:S(2)}) collective-permute-start(f32[16,128]{1,0:T(8,128)S(1)} %get-tuple-element.19), channel_id=1, source_target_pairs={{0,128},{1,129},{2,130},{3,131},{4,132},{5,133},{6,134},{7,135},{8... | collective-permute-start | bytes 24584 | tf_op jit(solution)/shard_map/ppermute | solution.py:436
  30.7 0.8 collective-permute-done
  31.5 0.3 collective-permute-start.2
  31.8 1.7 %collective-permute-start.1 = (f32[656,128]{1,0:T(8,128)S(1)}, f32[656,128]{1,0:T(8,128)S(1)}, u32[]{:S(2)}, u32[]{:S(2)}) collective-permute-start(f32[656,128]{1,0:T(8,128)S(1)} %constant_dynamic-update-slice_fusion.2.refs_3_.refs_1_), channel_id=1, source_target_pairs={{0,8},{8,16},{16,24},{24,32},{32,40},{40,48},{48,56},{56,120},{120... | collective-permute-start | bytes 1007624 | tf_op jit(solution)/shard_map/ppermute | solution.py:432
  33.5 0.6 broadcast_in_dim.28
  34.1 4.5 %all-to-all-start.1 = ((f32[16,1,128]{2,1,0:T(1,128)}), f32[16,1,128]{2,1,0:T(1,128)S(1)}, u32[]{:S(2)}, u32[]{:S(2)}) async-start(f32[16,1,128]{2,1,0:T(1,128)} %broadcast_in_dim.28), calls=%async_computation.1 | async-start | bytes 16384 | tf_op jit(solution)/shard_map/all_to_all | solution.py:445
  38.7 3.0 %collective-permute-done.2.refs_4_.refs_2_ = f32[656,128]{1,0:T(8,128)S(1)} collective-permute-done((f32[656,128]{1,0:T(8,128)S(1)}, f32[656,128]{1,0:T(8,128)S(1)}, u32[]{:S(2)}, u32[]{:S(2)}) %collective-permute-start.2) | collective-permute-done | bytes 335904 | tf_op jit(solution)/shard_map/ppermute | solution.py:432
  41.6 1.2 %collective-permute-done.1.refs_2_.refs_0_ = f32[656,128]{1,0:T(8,128)S(1)} collective-permute-done((f32[656,128]{1,0:T(8,128)S(1)}, f32[656,128]{1,0:T(8,128)S(1)}, u32[]{:S(2)}, u32[]{:S(2)}) %collective-permute-start.1) | collective-permute-done | bytes 335904 | tf_op jit(solution)/shard_map/ppermute | solution.py:432
  42.8 2.4 %section0.1 = (f32[528,128]{1,0:T(8,128)S(1)}, f32[16,128]{1,0:T(8,128)S(1)}, f32[1,128]{1,0:T(1,128)S(1)}) custom-call(s32[3]{0:T(128)S(1)} %pad_add_fusion.info, s32[8]{0:T(128)S(1)} %dynamic_slice.6.sample.refs_0_, f32[8]{0:T(128)S(1)} %get-tuple-element.31.refs_1_, f32[656,128]{1,0:T(8,128)S(1)} %collective-permute-done.1.refs_2_.refs_0_, ...), custom_call_target="tpu_custom_call" | custom-call | tf_op jit(solution)/shard_map/section0/pallas_call | solution.py:396
  45.2 1.4 %collective-permute-start.3 = (f32[16,128]{1,0:T(8,128)S(1)}, f32[16,128]{1,0:T(8,128)S(1)}, u32[]{:S(2)}, u32[]{:S(2)}) collective-permute-start(f32[16,128]{1,0:T(8,128)S(1)} %get-tuple-element.23), channel_id=1, source_target_pairs={{0,128},{1,129},{2,130},{3,131},{4,132},{5,133},{6,134},{7,135},{8... | collective-permute-start | bytes 24584 | tf_op jit(solution)/shard_map/ppermute | solution.py:436
  46.6 0.8 collective-permute-done.3
  47.4 3.8 %collective-permute-start.5 = (f32[528,128]{1,0:T(8,128)S(1)}, f32[528,128]{1,0:T(8,128)S(1)}, u32[]{:S(2)}, u32[]{:S(2)}) collective-permute-start(f32[528,128]{1,0:T(8,128)S(1)} %constant_dynamic-update-slice_fusion.1.refs_6_), channel_id=1, source_target_pairs={{0,7},{8,0},{16,8},{24,16},{32,24},{40,32},{48,40},{56,48},{120,56... | collective-permute-start | bytes 811016 | tf_op jit(solution)/shard_map/ppermute | solution.py:432
  51.2 0.6 broadcast_in_dim.30
  51.8 5.4 %all-to-all-start.2 = ((f32[8,1,128]{2,1,0:T(1,128)}), f32[8,1,128]{2,1,0:T(1,128)S(1)}, u32[]{:S(2)}, u32[]{:S(2)}) async-start(f32[8,1,128]{2,1,0:T(1,128)} %broadcast_in_dim.30), calls=%async_computation.2 | async-start | bytes 8192 | tf_op jit(solution)/shard_map/all_to_all | solution.py:451
  57.5 2.5 %collective-permute-done.4.refs_5_ = f32[528,128]{1,0:T(8,128)S(1)} collective-permute-done((f32[528,128]{1,0:T(8,128)S(1)}, f32[528,128]{1,0:T(8,128)S(1)}, u32[]{:S(2)}, u32[]{:S(2)}) %collective-permute-start.4) | collective-permute-done | bytes 270368 | tf_op jit(solution)/shard_map/ppermute | solution.py:432
  59.9 2.4 %section1.1 = (f32[528,128]{1,0:T(8,128)S(1)}, f32[16,128]{1,0:T(8,128)S(1)}, f32[1,128]{1,0:T(1,128)S(1)}) custom-call(s32[3]{0:T(128)S(1)} %pad_add_fusion.info, s32[8]{0:T(128)S(1)} %dynamic_slice.6.sample.refs_0_, f32[8]{0:T(128)S(1)} %get-tuple-element.32.refs_1_, f32[656,128]{1,0:T(8,128)S(1)} %collective-permute-done.1.refs_2_.refs_0_, ...), custom_call_target="tpu_custom_call" | custom-call | tf_op jit(solution)/shard_map/section1/pallas_call | solution.py:396
  62.3 1.1 %all-to-all-done.2 = f32[8,1,128]{2,1,0:T(1,128)S(1)} async-done(((f32[8,1,128]{2,1,0:T(1,128)}), f32[8,1,128]{2,1,0:T(1,128)S(1)}, u32[]{:S(2)}, u32[]{:S(2)}) %all-to-all-start.2) | async-done | bytes 4128 | tf_op jit(solution)/shard_map/all_to_all | solution.py:451
  63.4 1.3 %collective-permute-start.6 = (f32[16,128]{1,0:T(8,128)S(1)}, f32[16,128]{1,0:T(8,128)S(1)}, u32[]{:S(2)}, u32[]{:S(2)}) collective-permute-start(f32[16,128]{1,0:T(8,128)S(1)} %get-tuple-element.28), channel_id=1, source_target_pairs={{0,128},{1,129},{2,130},{3,131},{4,132},{5,133},{6,134},{7,135},{8... | collective-permute-start | bytes 24584 | tf_op jit(solution)/shard_map/ppermute | solution.py:436
  64.7 0.8 collective-permute-done.6
  65.5 2.8 %collective-permute-start.8 = (f32[528,128]{1,0:T(8,128)S(1)}, f32[528,128]{1,0:T(8,128)S(1)}, u32[]{:S(2)}, u32[]{:S(2)}) collective-permute-start(f32[528,128]{1,0:T(8,128)S(1)} %constant_dynamic-update-slice_fusion.refs_4_), channel_id=1, source_target_pairs={{0,7},{8,0},{16,8},{24,16},{32,24},{40,32},{48,40},{56,48},{120,56... | collective-permute-start | bytes 811016 | tf_op jit(solution)/shard_map/ppermute | solution.py:432
  68.4 12.6 %all_to_all.25 = f32[32,1,128]{2,1,0:T(1,128)S(1)} all-to-all(f32[32,1,128]{2,1,0:T(1,128)S(1)} %broadcast_in_dim.33), channel_id=1, replica_groups={{0,1,2,3,4,5,6,7,64,65,66,67,68,69,70,71,128,129,130,131,132,133,134,13..., dimensions={0} | all-to-all | bytes 32768 | tf_op jit(solution)/shard_map/all_to_all | solution.py:458
  81.0 2.5 %section2.1 = f32[16,5,8,128]{3,2,1,0:T(8,128)S(1)} custom-call(s32[3]{0:T(128)S(1)} %pad_add_fusion.info, f32[656,128]{1,0:T(8,128)S(1)} %collective-permute-done.1.refs_2_.refs_0_, f32[656,128]{1,0:T(8,128)S(1)} %constant_dynamic-update-slice_fusion.2.refs_3_.refs_1_, f32[656,128]{1,0:T(8,128)S(1)} %collective-permute-done.2.refs_4_.refs_2_, ...), custom_call_target="tpu_custom_call" | custom-call | tf_op jit(solution)/shard_map/section2/pallas_call | solution.py:396
  83.5 18.5 %all_to_all.26.chunks = f32[16,5,8,128]{3,2,1,0:T(8,128)S(1)} all-to-all(f32[16,5,8,128]{3,2,1,0:T(8,128)S(1)} %section2.1), channel_id=1, replica_groups=mesh['role'=2,'gx'=16,'gy'=8] {'gx'}, dimensions={0} | all-to-all | bytes 655360 | tf_op jit(solution)/shard_map/all_to_all | solution.py:497
  102.0 1.5 %last.1 = f32[4,128,128]{2,1,0:T(8,128)} custom-call(s32[3]{0:T(128)S(1)} %pad_add_fusion.info, f32[16,5,8,128]{3,2,1,0:T(8,128)S(1)} %all_to_all.26.chunks), custom_call_target="tpu_custom_call" | custom-call | tf_op jit(solution)/shard_map/last/pallas_call | solution.py:396
  (19 shorter events, 0.6 us)
Async XLA Ops:
  0.1 1.0 copy-start
  1.0 0.8 copy-start.1
  3.5 25.1 %all-to-all-start = ((f32[16,6,8,128]{3,2,1,0:T(8,128)}), f32[16,6,8,128]{3,2,1,0:T(8,128)S(1)}, u32[]{:S(2)}, u32[]{:S(2)}) async-start(f32[16,6,8,128]{3,2,1,0:T(8,128)} %pack.1), calls=%async_computation | async-start | bytes 786432 | tf_op jit(solution)/shard_map/all_to_all | solution.py:480
  15.6 0.7 copy-start.3
  16.3 0.7 copy-start.2
  29.4 2.1 %collective-permute-start = (f32[16,128]{1,0:T(8,128)S(1)}, f32[16,128]{1,0:T(8,128)S(1)}, u32[]{:S(2)}, u32[]{:S(2)}) collective-permute-start(f32[16,128]{1,0:T(8,128)S(1)} %get-tuple-element.19), channel_id=1, source_target_pairs={{0,128},{1,129},{2,130},{3,131},{4,132},{5,133},{6,134},{7,135},{8... | collective-permute-start | bytes 24584 | tf_op jit(solution)/shard_map/ppermute | solution.py:436
  31.5 10.1 %collective-permute-start.2 = (f32[656,128]{1,0:T(8,128)S(1)}, f32[656,128]{1,0:T(8,128)S(1)}, u32[]{:S(2)}, u32[]{:S(2)}) collective-permute-start(f32[656,128]{1,0:T(8,128)S(1)} %constant_dynamic-update-slice_fusion.2.refs_3_.refs_1_), channel_id=1, source_target_pairs={{0,7},{8,0},{16,8},{24,16},{32,24},{40,32},{48,40},{56,48},{120,56... | collective-permute-start | bytes 1007624 | tf_op jit(solution)/shard_map/ppermute | solution.py:432
  31.8 11.0 %collective-permute-start.1 = (f32[656,128]{1,0:T(8,128)S(1)}, f32[656,128]{1,0:T(8,128)S(1)}, u32[]{:S(2)}, u32[]{:S(2)}) collective-permute-start(f32[656,128]{1,0:T(8,128)S(1)} %constant_dynamic-update-slice_fusion.2.refs_3_.refs_1_), channel_id=1, source_target_pairs={{0,8},{8,16},{16,24},{24,32},{32,40},{40,48},{48,56},{56,120},{120... | collective-permute-start | bytes 1007624 | tf_op jit(solution)/shard_map/ppermute | solution.py:432
  34.1 11.0 %all-to-all-start.1 = ((f32[16,1,128]{2,1,0:T(1,128)}), f32[16,1,128]{2,1,0:T(1,128)S(1)}, u32[]{:S(2)}, u32[]{:S(2)}) async-start(f32[16,1,128]{2,1,0:T(1,128)} %broadcast_in_dim.28), calls=%async_computation.1 | async-start | bytes 16384 | tf_op jit(solution)/shard_map/all_to_all | solution.py:445
  45.2 2.3 %collective-permute-start.3 = (f32[16,128]{1,0:T(8,128)S(1)}, f32[16,128]{1,0:T(8,128)S(1)}, u32[]{:S(2)}, u32[]{:S(2)}) collective-permute-start(f32[16,128]{1,0:T(8,128)S(1)} %get-tuple-element.23), channel_id=1, source_target_pairs={{0,128},{1,129},{2,130},{3,131},{4,132},{5,133},{6,134},{7,135},{8... | collective-permute-start | bytes 24584 | tf_op jit(solution)/shard_map/ppermute | solution.py:436
  47.4 10.0 %collective-permute-start.5 = (f32[528,128]{1,0:T(8,128)S(1)}, f32[528,128]{1,0:T(8,128)S(1)}, u32[]{:S(2)}, u32[]{:S(2)}) collective-permute-start(f32[528,128]{1,0:T(8,128)S(1)} %constant_dynamic-update-slice_fusion.1.refs_6_), channel_id=1, source_target_pairs={{0,7},{8,0},{16,8},{24,16},{32,24},{40,32},{48,40},{56,48},{120,56... | collective-permute-start | bytes 811016 | tf_op jit(solution)/shard_map/ppermute | solution.py:432
  51.2 8.7 %collective-permute-start.4 = (f32[528,128]{1,0:T(8,128)S(1)}, f32[528,128]{1,0:T(8,128)S(1)}, u32[]{:S(2)}, u32[]{:S(2)}) collective-permute-start(f32[528,128]{1,0:T(8,128)S(1)} %constant_dynamic-update-slice_fusion.1.refs_6_), channel_id=1, source_target_pairs={{0,8},{8,16},{16,24},{24,32},{32,40},{40,48},{48,56},{56,120},{120... | collective-permute-start | bytes 811016 | tf_op jit(solution)/shard_map/ppermute | solution.py:432
  51.8 11.6 %all-to-all-start.2 = ((f32[8,1,128]{2,1,0:T(1,128)}), f32[8,1,128]{2,1,0:T(1,128)S(1)}, u32[]{:S(2)}, u32[]{:S(2)}) async-start(f32[8,1,128]{2,1,0:T(1,128)} %broadcast_in_dim.30), calls=%async_computation.2 | async-start | bytes 8192 | tf_op jit(solution)/shard_map/all_to_all | solution.py:451
  63.4 2.1 %collective-permute-start.6 = (f32[16,128]{1,0:T(8,128)S(1)}, f32[16,128]{1,0:T(8,128)S(1)}, u32[]{:S(2)}, u32[]{:S(2)}) collective-permute-start(f32[16,128]{1,0:T(8,128)S(1)} %get-tuple-element.28), channel_id=1, source_target_pairs={{0,128},{1,129},{2,130},{3,131},{4,132},{5,133},{6,134},{7,135},{8... | collective-permute-start | bytes 24584 | tf_op jit(solution)/shard_map/ppermute | solution.py:436
  65.5 15.5 %collective-permute-start.8 = (f32[528,128]{1,0:T(8,128)S(1)}, f32[528,128]{1,0:T(8,128)S(1)}, u32[]{:S(2)}, u32[]{:S(2)}) collective-permute-start(f32[528,128]{1,0:T(8,128)S(1)} %constant_dynamic-update-slice_fusion.refs_4_), channel_id=1, source_target_pairs={{0,7},{8,0},{16,8},{24,16},{32,24},{40,32},{48,40},{56,48},{120,56... | collective-permute-start | bytes 811016 | tf_op jit(solution)/shard_map/ppermute | solution.py:432
  68.3 12.7 %collective-permute-start.7 = (f32[528,128]{1,0:T(8,128)S(1)}, f32[528,128]{1,0:T(8,128)S(1)}, u32[]{:S(2)}, u32[]{:S(2)}) collective-permute-start(f32[528,128]{1,0:T(8,128)S(1)} %constant_dynamic-update-slice_fusion.refs_4_), channel_id=1, source_target_pairs={{0,8},{8,16},{16,24},{24,32},{32,40},{40,48},{48,56},{56,120},{120... | collective-permute-start | bytes 811016 | tf_op jit(solution)/shard_map/ppermute | solution.py:432

commit v4 on v3

--- a/solution.py
+++ b/solution.py
@@ -141,21 +141,26 @@
     return jnp.where(flip == 0, straight, other)
 
 
-def sampled(picked, f, r, cells, sample):
-    shift = lax.rem(f * ROWS + r - sample[r] + 2 * NX, NX)
+def sampled(picked, f, r, cells, sample, base):
+    shift = lax.rem(f * ROWS + r - sample[base + r] + 2 * NX, NX)
     return jnp.where(lanes() == f * ROWS + r, turn(cells, shift, 1), picked)
 
 
-def with_gust(picked, gust):
+def with_gust(picked, level, base, rise):
     lane = lanes()
     for r in range(ROWS):
-        picked = picked + jnp.where(lane == r, gust[r], 0.0)
+        gust = (1.5 + level[base + r].astype(jnp.float32)) * rise
+        picked = picked + jnp.where(lane == r, gust, 0.0)
     return picked
 
 
-def pack_kernel(info, state, mask, out):
+def pack_kernel(info, began, state, mask, out, rises):
     role = info[0]
     flip = info[1]
+    for section in range(3):
+        span = jnp.full((1, NX), SECTION_T[section], jnp.float32) - began[0].astype(jnp.float32)
+        angle = math.pi * jnp.clip(span / RISE, 0.0, 1.0)
+        rises[section : section + 1] = 0.5 * (1.0 - jnp.cos(angle))
     for f in range(5):
         if f < 4:
             cells = state[f]
@@ -171,8 +176,8 @@
             out[owner_of(block, flip), f] = flat[ROWS * block : ROWS * (block + 1)]
 
 
-def first_kernel(info, sample, gust, chunks, buf, plane, sums_out):
-    del info
+def first_kernel(info, sample, level, rises, chunks, buf, plane, sums_out):
+    base = info[3]
     picked = jnp.zeros((NZ, NX), jnp.float32)
     sums = chunks[0, 5, :1]
     for s in range(1, BLOCKS):
@@ -186,8 +191,8 @@
         for r in range(ROWS):
             spot = f * ROWS + r
             cells = buf[spot * NZ : (spot + 1) * NZ, :]
-            picked = sampled(picked, f, r, cells, sample)
-    picked = with_gust(picked, gust)
+            picked = sampled(picked, f, r, cells, sample, base)
+    picked = with_gust(picked, level, base, rises[:1])
     plane[...] = picked
     buf[5 * FIELD :, :] = picked
 
@@ -201,7 +206,8 @@
         return out
 
     if section < 2:
-        sample, gust = take(2)
+        sample, level, rises = take(3)
+        base = info[3]
     starts = take(3)
     bufs = take(3) if section else starts
     if section:
@@ -344,12 +350,12 @@
             spot = f * ROWS + r
             if section < 2:
                 new_out[spot * NZ : (spot + 1) * NZ, :] = fresh[f]
-                picked = sampled(picked, f, r, fresh[f], sample)
+                picked = sampled(picked, f, r, fresh[f], sample, base)
             else:
                 natural[pl.ds(f * FIELD + r, NZ, stride=ROWS), :] = fresh[f]
         sums = sums + fresh[3]
     if section < 2:
-        picked = with_gust(picked, gust)
+        picked = with_gust(picked, level, base, rises[section + 1 : section + 2])
         new_out[plane_at if section else 4 * FIELD :, :] = picked
         plane_out[...] = picked
         sums_out[...] = level_lanes(jnp.sum(sums, axis=1, keepdims=True))
@@ -462,32 +468,26 @@
     role = lax.axis_index("role")
     gx = lax.axis_index("gx")
     flip = lax.axis_index("gy") % 2
-    info = jnp.stack([role, flip, gx]).astype(jnp.int32)
     even = jnp.where(gx < 8, gx, 23 - gx)
     odd = jnp.where(gx < 8, 8 + (gx + 7) % 8, jnp.where(gx == 8, 0, 16 - gx))
     block = jnp.where(flip == 0, even, odd)
-    sample = lax.dynamic_slice(sample_x, (block * ROWS,), (ROWS,)).astype(jnp.int32)
-    level = lax.dynamic_slice(gust_level, (block * ROWS,), (ROWS,))
-    amp = 1.5 + level.astype(jnp.float32)
-    began = gust_start[0].astype(jnp.float32)
-    gusts = []
-    for section in range(3):
-        rise = jnp.clip((SECTION_T[section] - began) / RISE, 0.0, 1.0)
-        gusts.append(amp * 0.5 * (1.0 - jnp.cos(math.pi * rise)))
-
+    info = jnp.stack([role, flip, gx, block * ROWS]).astype(jnp.int32)
     args = (state.reshape(4, 128, 128), turbine_mask.reshape(128, 128))
-    (chunks,) = call(pack_kernel, "pack", (info,), args, [shape(BLOCKS, 6, ROWS, NX)])
+    outs = [shape(BLOCKS, 6, ROWS, NX), shape(3, NX)]
+    chunks, rises = call(pack_kernel, "pack", (info, gust_start), args, outs)
+    chunks, rises = lax.optimization_barrier((chunks, rises))
+    inlet = (info, sample_x, gust_level)
     chunks = lax.all_to_all(chunks, "gx", 0, 0)
     outs = [shape(5 * FIELD + NZ, NX), shape(NZ, NX), shape(1, NX)]
-    args = (chunks,)
-    buf, plane, sums = call(first_kernel, "first", (info, sample, gusts[0]), args, outs)
+    args = (rises, chunks)
+    buf, plane, sums = call(first_kernel, "first", inlet, args, outs)
     starts = halo(inflow_to(buf, plane))
     totals = every(sums, ("role", "gy"), 16)
-    buf, plane, sums = section_call(0, (info, sample, gusts[1]), starts)
+    buf, plane, sums = section_call(0, inlet, (rises, *starts))
     plane, totals = lax.optimization_barrier((plane, totals))
     bufs = halo(inflow_to(buf, plane))
     rows = along_z(sums)
-    buf, plane, sums = section_call(1, (info, sample, gusts[2]), (*starts, *bufs, totals))
+    buf, plane, sums = section_call(1, inlet, (rises, *starts, *bufs, totals))
     plane, rows = lax.optimization_barrier((plane, rows))
     bufs = halo(inflow_to(buf, plane))
     row = jnp.sum(rows, axis=0, keepdims=True)

time: 104 us -> 103 us (level)
  blocking collectives: 31.1 us -> 56 us
  waiting for transfers between devices: 21.9 us -> 10.3 us
  starting transfers between devices: 33.8 us -> 22.5 us
  local copies, waits for them, and re-layouts: 4.38 us -> 2.91 us
    all_to_all x1 -> x2, blocking collectives: 18.5 us -> 43.4 us  [per_device(): chunks = lax.all_to_all(chunks, 'gx', 0, 0)]
    all_to_all x1 -> x0, waiting for transfers between devices: 11.5 us -> none  [per_device(): chunks = lax.all_to_all(chunks, 'gx', 0, 0)]
    all_to_all x1 -> x0, starting transfers between devices: 11.2 us -> none  [per_device(): chunks = lax.all_to_all(chunks, 'gx', 0, 0)]
    unnamed x8, local copies, waits for them, and re-layouts: 3.1 us -> 1.7 us
  transfers between devices with their start and end apart: 12 -> 11, of which waited for: 9 -> 8; matrix products, arithmetic and copies ran while one was open for 1% -> 1% of each run, Pallas kernels for 5% -> 5%
where the time goes in v4:
time: 103 us
  blocking collectives  56 us (54%)
  starting transfers between devices  22.5 us (22%)
  Pallas kernels  10.3 us (10%)
  waiting for transfers between devices  10.3 us (10%)
  local copies, waits for them, and re-layouts  2.91 us (3%)
    all_to_all x2, blocking collectives, per_device(): chunks = lax.all_to_all(chunks, 'gx', 0, 0)  43.4 us
    all_to_all x1, blocking collectives, across_z(): lax.all_to_all(rows, ('role', 'gx', 'gy'), 0, 0, axis_index_groups=groups)  12.6 us
    pallas_call x6, Pallas kernels, call(): pl.pallas_call(body, name=name, out_shape=outs, in_specs=[SMEM] * len(sma...  10.3 us
    ppermute x6, starting transfers between devices, around(): return lax.ppermute(cells, ('gx', 'gy'), route)  8.58 us
    ppermute x6, waiting for transfers between devices, around(): return lax.ppermute(cells, ('gx', 'gy'), route)  6.83 us
    all_to_all x1, starting transfers between devices, along_z(): return lax.all_to_all(rows, 'gx', 0, 0, axis_index_groups=groups)[:, 0]  5.44 us
    all_to_all x1, starting transfers between devices, every(): lax.all_to_all(jnp.broadcast_to(row[None], (count, 1, NX)), axes, 0, 0)  4.52 us
    ppermute x3, starting transfers between devices, inflow_to(): plane = lax.ppermute(plane, 'role', [(0, 1)])  4.01 us
  transfers between devices with their start and end apart: 11, of which 8 were waited for; matrix products, arithmetic and copies ran while one was open for 1% of the time, Pallas kernels for 5%

profile of v4, /device:TPU:32, one launch (start us, length us, event | category | flops | bytes accessed | tf_op | source)
XLA Modules:
  0.0 103.1 jit_solution(6990189462996665843)
XLA Ops:
  0.7 0.1 pad_add_fusion.info
  0.8 0.9 copy-done
  1.8 0.8 pack.1
  2.6 24.9 %all_to_all.25.chunks = f32[16,6,8,128]{3,2,1,0:T(8,128)S(1)} all-to-all(f32[16,6,8,128]{3,2,1,0:T(8,128)S(1)} %get-tuple-element.21), channel_id=1, replica_groups=mesh['role'=2,'gx'=16,'gy'=8] {'gx'}, dimensions={0} | all-to-all | bytes 786432 | tf_op jit(solution)/shard_map/all_to_all | solution.py:480
  27.5 0.7 copy-done.2
  28.2 0.8 first.1
  29.0 1.3 %collective-permute-start = (f32[16,128]{1,0:T(8,128)S(1)}, f32[16,128]{1,0:T(8,128)S(1)}, u32[]{:S(2)}, u32[]{:S(2)}) collective-permute-start(f32[16,128]{1,0:T(8,128)S(1)} %get-tuple-element.23), channel_id=1, source_target_pairs={{0,128},{1,129},{2,130},{3,131},{4,132},{5,133},{6,134},{7,135},{8... | collective-permute-start | bytes 24584 | tf_op jit(solution)/shard_map/ppermute | solution.py:442
  30.3 0.8 collective-permute-done
  31.1 0.3 collective-permute-start.2
  31.5 1.7 %collective-permute-start.1 = (f32[656,128]{1,0:T(8,128)S(1)}, f32[656,128]{1,0:T(8,128)S(1)}, u32[]{:S(2)}, u32[]{:S(2)}) collective-permute-start(f32[656,128]{1,0:T(8,128)S(1)} %constant_dynamic-update-slice_fusion.2.refs_4_.refs_1_), channel_id=1, source_target_pairs={{0,8},{8,16},{16,24},{24,32},{32,40},{40,48},{48,56},{56,120},{120... | collective-permute-start | bytes 1007624 | tf_op jit(solution)/shard_map/ppermute | solution.py:438
  33.2 0.6 broadcast_in_dim.28
  33.8 4.5 %all-to-all-start.1 = ((f32[16,1,128]{2,1,0:T(1,128)}), f32[16,1,128]{2,1,0:T(1,128)S(1)}, u32[]{:S(2)}, u32[]{:S(2)}) async-start(f32[16,1,128]{2,1,0:T(1,128)} %broadcast_in_dim.28), calls=%async_computation.1 | async-start | bytes 16384 | tf_op jit(solution)/shard_map/all_to_all | solution.py:451
  38.3 3.0 %collective-permute-done.2.refs_5_.refs_2_ = f32[656,128]{1,0:T(8,128)S(1)} collective-permute-done((f32[656,128]{1,0:T(8,128)S(1)}, f32[656,128]{1,0:T(8,128)S(1)}, u32[]{:S(2)}, u32[]{:S(2)}) %collective-permute-start.2) | collective-permute-done | bytes 335904 | tf_op jit(solution)/shard_map/ppermute | solution.py:438
  41.3 1.2 %collective-permute-done.1.refs_3_.refs_0_ = f32[656,128]{1,0:T(8,128)S(1)} collective-permute-done((f32[656,128]{1,0:T(8,128)S(1)}, f32[656,128]{1,0:T(8,128)S(1)}, u32[]{:S(2)}, u32[]{:S(2)}) %collective-permute-start.1) | collective-permute-done | bytes 335904 | tf_op jit(solution)/shard_map/ppermute | solution.py:438
  42.4 2.4 %section0.1 = (f32[528,128]{1,0:T(8,128)S(1)}, f32[16,128]{1,0:T(8,128)S(1)}, f32[1,128]{1,0:T(1,128)S(1)}) custom-call(s32[4]{0:T(128)S(1)} %pad_add_fusion.info, s32[128]{0:T(128)S(1)} %copy-done.2, s32[128]{0:T(128)S(1)} %copy-done.3, f32[3,128]{1,0:T(4,128)S(1)} %get-tuple-element.20.rises.refs_2_, ...), custom_call_target="tpu_custom_call" | custom-call | tf_op jit(solution)/shard_map/section0/pallas_call | solution.py:402
  44.8 1.4 %collective-permute-start.3 = (f32[16,128]{1,0:T(8,128)S(1)}, f32[16,128]{1,0:T(8,128)S(1)}, u32[]{:S(2)}, u32[]{:S(2)}) collective-permute-start(f32[16,128]{1,0:T(8,128)S(1)} %get-tuple-element.27), channel_id=1, source_target_pairs={{0,128},{1,129},{2,130},{3,131},{4,132},{5,133},{6,134},{7,135},{8... | collective-permute-start | bytes 24584 | tf_op jit(solution)/shard_map/ppermute | solution.py:442
  46.3 0.8 collective-permute-done.3
  47.1 3.8 %collective-permute-start.5 = (f32[528,128]{1,0:T(8,128)S(1)}, f32[528,128]{1,0:T(8,128)S(1)}, u32[]{:S(2)}, u32[]{:S(2)}) collective-permute-start(f32[528,128]{1,0:T(8,128)S(1)} %constant_dynamic-update-slice_fusion.1.refs_7_), channel_id=1, source_target_pairs={{0,7},{8,0},{16,8},{24,16},{32,24},{40,32},{48,40},{56,48},{120,56... | collective-permute-start | bytes 811016 | tf_op jit(solution)/shard_map/ppermute | solution.py:438
  50.8 0.6 broadcast_in_dim.30
  51.4 5.4 %all-to-all-start.2 = ((f32[8,1,128]{2,1,0:T(1,128)}), f32[8,1,128]{2,1,0:T(1,128)S(1)}, u32[]{:S(2)}, u32[]{:S(2)}) async-start(f32[8,1,128]{2,1,0:T(1,128)} %broadcast_in_dim.30), calls=%async_computation.2 | async-start | bytes 8192 | tf_op jit(solution)/shard_map/all_to_all | solution.py:457
  56.9 0.2 collective-permute-done.5.refs_8_
  57.1 2.5 %collective-permute-done.4.refs_6_ = f32[528,128]{1,0:T(8,128)S(1)} collective-permute-done((f32[528,128]{1,0:T(8,128)S(1)}, f32[528,128]{1,0:T(8,128)S(1)}, u32[]{:S(2)}, u32[]{:S(2)}) %collective-permute-start.4) | collective-permute-done | bytes 270368 | tf_op jit(solution)/shard_map/ppermute | solution.py:438
  59.6 2.4 %section1.1 = (f32[528,128]{1,0:T(8,128)S(1)}, f32[16,128]{1,0:T(8,128)S(1)}, f32[1,128]{1,0:T(1,128)S(1)}) custom-call(s32[4]{0:T(128)S(1)} %pad_add_fusion.info, s32[128]{0:T(128)S(1)} %copy-done.2, s32[128]{0:T(128)S(1)} %copy-done.3, f32[3,128]{1,0:T(4,128)S(1)} %get-tuple-element.20.rises.refs_2_, ...), custom_call_target="tpu_custom_call" | custom-call | tf_op jit(solution)/shard_map/section1/pallas_call | solution.py:402
  62.0 1.1 %all-to-all-done.2 = f32[8,1,128]{2,1,0:T(1,128)S(1)} async-done(((f32[8,1,128]{2,1,0:T(1,128)}), f32[8,1,128]{2,1,0:T(1,128)S(1)}, u32[]{:S(2)}, u32[]{:S(2)}) %all-to-all-start.2) | async-done | bytes 4128 | tf_op jit(solution)/shard_map/all_to_all | solution.py:457
  63.0 1.3 %collective-permute-start.6 = (f32[16,128]{1,0:T(8,128)S(1)}, f32[16,128]{1,0:T(8,128)S(1)}, u32[]{:S(2)}, u32[]{:S(2)}) collective-permute-start(f32[16,128]{1,0:T(8,128)S(1)} %get-tuple-element.32), channel_id=1, source_target_pairs={{0,128},{1,129},{2,130},{3,131},{4,132},{5,133},{6,134},{7,135},{8... | collective-permute-start | bytes 24584 | tf_op jit(solution)/shard_map/ppermute | solution.py:442
  64.3 0.8 collective-permute-done.6
  65.1 2.8 %collective-permute-start.8 = (f32[528,128]{1,0:T(8,128)S(1)}, f32[528,128]{1,0:T(8,128)S(1)}, u32[]{:S(2)}, u32[]{:S(2)}) collective-permute-start(f32[528,128]{1,0:T(8,128)S(1)} %constant_dynamic-update-slice_fusion.refs_4_), channel_id=1, source_target_pairs={{0,7},{8,0},{16,8},{24,16},{32,24},{40,32},{48,40},{56,48},{120,56... | collective-permute-start | bytes 811016 | tf_op jit(solution)/shard_map/ppermute | solution.py:438
  67.9 0.1 maximum_bitcast_fusion
  68.0 12.6 %all_to_all.26 = f32[32,1,128]{2,1,0:T(1,128)S(1)} all-to-all(f32[32,1,128]{2,1,0:T(1,128)S(1)} %broadcast_in_dim.33), channel_id=1, replica_groups={{0,1,2,3,4,5,6,7,64,65,66,67,68,69,70,71,128,129,130,131,132,133,134,13..., dimensions={0} | all-to-all | bytes 32768 | tf_op jit(solution)/shard_map/all_to_all | solution.py:464
  80.6 2.5 %section2.1 = f32[16,5,8,128]{3,2,1,0:T(8,128)S(1)} custom-call(s32[4]{0:T(128)S(1)} %pad_add_fusion.info, f32[656,128]{1,0:T(8,128)S(1)} %collective-permute-done.1.refs_3_.refs_0_, f32[656,128]{1,0:T(8,128)S(1)} %constant_dynamic-update-slice_fusion.2.refs_4_.refs_1_, f32[656,128]{1,0:T(8,128)S(1)} %collective-permute-done.2.refs_5_.refs_2_, ...), custom_call_target="tpu_custom_call" | custom-call | tf_op jit(solution)/shard_map/section2/pallas_call | solution.py:402
  83.1 18.5 %all_to_all.27.chunks = f32[16,5,8,128]{3,2,1,0:T(8,128)S(1)} all-to-all(f32[16,5,8,128]{3,2,1,0:T(8,128)S(1)} %section2.1), channel_id=1, replica_groups=mesh['role'=2,'gx'=16,'gy'=8] {'gx'}, dimensions={0} | all-to-all | bytes 655360 | tf_op jit(solution)/shard_map/all_to_all | solution.py:497
  101.6 1.5 %last.1 = f32[4,128,128]{2,1,0:T(8,128)} custom-call(s32[4]{0:T(128)S(1)} %pad_add_fusion.info, f32[16,5,8,128]{3,2,1,0:T(8,128)S(1)} %all_to_all.27.chunks), custom_call_target="tpu_custom_call" | custom-call | tf_op jit(solution)/shard_map/last/pallas_call | solution.py:402
  (16 shorter events, 0.1 us)
Async XLA Ops:
  0.0 0.8 copy-start.1
  0.8 0.9 copy-start
  27.5 0.7 copy-start.2
  27.5 0.7 copy-start.3
  29.0 2.1 %collective-permute-start = (f32[16,128]{1,0:T(8,128)S(1)}, f32[16,128]{1,0:T(8,128)S(1)}, u32[]{:S(2)}, u32[]{:S(2)}) collective-permute-start(f32[16,128]{1,0:T(8,128)S(1)} %get-tuple-element.23), channel_id=1, source_target_pairs={{0,128},{1,129},{2,130},{3,131},{4,132},{5,133},{6,134},{7,135},{8... | collective-permute-start | bytes 24584 | tf_op jit(solution)/shard_map/ppermute | solution.py:442
  31.1 10.1 %collective-permute-start.2 = (f32[656,128]{1,0:T(8,128)S(1)}, f32[656,128]{1,0:T(8,128)S(1)}, u32[]{:S(2)}, u32[]{:S(2)}) collective-permute-start(f32[656,128]{1,0:T(8,128)S(1)} %constant_dynamic-update-slice_fusion.2.refs_4_.refs_1_), channel_id=1, source_target_pairs={{0,7},{8,0},{16,8},{24,16},{32,24},{40,32},{48,40},{56,48},{120,56... | collective-permute-start | bytes 1007624 | tf_op jit(solution)/shard_map/ppermute | solution.py:438
  31.5 11.0 %collective-permute-start.1 = (f32[656,128]{1,0:T(8,128)S(1)}, f32[656,128]{1,0:T(8,128)S(1)}, u32[]{:S(2)}, u32[]{:S(2)}) collective-permute-start(f32[656,128]{1,0:T(8,128)S(1)} %constant_dynamic-update-slice_fusion.2.refs_4_.refs_1_), channel_id=1, source_target_pairs={{0,8},{8,16},{16,24},{24,32},{32,40},{40,48},{48,56},{56,120},{120... | collective-permute-start | bytes 1007624 | tf_op jit(solution)/shard_map/ppermute | solution.py:438
  33.8 11.0 %all-to-all-start.1 = ((f32[16,1,128]{2,1,0:T(1,128)}), f32[16,1,128]{2,1,0:T(1,128)S(1)}, u32[]{:S(2)}, u32[]{:S(2)}) async-start(f32[16,1,128]{2,1,0:T(1,128)} %broadcast_in_dim.28), calls=%async_computation.1 | async-start | bytes 16384 | tf_op jit(solution)/shard_map/all_to_all | solution.py:451
  44.8 2.3 %collective-permute-start.3 = (f32[16,128]{1,0:T(8,128)S(1)}, f32[16,128]{1,0:T(8,128)S(1)}, u32[]{:S(2)}, u32[]{:S(2)}) collective-permute-start(f32[16,128]{1,0:T(8,128)S(1)} %get-tuple-element.27), channel_id=1, source_target_pairs={{0,128},{1,129},{2,130},{3,131},{4,132},{5,133},{6,134},{7,135},{8... | collective-permute-start | bytes 24584 | tf_op jit(solution)/shard_map/ppermute | solution.py:442
  47.1 10.0 %collective-permute-start.5 = (f32[528,128]{1,0:T(8,128)S(1)}, f32[528,128]{1,0:T(8,128)S(1)}, u32[]{:S(2)}, u32[]{:S(2)}) collective-permute-start(f32[528,128]{1,0:T(8,128)S(1)} %constant_dynamic-update-slice_fusion.1.refs_7_), channel_id=1, source_target_pairs={{0,7},{8,0},{16,8},{24,16},{32,24},{40,32},{48,40},{56,48},{120,56... | collective-permute-start | bytes 811016 | tf_op jit(solution)/shard_map/ppermute | solution.py:438
  50.8 8.7 %collective-permute-start.4 = (f32[528,128]{1,0:T(8,128)S(1)}, f32[528,128]{1,0:T(8,128)S(1)}, u32[]{:S(2)}, u32[]{:S(2)}) collective-permute-start(f32[528,128]{1,0:T(8,128)S(1)} %constant_dynamic-update-slice_fusion.1.refs_7_), channel_id=1, source_target_pairs={{0,8},{8,16},{16,24},{24,32},{32,40},{40,48},{48,56},{56,120},{120... | collective-permute-start | bytes 811016 | tf_op jit(solution)/shard_map/ppermute | solution.py:438
  51.4 11.6 %all-to-all-start.2 = ((f32[8,1,128]{2,1,0:T(1,128)}), f32[8,1,128]{2,1,0:T(1,128)S(1)}, u32[]{:S(2)}, u32[]{:S(2)}) async-start(f32[8,1,128]{2,1,0:T(1,128)} %broadcast_in_dim.30), calls=%async_computation.2 | async-start | bytes 8192 | tf_op jit(solution)/shard_map/all_to_all | solution.py:457
  63.0 2.1 %collective-permute-start.6 = (f32[16,128]{1,0:T(8,128)S(1)}, f32[16,128]{1,0:T(8,128)S(1)}, u32[]{:S(2)}, u32[]{:S(2)}) collective-permute-start(f32[16,128]{1,0:T(8,128)S(1)} %get-tuple-element.32), channel_id=1, source_target_pairs={{0,128},{1,129},{2,130},{3,131},{4,132},{5,133},{6,134},{7,135},{8... | collective-permute-start | bytes 24584 | tf_op jit(solution)/shard_map/ppermute | solution.py:442
  65.1 15.5 %collective-permute-start.8 = (f32[528,128]{1,0:T(8,128)S(1)}, f32[528,128]{1,0:T(8,128)S(1)}, u32[]{:S(2)}, u32[]{:S(2)}) collective-permute-start(f32[528,128]{1,0:T(8,128)S(1)} %constant_dynamic-update-slice_fusion.refs_4_), channel_id=1, source_target_pairs={{0,7},{8,0},{16,8},{24,16},{32,24},{40,32},{48,40},{56,48},{120,56... | collective-permute-start | bytes 811016 | tf_op jit(solution)/shard_map/ppermute | solution.py:438
  67.9 12.7 %collective-permute-start.7 = (f32[528,128]{1,0:T(8,128)S(1)}, f32[528,128]{1,0:T(8,128)S(1)}, u32[]{:S(2)}, u32[]{:S(2)}) collective-permute-start(f32[528,128]{1,0:T(8,128)S(1)} %constant_dynamic-update-slice_fusion.refs_4_), channel_id=1, source_target_pairs={{0,8},{8,16},{16,24},{24,32},{32,40},{40,48},{48,56},{56,120},{120... | collective-permute-start | bytes 811016 | tf_op jit(solution)/shard_map/ppermute | solution.py:438

commit v5 on v4

--- a/solution.py
+++ b/solution.py
@@ -418,7 +418,7 @@
     row = (NZ, NX)
     scratch = [(4, EXT), (4, EXT), (2, EXT), (EXT,), (4, EXT)]
     scratch = [pltpu.VMEM((*lead, *row), jnp.float32) for lead in scratch]
-    scratch.append(pltpu.VMEM((4 * FIELD, NX), jnp.float32))
+    scratch.append(pltpu.VMEM((4 * FIELD + ROWS, NX), jnp.float32))
     body = functools.partial(section_kernel, section)
     return call(body, f"section{section}", small, args, outs, scratch)
 

time: 103 us -> 103 us (level)
  no operation moved by 1% of the time
where the time goes in v5:
time: 103 us
  blocking collectives  56 us (54%)
  starting transfers between devices  22.5 us (22%)
  Pallas kernels  10.3 us (10%)
  waiting for transfers between devices  10.3 us (10%)
  local copies, waits for them, and re-layouts  2.91 us (3%)
    all_to_all x2, blocking collectives, per_device(): chunks = lax.all_to_all(chunks, 'gx', 0, 0)  43.4 us
    all_to_all x1, blocking collectives, across_z(): lax.all_to_all(rows, ('role', 'gx', 'gy'), 0, 0, axis_index_groups=groups)  12.6 us
    pallas_call x6, Pallas kernels, call(): pl.pallas_call(body, name=name, out_shape=outs, in_specs=[SMEM] * len(sma...  10.3 us
    ppermute x6, starting transfers between devices, around(): return lax.ppermute(cells, ('gx', 'gy'), route)  8.58 us
    ppermute x6, waiting for transfers between devices, around(): return lax.ppermute(cells, ('gx', 'gy'), route)  6.83 us
    all_to_all x1, starting transfers between devices, along_z(): return lax.all_to_all(rows, 'gx', 0, 0, axis_index_groups=groups)[:, 0]  5.44 us
    all_to_all x1, starting transfers between devices, every(): lax.all_to_all(jnp.broadcast_to(row[None], (count, 1, NX)), axes, 0, 0)  4.52 us
    ppermute x3, starting transfers between devices, inflow_to(): plane = lax.ppermute(plane, 'role', [(0, 1)])  4.01 us
  transfers between devices with their start and end apart: 11, of which 8 were waited for; matrix products, arithmetic and copies ran while one was open for 1% of the time, Pallas kernels for 5%

profile of v5, /device:TPU:32, one launch (start us, length us, event | category | flops | bytes accessed | tf_op | source)
XLA Modules:
  0.0 103.1 jit_solution(1500884393216185096)
XLA Ops:
  0.7 0.1 pad_add_fusion.info
  0.8 0.9 copy-done
  1.8 0.8 pack.1
  2.6 24.9 %all_to_all.25.chunks = f32[16,6,8,128]{3,2,1,0:T(8,128)S(1)} all-to-all(f32[16,6,8,128]{3,2,1,0:T(8,128)S(1)} %get-tuple-element.21), channel_id=1, replica_groups=mesh['role'=2,'gx'=16,'gy'=8] {'gx'}, dimensions={0} | all-to-all | bytes 786432 | tf_op jit(solution)/shard_map/all_to_all | solution.py:480
  27.5 0.7 copy-done.2
  28.2 0.8 first.1
  29.0 1.3 %collective-permute-start = (f32[16,128]{1,0:T(8,128)S(1)}, f32[16,128]{1,0:T(8,128)S(1)}, u32[]{:S(2)}, u32[]{:S(2)}) collective-permute-start(f32[16,128]{1,0:T(8,128)S(1)} %get-tuple-element.23), channel_id=1, source_target_pairs={{0,128},{1,129},{2,130},{3,131},{4,132},{5,133},{6,134},{7,135},{8... | collective-permute-start | bytes 24584 | tf_op jit(solution)/shard_map/ppermute | solution.py:442
  30.3 0.8 collective-permute-done
  31.1 0.3 collective-permute-start.2
  31.5 1.7 %collective-permute-start.1 = (f32[656,128]{1,0:T(8,128)S(1)}, f32[656,128]{1,0:T(8,128)S(1)}, u32[]{:S(2)}, u32[]{:S(2)}) collective-permute-start(f32[656,128]{1,0:T(8,128)S(1)} %constant_dynamic-update-slice_fusion.2.refs_4_.refs_1_), channel_id=1, source_target_pairs={{0,8},{8,16},{16,24},{24,32},{32,40},{40,48},{48,56},{56,120},{120... | collective-permute-start | bytes 1007624 | tf_op jit(solution)/shard_map/ppermute | solution.py:438
  33.2 0.6 broadcast_in_dim.28
  33.8 4.5 %all-to-all-start.1 = ((f32[16,1,128]{2,1,0:T(1,128)}), f32[16,1,128]{2,1,0:T(1,128)S(1)}, u32[]{:S(2)}, u32[]{:S(2)}) async-start(f32[16,1,128]{2,1,0:T(1,128)} %broadcast_in_dim.28), calls=%async_computation.1 | async-start | bytes 16384 | tf_op jit(solution)/shard_map/all_to_all | solution.py:451
  38.3 3.0 %collective-permute-done.2.refs_5_.refs_2_ = f32[656,128]{1,0:T(8,128)S(1)} collective-permute-done((f32[656,128]{1,0:T(8,128)S(1)}, f32[656,128]{1,0:T(8,128)S(1)}, u32[]{:S(2)}, u32[]{:S(2)}) %collective-permute-start.2) | collective-permute-done | bytes 335904 | tf_op jit(solution)/shard_map/ppermute | solution.py:438
  41.3 1.2 %collective-permute-done.1.refs_3_.refs_0_ = f32[656,128]{1,0:T(8,128)S(1)} collective-permute-done((f32[656,128]{1,0:T(8,128)S(1)}, f32[656,128]{1,0:T(8,128)S(1)}, u32[]{:S(2)}, u32[]{:S(2)}) %collective-permute-start.1) | collective-permute-done | bytes 335904 | tf_op jit(solution)/shard_map/ppermute | solution.py:438
  42.4 2.4 %section0.1 = (f32[528,128]{1,0:T(8,128)S(1)}, f32[16,128]{1,0:T(8,128)S(1)}, f32[1,128]{1,0:T(1,128)S(1)}) custom-call(s32[4]{0:T(128)S(1)} %pad_add_fusion.info, s32[128]{0:T(128)S(1)} %copy-done.2, s32[128]{0:T(128)S(1)} %copy-done.3, f32[3,128]{1,0:T(4,128)S(1)} %get-tuple-element.20.rises.refs_2_, ...), custom_call_target="tpu_custom_call" | custom-call | tf_op jit(solution)/shard_map/section0/pallas_call | solution.py:402
  44.8 1.4 %collective-permute-start.3 = (f32[16,128]{1,0:T(8,128)S(1)}, f32[16,128]{1,0:T(8,128)S(1)}, u32[]{:S(2)}, u32[]{:S(2)}) collective-permute-start(f32[16,128]{1,0:T(8,128)S(1)} %get-tuple-element.27), channel_id=1, source_target_pairs={{0,128},{1,129},{2,130},{3,131},{4,132},{5,133},{6,134},{7,135},{8... | collective-permute-start | bytes 24584 | tf_op jit(solution)/shard_map/ppermute | solution.py:442
  46.3 0.8 collective-permute-done.3
  47.1 3.8 %collective-permute-start.5 = (f32[528,128]{1,0:T(8,128)S(1)}, f32[528,128]{1,0:T(8,128)S(1)}, u32[]{:S(2)}, u32[]{:S(2)}) collective-permute-start(f32[528,128]{1,0:T(8,128)S(1)} %constant_dynamic-update-slice_fusion.1.refs_7_), channel_id=1, source_target_pairs={{0,7},{8,0},{16,8},{24,16},{32,24},{40,32},{48,40},{56,48},{120,56... | collective-permute-start | bytes 811016 | tf_op jit(solution)/shard_map/ppermute | solution.py:438
  50.8 0.6 broadcast_in_dim.30
  51.4 5.4 %all-to-all-start.2 = ((f32[8,1,128]{2,1,0:T(1,128)}), f32[8,1,128]{2,1,0:T(1,128)S(1)}, u32[]{:S(2)}, u32[]{:S(2)}) async-start(f32[8,1,128]{2,1,0:T(1,128)} %broadcast_in_dim.30), calls=%async_computation.2 | async-start | bytes 8192 | tf_op jit(solution)/shard_map/all_to_all | solution.py:457
  56.9 0.2 collective-permute-done.5.refs_8_
  57.1 2.5 %collective-permute-done.4.refs_6_ = f32[528,128]{1,0:T(8,128)S(1)} collective-permute-done((f32[528,128]{1,0:T(8,128)S(1)}, f32[528,128]{1,0:T(8,128)S(1)}, u32[]{:S(2)}, u32[]{:S(2)}) %collective-permute-start.4) | collective-permute-done | bytes 270368 | tf_op jit(solution)/shard_map/ppermute | solution.py:438
  59.6 2.4 %section1.1 = (f32[528,128]{1,0:T(8,128)S(1)}, f32[16,128]{1,0:T(8,128)S(1)}, f32[1,128]{1,0:T(1,128)S(1)}) custom-call(s32[4]{0:T(128)S(1)} %pad_add_fusion.info, s32[128]{0:T(128)S(1)} %copy-done.2, s32[128]{0:T(128)S(1)} %copy-done.3, f32[3,128]{1,0:T(4,128)S(1)} %get-tuple-element.20.rises.refs_2_, ...), custom_call_target="tpu_custom_call" | custom-call | tf_op jit(solution)/shard_map/section1/pallas_call | solution.py:402
  62.0 1.1 %all-to-all-done.2 = f32[8,1,128]{2,1,0:T(1,128)S(1)} async-done(((f32[8,1,128]{2,1,0:T(1,128)}), f32[8,1,128]{2,1,0:T(1,128)S(1)}, u32[]{:S(2)}, u32[]{:S(2)}) %all-to-all-start.2) | async-done | bytes 4128 | tf_op jit(solution)/shard_map/all_to_all | solution.py:457
  63.0 1.3 %collective-permute-start.6 = (f32[16,128]{1,0:T(8,128)S(1)}, f32[16,128]{1,0:T(8,128)S(1)}, u32[]{:S(2)}, u32[]{:S(2)}) collective-permute-start(f32[16,128]{1,0:T(8,128)S(1)} %get-tuple-element.32), channel_id=1, source_target_pairs={{0,128},{1,129},{2,130},{3,131},{4,132},{5,133},{6,134},{7,135},{8... | collective-permute-start | bytes 24584 | tf_op jit(solution)/shard_map/ppermute | solution.py:442
  64.3 0.8 collective-permute-done.6
  65.1 2.8 %collective-permute-start.8 = (f32[528,128]{1,0:T(8,128)S(1)}, f32[528,128]{1,0:T(8,128)S(1)}, u32[]{:S(2)}, u32[]{:S(2)}) collective-permute-start(f32[528,128]{1,0:T(8,128)S(1)} %constant_dynamic-update-slice_fusion.refs_4_), channel_id=1, source_target_pairs={{0,7},{8,0},{16,8},{24,16},{32,24},{40,32},{48,40},{56,48},{120,56... | collective-permute-start | bytes 811016 | tf_op jit(solution)/shard_map/ppermute | solution.py:438
  67.9 0.1 maximum_bitcast_fusion
  68.0 12.6 %all_to_all.26 = f32[32,1,128]{2,1,0:T(1,128)S(1)} all-to-all(f32[32,1,128]{2,1,0:T(1,128)S(1)} %broadcast_in_dim.33), channel_id=1, replica_groups={{0,1,2,3,4,5,6,7,64,65,66,67,68,69,70,71,128,129,130,131,132,133,134,13..., dimensions={0} | all-to-all | bytes 32768 | tf_op jit(solution)/shard_map/all_to_all | solution.py:464
  80.6 2.5 %section2.1 = f32[16,5,8,128]{3,2,1,0:T(8,128)S(1)} custom-call(s32[4]{0:T(128)S(1)} %pad_add_fusion.info, f32[656,128]{1,0:T(8,128)S(1)} %collective-permute-done.1.refs_3_.refs_0_, f32[656,128]{1,0:T(8,128)S(1)} %constant_dynamic-update-slice_fusion.2.refs_4_.refs_1_, f32[656,128]{1,0:T(8,128)S(1)} %collective-permute-done.2.refs_5_.refs_2_, ...), custom_call_target="tpu_custom_call" | custom-call | tf_op jit(solution)/shard_map/section2/pallas_call | solution.py:402
  83.1 18.5 %all_to_all.27.chunks = f32[16,5,8,128]{3,2,1,0:T(8,128)S(1)} all-to-all(f32[16,5,8,128]{3,2,1,0:T(8,128)S(1)} %section2.1), channel_id=1, replica_groups=mesh['role'=2,'gx'=16,'gy'=8] {'gx'}, dimensions={0} | all-to-all | bytes 655360 | tf_op jit(solution)/shard_map/all_to_all | solution.py:497
  101.6 1.5 %last.1 = f32[4,128,128]{2,1,0:T(8,128)} custom-call(s32[4]{0:T(128)S(1)} %pad_add_fusion.info, f32[16,5,8,128]{3,2,1,0:T(8,128)S(1)} %all_to_all.27.chunks), custom_call_target="tpu_custom_call" | custom-call | tf_op jit(solution)/shard_map/last/pallas_call | solution.py:402
  (16 shorter events, 0.1 us)
Async XLA Ops:
  0.0 0.8 copy-start.1
  0.8 0.9 copy-start
  27.5 0.7 copy-start.2
  27.5 0.7 copy-start.3
  29.0 2.1 %collective-permute-start = (f32[16,128]{1,0:T(8,128)S(1)}, f32[16,128]{1,0:T(8,128)S(1)}, u32[]{:S(2)}, u32[]{:S(2)}) collective-permute-start(f32[16,128]{1,0:T(8,128)S(1)} %get-tuple-element.23), channel_id=1, source_target_pairs={{0,128},{1,129},{2,130},{3,131},{4,132},{5,133},{6,134},{7,135},{8... | collective-permute-start | bytes 24584 | tf_op jit(solution)/shard_map/ppermute | solution.py:442
  31.1 10.1 %collective-permute-start.2 = (f32[656,128]{1,0:T(8,128)S(1)}, f32[656,128]{1,0:T(8,128)S(1)}, u32[]{:S(2)}, u32[]{:S(2)}) collective-permute-start(f32[656,128]{1,0:T(8,128)S(1)} %constant_dynamic-update-slice_fusion.2.refs_4_.refs_1_), channel_id=1, source_target_pairs={{0,7},{8,0},{16,8},{24,16},{32,24},{40,32},{48,40},{56,48},{120,56... | collective-permute-start | bytes 1007624 | tf_op jit(solution)/shard_map/ppermute | solution.py:438
  31.5 11.0 %collective-permute-start.1 = (f32[656,128]{1,0:T(8,128)S(1)}, f32[656,128]{1,0:T(8,128)S(1)}, u32[]{:S(2)}, u32[]{:S(2)}) collective-permute-start(f32[656,128]{1,0:T(8,128)S(1)} %constant_dynamic-update-slice_fusion.2.refs_4_.refs_1_), channel_id=1, source_target_pairs={{0,8},{8,16},{16,24},{24,32},{32,40},{40,48},{48,56},{56,120},{120... | collective-permute-start | bytes 1007624 | tf_op jit(solution)/shard_map/ppermute | solution.py:438
  33.8 11.0 %all-to-all-start.1 = ((f32[16,1,128]{2,1,0:T(1,128)}), f32[16,1,128]{2,1,0:T(1,128)S(1)}, u32[]{:S(2)}, u32[]{:S(2)}) async-start(f32[16,1,128]{2,1,0:T(1,128)} %broadcast_in_dim.28), calls=%async_computation.1 | async-start | bytes 16384 | tf_op jit(solution)/shard_map/all_to_all | solution.py:451
  44.8 2.3 %collective-permute-start.3 = (f32[16,128]{1,0:T(8,128)S(1)}, f32[16,128]{1,0:T(8,128)S(1)}, u32[]{:S(2)}, u32[]{:S(2)}) collective-permute-start(f32[16,128]{1,0:T(8,128)S(1)} %get-tuple-element.27), channel_id=1, source_target_pairs={{0,128},{1,129},{2,130},{3,131},{4,132},{5,133},{6,134},{7,135},{8... | collective-permute-start | bytes 24584 | tf_op jit(solution)/shard_map/ppermute | solution.py:442
  47.1 10.0 %collective-permute-start.5 = (f32[528,128]{1,0:T(8,128)S(1)}, f32[528,128]{1,0:T(8,128)S(1)}, u32[]{:S(2)}, u32[]{:S(2)}) collective-permute-start(f32[528,128]{1,0:T(8,128)S(1)} %constant_dynamic-update-slice_fusion.1.refs_7_), channel_id=1, source_target_pairs={{0,7},{8,0},{16,8},{24,16},{32,24},{40,32},{48,40},{56,48},{120,56... | collective-permute-start | bytes 811016 | tf_op jit(solution)/shard_map/ppermute | solution.py:438
  50.8 8.7 %collective-permute-start.4 = (f32[528,128]{1,0:T(8,128)S(1)}, f32[528,128]{1,0:T(8,128)S(1)}, u32[]{:S(2)}, u32[]{:S(2)}) collective-permute-start(f32[528,128]{1,0:T(8,128)S(1)} %constant_dynamic-update-slice_fusion.1.refs_7_), channel_id=1, source_target_pairs={{0,8},{8,16},{16,24},{24,32},{32,40},{40,48},{48,56},{56,120},{120... | collective-permute-start | bytes 811016 | tf_op jit(solution)/shard_map/ppermute | solution.py:438
  51.4 11.6 %all-to-all-start.2 = ((f32[8,1,128]{2,1,0:T(1,128)}), f32[8,1,128]{2,1,0:T(1,128)S(1)}, u32[]{:S(2)}, u32[]{:S(2)}) async-start(f32[8,1,128]{2,1,0:T(1,128)} %broadcast_in_dim.30), calls=%async_computation.2 | async-start | bytes 8192 | tf_op jit(solution)/shard_map/all_to_all | solution.py:457
  63.0 2.1 %collective-permute-start.6 = (f32[16,128]{1,0:T(8,128)S(1)}, f32[16,128]{1,0:T(8,128)S(1)}, u32[]{:S(2)}, u32[]{:S(2)}) collective-permute-start(f32[16,128]{1,0:T(8,128)S(1)} %get-tuple-element.32), channel_id=1, source_target_pairs={{0,128},{1,129},{2,130},{3,131},{4,132},{5,133},{6,134},{7,135},{8... | collective-permute-start | bytes 24584 | tf_op jit(solution)/shard_map/ppermute | solution.py:442
  65.1 15.5 %collective-permute-start.8 = (f32[528,128]{1,0:T(8,128)S(1)}, f32[528,128]{1,0:T(8,128)S(1)}, u32[]{:S(2)}, u32[]{:S(2)}) collective-permute-start(f32[528,128]{1,0:T(8,128)S(1)} %constant_dynamic-update-slice_fusion.refs_4_), channel_id=1, source_target_pairs={{0,7},{8,0},{16,8},{24,16},{32,24},{40,32},{48,40},{56,48},{120,56... | collective-permute-start | bytes 811016 | tf_op jit(solution)/shard_map/ppermute | solution.py:438
  67.9 12.7 %collective-permute-start.7 = (f32[528,128]{1,0:T(8,128)S(1)}, f32[528,128]{1,0:T(8,128)S(1)}, u32[]{:S(2)}, u32[]{:S(2)}) collective-permute-start(f32[528,128]{1,0:T(8,128)S(1)} %constant_dynamic-update-slice_fusion.refs_4_), channel_id=1, source_target_pairs={{0,8},{8,16},{16,24},{24,32},{32,40},{40,48},{48,56},{56,120},{120... | collective-permute-start | bytes 811016 | tf_op jit(solution)/shard_map/ppermute | solution.py:438

commit v6 on v5

--- a/solution.py
+++ b/solution.py
@@ -27,7 +27,6 @@
 CELLS = 131072.0
 SIXTH = 1.0 / 6.0
 FIELD = ROWS * NZ
-DRAG_AT = 4 * FIELD
 
 
 def lanes(rows=NZ):
@@ -176,7 +175,7 @@
             out[owner_of(block, flip), f] = flat[ROWS * block : ROWS * (block + 1)]
 
 
-def first_kernel(info, sample, level, rises, chunks, buf, plane, sums_out):
+def first_kernel(info, sample, level, rises, chunks, buf, drag, plane, sums_out):
     base = info[3]
     picked = jnp.zeros((NZ, NX), jnp.float32)
     sums = chunks[0, 5, :1]
@@ -186,7 +185,10 @@
     for f in range(5):
         tiles = skewed([chunks[s, f] for s in range(BLOCKS)])
         for z in range(NZ):
-            buf[pl.ds(f * FIELD + z, ROWS, stride=NZ), :] = turned(tiles[z], -z)
+            if f < 4:
+                buf[pl.ds(f * FIELD + z, ROWS, stride=NZ), :] = turned(tiles[z], -z)
+            else:
+                drag[pl.ds(z, ROWS, stride=NZ), :] = turned(tiles[z], -z)
     for f in range(4):
         for r in range(ROWS):
             spot = f * ROWS + r
@@ -194,7 +196,7 @@
             picked = sampled(picked, f, r, cells, sample, base)
     picked = with_gust(picked, level, base, rises[:1])
     plane[...] = picked
-    buf[5 * FIELD :, :] = picked
+    buf[4 * FIELD :, :] = picked
 
 
 def section_kernel(section, info, *refs):
@@ -208,6 +210,7 @@
     if section < 2:
         sample, level, rises = take(3)
         base = info[3]
+    drags = take(3)
     starts = take(3)
     bufs = take(3) if section else starts
     if section:
@@ -221,7 +224,7 @@
     role = info[0]
     step = SECTION_C[section] * DT
     walls = Walls(role == 1)
-    plane_at = (4 if section else 5) * FIELD
+    plane_at = 4 * FIELD
 
     if section:
         pre, own = role_totals(sums_in, role)
@@ -273,8 +276,8 @@
         e = g_z[1] + g_y[2]
         strain = g_x[0] * g_x[0] + g_y[1] * g_y[1] + g_z[2] * g_z[2] + 0.5 * (a * a + b * b + e * e)
         nu = SMAG * jnp.sqrt(2.0 * strain + EPS)
-        at = pl.multiple_of(DRAG_AT + r * NZ, NZ)
-        resist = starts[side][pl.ds(at, NZ), :] * jnp.sqrt(u * u + v * v + EPS)
+        at = pl.multiple_of(r * NZ, NZ)
+        resist = drags[side][pl.ds(at, NZ), :] * jnp.sqrt(u * u + v * v + EPS)
         rates = []
         for f in range(3):
             lap = after[f] + before[f] + nxt[f] + prv[f] + hi[f] + lo[f] - 6.0 * mid[f]
@@ -438,6 +441,12 @@
     return lax.ppermute(cells, ("gx", "gy"), route)
 
 
+def farm_around(cells, distance):
+    order = ring_order()
+    route = [(128 + d, 128 + order[(i + distance) % 128]) for i, d in enumerate(order)]
+    return lax.ppermute(cells, ("role", "gx", "gy"), route)
+
+
 def inflow_to(buf, plane):
     plane = lax.ppermute(plane, "role", [(0, 1)])
     return lax.dynamic_update_slice(buf, plane, (buf.shape[0] - NZ, 0))
@@ -478,22 +487,23 @@
     chunks, rises = lax.optimization_barrier((chunks, rises))
     inlet = (info, sample_x, gust_level)
     chunks = lax.all_to_all(chunks, "gx", 0, 0)
-    outs = [shape(5 * FIELD + NZ, NX), shape(NZ, NX), shape(1, NX)]
+    outs = [shape(4 * FIELD + NZ, NX), shape(FIELD + NZ, NX), shape(NZ, NX), shape(1, NX)]
     args = (rises, chunks)
-    buf, plane, sums = call(first_kernel, "first", inlet, args, outs)
+    buf, drag, plane, sums = call(first_kernel, "first", inlet, args, outs)
     starts = halo(inflow_to(buf, plane))
+    drags = (farm_around(drag, 1), drag, farm_around(drag, -1))
     totals = every(sums, ("role", "gy"), 16)
-    buf, plane, sums = section_call(0, inlet, (rises, *starts))
+    buf, plane, sums = section_call(0, inlet, (rises, *drags, *starts))
     plane, totals = lax.optimization_barrier((plane, totals))
     bufs = halo(inflow_to(buf, plane))
     rows = along_z(sums)
-    buf, plane, sums = section_call(1, inlet, (rises, *starts, *bufs, totals))
+    buf, plane, sums = section_call(1, inlet, (rises, *drags, *starts, *bufs, totals))
     plane, rows = lax.optimization_barrier((plane, rows))
     bufs = halo(inflow_to(buf, plane))
     row = jnp.sum(rows, axis=0, keepdims=True)
     row = jnp.concatenate([sums[:, :NZ], row[:, : NX - NZ]], axis=1)
     totals = across_z(row)
-    (chunks,) = section_call(2, (info,), (*starts, *bufs, totals))
+    (chunks,) = section_call(2, (info,), (*drags, *starts, *bufs, totals))
     chunks = lax.all_to_all(chunks, "gx", 0, 0)
     scratch = [pltpu.VMEM((4, 128, 128), jnp.float32), pltpu.SemaphoreType.DMA((4,))]
     outs = [shape(4, 128, 128)]

time: 103 us -> 108 us (1.049)
  starting transfers between devices: 22.5 us -> 28.5 us
  blocking collectives: 56 us -> 54.7 us
    ppermute x6, waiting for transfers between devices: 6.83 us -> 1.19 us  [around(): return lax.ppermute(cells, ('gx', 'gy'), route)]
    all_to_all x1, starting transfers between devices: 4.52 us -> 9.36 us  [every(): lax.all_to_all(jnp.broadcast_to(row[None], (count, 1, NX)), axes, 0, 0)]
    all_to_all x1, waiting for transfers between devices: 0.01 us -> 3.59 us  [every(): lax.all_to_all(jnp.broadcast_to(row[None], (count, 1, NX)), axes, 0, 0)]
    ppermute x6, starting transfers between devices: 8.58 us -> 6.83 us  [around(): return lax.ppermute(cells, ('gx', 'gy'), route)]
    all_to_all x1, waiting for transfers between devices: 1.07 us -> 2.54 us  [along_z(): return lax.all_to_all(rows, 'gx', 0, 0, axis_index_groups=groups)[:, 0]]
    ppermute x0 -> x2, starting transfers between devices: none -> 1.32 us  [farm_around(): return lax.ppermute(cells, ('role', 'gx', 'gy'), route)]
    all_to_all x1, blocking collectives: 12.6 us -> 11.3 us  [across_z(): lax.all_to_all(rows, ('role', 'gx', 'gy'), 0, 0, axis_index_groups=groups)]
    all_to_all x1, starting transfers between devices: 5.44 us -> 6.69 us  [along_z(): return lax.all_to_all(rows, 'gx', 0, 0, axis_index_groups=groups)[:, 0]]
  transfers between devices with their start and end apart: 11 -> 13, of which waited for: 8 -> 6; matrix products, arithmetic and copies ran while one was open for 1% -> 1% of each run, Pallas kernels for 5% -> 4%
where the time goes in v6:
time: 108 us; the launch traced here: 107 us
  blocking collectives  54.7 us (51%)
  starting transfers between devices  28.5 us (26%)
  Pallas kernels  10.4 us (10%)
  waiting for transfers between devices  9.76 us (9%)
  local copies, waits for them, and re-layouts  2.91 us (3%)
    all_to_all x2, blocking collectives, per_device(): chunks = lax.all_to_all(chunks, 'gx', 0, 0)  43.4 us
    all_to_all x1, blocking collectives, across_z(): lax.all_to_all(rows, ('role', 'gx', 'gy'), 0, 0, axis_index_groups=groups)  11.3 us
    pallas_call x6, Pallas kernels, call(): pl.pallas_call(body, name=name, out_shape=outs, in_specs=[SMEM] * len(sma...  10.4 us
    all_to_all x1, starting transfers between devices, every(): lax.all_to_all(jnp.broadcast_to(row[None], (count, 1, NX)), axes, 0, 0)  9.36 us
    ppermute x6, starting transfers between devices, around(): return lax.ppermute(cells, ('gx', 'gy'), route)  6.83 us
    all_to_all x1, starting transfers between devices, along_z(): return lax.all_to_all(rows, 'gx', 0, 0, axis_index_groups=groups)[:, 0]  6.69 us
    ppermute x3, starting transfers between devices, inflow_to(): plane = lax.ppermute(plane, 'role', [(0, 1)])  4.27 us
    all_to_all x1, waiting for transfers between devices, every(): lax.all_to_all(jnp.broadcast_to(row[None], (count, 1, NX)), axes, 0, 0)  3.59 us
  transfers between devices with their start and end apart: 13, of which 6 were waited for; matrix products, arithmetic and copies ran while one was open for 1% of the time, Pallas kernels for 4%

profile of v6, /device:TPU:32, one launch (start us, length us, event | category | flops | bytes accessed | tf_op | source)
XLA Modules:
  0.0 107.2 jit_solution(2667948521829619801)
XLA Ops:
  0.7 0.1 pad_add_fusion.info
  0.8 0.9 copy-done
  1.8 0.8 pack.1
  2.6 24.9 %all_to_all.25.chunks = f32[16,6,8,128]{3,2,1,0:T(8,128)S(1)} all-to-all(f32[16,6,8,128]{3,2,1,0:T(8,128)S(1)} %get-tuple-element.22), channel_id=1, replica_groups=mesh['role'=2,'gx'=16,'gy'=8] {'gx'}, dimensions={0} | all-to-all | bytes 786432 | tf_op jit(solution)/shard_map/all_to_all | solution.py:489
  27.5 0.7 copy-done.2
  28.2 0.8 first.1
  29.0 1.3 %collective-permute-start.2 = (f32[16,128]{1,0:T(8,128)S(1)}, f32[16,128]{1,0:T(8,128)S(1)}, u32[]{:S(2)}, u32[]{:S(2)}) collective-permute-start(f32[16,128]{1,0:T(8,128)S(1)} %get-tuple-element.25), channel_id=1, source_target_pairs={{0,128},{1,129},{2,130},{3,131},{4,132},{5,133},{6,134},{7,135},{8... | collective-permute-start | bytes 24584 | tf_op jit(solution)/shard_map/ppermute | solution.py:451
  30.3 0.8 collective-permute-done.2
  31.1 0.3 collective-permute-start.4
  31.5 1.7 %collective-permute-start.3 = (f32[528,128]{1,0:T(8,128)S(1)}, f32[528,128]{1,0:T(8,128)S(1)}, u32[]{:S(2)}, u32[]{:S(2)}) collective-permute-start(f32[528,128]{1,0:T(8,128)S(1)} %constant_dynamic-update-slice_fusion.2.refs_7_.refs_4_), channel_id=1, source_target_pairs={{0,8},{8,16},{16,24},{24,32},{32,40},{40,48},{48,56},{56,120},{120... | collective-permute-start | bytes 811016 | tf_op jit(solution)/shard_map/ppermute | solution.py:441
  33.2 0.7 collective-permute-start.1
  33.8 0.7 collective-permute-start
  34.5 0.6 broadcast_in_dim.28
  35.1 9.4 %all-to-all-start.1 = ((f32[16,1,128]{2,1,0:T(1,128)}), f32[16,1,128]{2,1,0:T(1,128)S(1)}, u32[]{:S(2)}, u32[]{:S(2)}) async-start(f32[16,1,128]{2,1,0:T(1,128)} %broadcast_in_dim.28), calls=%async_computation.1 | async-start | bytes 16384 | tf_op jit(solution)/shard_map/all_to_all | solution.py:460
  44.5 2.4 %section0.1 = (f32[528,128]{1,0:T(8,128)S(1)}, f32[16,128]{1,0:T(8,128)S(1)}, f32[1,128]{1,0:T(1,128)S(1)}) custom-call(s32[4]{0:T(128)S(1)} %pad_add_fusion.info, s32[128]{0:T(128)S(1)} %copy-done.2, s32[128]{0:T(128)S(1)} %copy-done.3, f32[3,128]{1,0:T(4,128)S(1)} %get-tuple-element.21.rises.refs_2_, f32[144,128]{1,0:T(8,128)S(1)} %collective-permute-done.refs_3_.refs_0_, ...), custom_call_target="tpu_custom_call" | custom-call | tf_op jit(solution)/shard_map/section0/pallas_call | solution.py:405
  46.9 3.6 %all-to-all-done.1 = f32[16,1,128]{2,1,0:T(1,128)S(1)} async-done(((f32[16,1,128]{2,1,0:T(1,128)}), f32[16,1,128]{2,1,0:T(1,128)S(1)}, u32[]{:S(2)}, u32[]{:S(2)}) %all-to-all-start.1) | async-done | bytes 8224 | tf_op jit(solution)/shard_map/all_to_all | solution.py:460
  50.5 1.7 %collective-permute-start.5 = (f32[16,128]{1,0:T(8,128)S(1)}, f32[16,128]{1,0:T(8,128)S(1)}, u32[]{:S(2)}, u32[]{:S(2)}) collective-permute-start(f32[16,128]{1,0:T(8,128)S(1)} %get-tuple-element.29), channel_id=1, source_target_pairs={{0,128},{1,129},{2,130},{3,131},{4,132},{5,133},{6,134},{7,135},{8... | collective-permute-start | bytes 24584 | tf_op jit(solution)/shard_map/ppermute | solution.py:451
  52.2 0.8 collective-permute-done.5
  53.0 2.8 %collective-permute-start.7 = (f32[528,128]{1,0:T(8,128)S(1)}, f32[528,128]{1,0:T(8,128)S(1)}, u32[]{:S(2)}, u32[]{:S(2)}) collective-permute-start(f32[528,128]{1,0:T(8,128)S(1)} %constant_dynamic-update-slice_fusion.1.refs_10_), channel_id=1, source_target_pairs={{0,7},{8,0},{16,8},{24,16},{32,24},{40,32},{48,40},{56,48},{120,56... | collective-permute-start | bytes 811016 | tf_op jit(solution)/shard_map/ppermute | solution.py:441
  55.8 0.6 broadcast_in_dim.30
  56.4 6.7 %all-to-all-start.2 = ((f32[8,1,128]{2,1,0:T(1,128)}), f32[8,1,128]{2,1,0:T(1,128)S(1)}, u32[]{:S(2)}, u32[]{:S(2)}) async-start(f32[8,1,128]{2,1,0:T(1,128)} %broadcast_in_dim.30), calls=%async_computation.2 | async-start | bytes 8192 | tf_op jit(solution)/shard_map/all_to_all | solution.py:466
  63.1 1.2 %collective-permute-done.6.refs_9_ = f32[528,128]{1,0:T(8,128)S(1)} collective-permute-done((f32[528,128]{1,0:T(8,128)S(1)}, f32[528,128]{1,0:T(8,128)S(1)}, u32[]{:S(2)}, u32[]{:S(2)}) %collective-permute-start.6) | collective-permute-done | bytes 270368 | tf_op jit(solution)/shard_map/ppermute | solution.py:441
  64.2 2.4 %section1.1 = (f32[528,128]{1,0:T(8,128)S(1)}, f32[16,128]{1,0:T(8,128)S(1)}, f32[1,128]{1,0:T(1,128)S(1)}) custom-call(s32[4]{0:T(128)S(1)} %pad_add_fusion.info, s32[128]{0:T(128)S(1)} %copy-done.2, s32[128]{0:T(128)S(1)} %copy-done.3, f32[3,128]{1,0:T(4,128)S(1)} %get-tuple-element.21.rises.refs_2_, f32[144,128]{1,0:T(8,128)S(1)} %collective-permute-done.refs_3_.refs_0_, ...), custom_call_target="tpu_custom_call" | custom-call | tf_op jit(solution)/shard_map/section1/pallas_call | solution.py:405
  66.7 2.5 %all-to-all-done.2 = f32[8,1,128]{2,1,0:T(1,128)S(1)} async-done(((f32[8,1,128]{2,1,0:T(1,128)}), f32[8,1,128]{2,1,0:T(1,128)S(1)}, u32[]{:S(2)}, u32[]{:S(2)}) %all-to-all-start.2) | async-done | bytes 4128 | tf_op jit(solution)/shard_map/all_to_all | solution.py:466
  69.2 1.3 %collective-permute-start.8 = (f32[16,128]{1,0:T(8,128)S(1)}, f32[16,128]{1,0:T(8,128)S(1)}, u32[]{:S(2)}, u32[]{:S(2)}) collective-permute-start(f32[16,128]{1,0:T(8,128)S(1)} %get-tuple-element.34), channel_id=1, source_target_pairs={{0,128},{1,129},{2,130},{3,131},{4,132},{5,133},{6,134},{7,135},{8... | collective-permute-start | bytes 24584 | tf_op jit(solution)/shard_map/ppermute | solution.py:451
  70.5 0.8 collective-permute-done.8
  71.3 1.5 %collective-permute-start.10 = (f32[528,128]{1,0:T(8,128)S(1)}, f32[528,128]{1,0:T(8,128)S(1)}, u32[]{:S(2)}, u32[]{:S(2)}) collective-permute-start(f32[528,128]{1,0:T(8,128)S(1)} %constant_dynamic-update-slice_fusion.refs_7_), channel_id=1, source_target_pairs={{0,7},{8,0},{16,8},{24,16},{32,24},{40,32},{48,40},{56,48},{120,56... | collective-permute-start | bytes 811016 | tf_op jit(solution)/shard_map/ppermute | solution.py:441
  72.8 0.6 collective-permute-start.9
  73.4 11.3 %all_to_all.26 = f32[32,1,128]{2,1,0:T(1,128)S(1)} all-to-all(f32[32,1,128]{2,1,0:T(1,128)S(1)} %broadcast_in_dim.33), channel_id=1, replica_groups={{0,1,2,3,4,5,6,7,64,65,66,67,68,69,70,71,128,129,130,131,132,133,134,13..., dimensions={0} | all-to-all | bytes 32768 | tf_op jit(solution)/shard_map/all_to_all | solution.py:473
  84.8 2.5 %section2.1 = f32[16,5,8,128]{3,2,1,0:T(8,128)S(1)} custom-call(s32[4]{0:T(128)S(1)} %pad_add_fusion.info, f32[144,128]{1,0:T(8,128)S(1)} %collective-permute-done.refs_3_.refs_0_, f32[144,128]{1,0:T(8,128)S(1)} %get-tuple-element.23.refs_4_.refs_1_, f32[144,128]{1,0:T(8,128)S(1)} %collective-permute-done.1.refs_5_.refs_2_, ...), custom_call_target="tpu_custom_call" | custom-call | tf_op jit(solution)/shard_map/section2/pallas_call | solution.py:405
  87.2 18.5 %all_to_all.27.chunks = f32[16,5,8,128]{3,2,1,0:T(8,128)S(1)} all-to-all(f32[16,5,8,128]{3,2,1,0:T(8,128)S(1)} %section2.1), channel_id=1, replica_groups=mesh['role'=2,'gx'=16,'gy'=8] {'gx'}, dimensions={0} | all-to-all | bytes 655360 | tf_op jit(solution)/shard_map/all_to_all | solution.py:507
  105.7 1.5 %last.1 = f32[4,128,128]{2,1,0:T(8,128)} custom-call(s32[4]{0:T(128)S(1)} %pad_add_fusion.info, f32[16,5,8,128]{3,2,1,0:T(8,128)S(1)} %all_to_all.27.chunks), custom_call_target="tpu_custom_call" | custom-call | tf_op jit(solution)/shard_map/last/pallas_call | solution.py:405
  (20 shorter events, 0.2 us)
Async XLA Ops:
  0.0 0.8 copy-start.1
  0.8 0.9 copy-start
  27.5 0.7 copy-start.2
  27.5 0.7 copy-start.3
  29.0 2.1 %collective-permute-start.2 = (f32[16,128]{1,0:T(8,128)S(1)}, f32[16,128]{1,0:T(8,128)S(1)}, u32[]{:S(2)}, u32[]{:S(2)}) collective-permute-start(f32[16,128]{1,0:T(8,128)S(1)} %get-tuple-element.25), channel_id=1, source_target_pairs={{0,128},{1,129},{2,130},{3,131},{4,132},{5,133},{6,134},{7,135},{8... | collective-permute-start | bytes 24584 | tf_op jit(solution)/shard_map/ppermute | solution.py:451
  31.1 13.4 %collective-permute-start.4 = (f32[528,128]{1,0:T(8,128)S(1)}, f32[528,128]{1,0:T(8,128)S(1)}, u32[]{:S(2)}, u32[]{:S(2)}) collective-permute-start(f32[528,128]{1,0:T(8,128)S(1)} %constant_dynamic-update-slice_fusion.2.refs_7_.refs_4_), channel_id=1, source_target_pairs={{0,7},{8,0},{16,8},{24,16},{32,24},{40,32},{48,40},{56,48},{120,56... | collective-permute-start | bytes 811016 | tf_op jit(solution)/shard_map/ppermute | solution.py:441
  31.5 13.0 %collective-permute-start.3 = (f32[528,128]{1,0:T(8,128)S(1)}, f32[528,128]{1,0:T(8,128)S(1)}, u32[]{:S(2)}, u32[]{:S(2)}) collective-permute-start(f32[528,128]{1,0:T(8,128)S(1)} %constant_dynamic-update-slice_fusion.2.refs_7_.refs_4_), channel_id=1, source_target_pairs={{0,8},{8,16},{16,24},{24,32},{32,40},{40,48},{48,56},{56,120},{120... | collective-permute-start | bytes 811016 | tf_op jit(solution)/shard_map/ppermute | solution.py:441
  33.2 11.3 %collective-permute-start.1 = (f32[144,128]{1,0:T(8,128)S(1)}, f32[144,128]{1,0:T(8,128)S(1)}, u32[]{:S(2)}, u32[]{:S(2)}) collective-permute-start(f32[144,128]{1,0:T(8,128)S(1)} %get-tuple-element.23.refs_4_.refs_1_), channel_id=1, source_target_pairs={{128,135},{136,128},{144,136},{152,144},{160,152},{168,160},{176,1... | collective-permute-start | bytes 221192 | tf_op jit(solution)/shard_map/ppermute | solution.py:447
  33.8 10.7 %collective-permute-start = (f32[144,128]{1,0:T(8,128)S(1)}, f32[144,128]{1,0:T(8,128)S(1)}, u32[]{:S(2)}, u32[]{:S(2)}) collective-permute-start(f32[144,128]{1,0:T(8,128)S(1)} %get-tuple-element.23.refs_4_.refs_1_), channel_id=1, source_target_pairs={{128,136},{136,144},{144,152},{152,160},{160,168},{168,176},{176,1... | collective-permute-start | bytes 221192 | tf_op jit(solution)/shard_map/ppermute | solution.py:447
  35.1 15.4 %all-to-all-start.1 = ((f32[16,1,128]{2,1,0:T(1,128)}), f32[16,1,128]{2,1,0:T(1,128)S(1)}, u32[]{:S(2)}, u32[]{:S(2)}) async-start(f32[16,1,128]{2,1,0:T(1,128)} %broadcast_in_dim.28), calls=%async_computation.1 | async-start | bytes 16384 | tf_op jit(solution)/shard_map/all_to_all | solution.py:460
  50.5 2.5 %collective-permute-start.5 = (f32[16,128]{1,0:T(8,128)S(1)}, f32[16,128]{1,0:T(8,128)S(1)}, u32[]{:S(2)}, u32[]{:S(2)}) collective-permute-start(f32[16,128]{1,0:T(8,128)S(1)} %get-tuple-element.29), channel_id=1, source_target_pairs={{0,128},{1,129},{2,130},{3,131},{4,132},{5,133},{6,134},{7,135},{8... | collective-permute-start | bytes 24584 | tf_op jit(solution)/shard_map/ppermute | solution.py:451
  53.0 10.1 %collective-permute-start.7 = (f32[528,128]{1,0:T(8,128)S(1)}, f32[528,128]{1,0:T(8,128)S(1)}, u32[]{:S(2)}, u32[]{:S(2)}) collective-permute-start(f32[528,128]{1,0:T(8,128)S(1)} %constant_dynamic-update-slice_fusion.1.refs_10_), channel_id=1, source_target_pairs={{0,7},{8,0},{16,8},{24,16},{32,24},{40,32},{48,40},{56,48},{120,56... | collective-permute-start | bytes 811016 | tf_op jit(solution)/shard_map/ppermute | solution.py:441
  55.8 8.5 %collective-permute-start.6 = (f32[528,128]{1,0:T(8,128)S(1)}, f32[528,128]{1,0:T(8,128)S(1)}, u32[]{:S(2)}, u32[]{:S(2)}) collective-permute-start(f32[528,128]{1,0:T(8,128)S(1)} %constant_dynamic-update-slice_fusion.1.refs_10_), channel_id=1, source_target_pairs={{0,8},{8,16},{16,24},{24,32},{32,40},{40,48},{48,56},{56,120},{120... | collective-permute-start | bytes 811016 | tf_op jit(solution)/shard_map/ppermute | solution.py:441
  56.4 12.8 %all-to-all-start.2 = ((f32[8,1,128]{2,1,0:T(1,128)}), f32[8,1,128]{2,1,0:T(1,128)S(1)}, u32[]{:S(2)}, u32[]{:S(2)}) async-start(f32[8,1,128]{2,1,0:T(1,128)} %broadcast_in_dim.30), calls=%async_computation.2 | async-start | bytes 8192 | tf_op jit(solution)/shard_map/all_to_all | solution.py:466
  69.2 2.1 %collective-permute-start.8 = (f32[16,128]{1,0:T(8,128)S(1)}, f32[16,128]{1,0:T(8,128)S(1)}, u32[]{:S(2)}, u32[]{:S(2)}) collective-permute-start(f32[16,128]{1,0:T(8,128)S(1)} %get-tuple-element.34), channel_id=1, source_target_pairs={{0,128},{1,129},{2,130},{3,131},{4,132},{5,133},{6,134},{7,135},{8... | collective-permute-start | bytes 24584 | tf_op jit(solution)/shard_map/ppermute | solution.py:451
  71.3 13.4 %collective-permute-start.10 = (f32[528,128]{1,0:T(8,128)S(1)}, f32[528,128]{1,0:T(8,128)S(1)}, u32[]{:S(2)}, u32[]{:S(2)}) collective-permute-start(f32[528,128]{1,0:T(8,128)S(1)} %constant_dynamic-update-slice_fusion.refs_7_), channel_id=1, source_target_pairs={{0,7},{8,0},{16,8},{24,16},{32,24},{40,32},{48,40},{56,48},{120,56... | collective-permute-start | bytes 811016 | tf_op jit(solution)/shard_map/ppermute | solution.py:441
  72.8 12.0 %collective-permute-start.9 = (f32[528,128]{1,0:T(8,128)S(1)}, f32[528,128]{1,0:T(8,128)S(1)}, u32[]{:S(2)}, u32[]{:S(2)}) collective-permute-start(f32[528,128]{1,0:T(8,128)S(1)} %constant_dynamic-update-slice_fusion.refs_7_), channel_id=1, source_target_pairs={{0,8},{8,16},{16,24},{24,32},{32,40},{40,48},{48,56},{56,120},{120... | collective-permute-start | bytes 811016 | tf_op jit(solution)/shard_map/ppermute | solution.py:441
